TPU v7x, 32 devices: a whole 2x2x4 slice. The times are simulated.
32 devices in a mesh: grp: 2 (over y), row: 4 (over z), col: 4 (over x, core).
Axes of the slice: x: 2, y: 2, z: 4, core: 2. Of those that a mesh axis runs over, the one named last changes fastest.
Arguments:
- tile_values: bfloat16 [8, 4, 256, 128, 128], P(('grp', 'row'), 'col'), parts along dimension 0, may hold values from -0.0625 to 0.0625
- tile_rows: int32 [8, 4, 256], P(('grp', 'row'), 'col'), parts along dimension 0, may hold values from 0 to 7
- tile_cols: int32 [8, 4, 256], P(('grp', 'row'), 'col'), parts along dimension 0, may hold values from 0 to 63
- tile_count: int32 [8, 4], P(('grp', 'row'), 'col'), parts along dimension 0, may hold values from 32 to 256, as said below
- primal_vars: float32 [64, 32768], P('grp', ('col', 'row')), parts along dimension 0, may hold values from -6 to 6
- dual_vars: float32 [64, 4096], P('grp', ('row', 'col')), parts along dimension 0, may hold values from 0 to 2
- objective: float32 [64, 32768], P('grp', ('col', 'row')), parts along dimension 0
- right_side: float32 [64, 4096], P('grp', ('row', 'col')), parts along dimension 0
- lower_bound: float32 [65536], P(('grp', 'col', 'row')), parts along dimension 0, may hold values from -1.5 to -0.2
- upper_bound: float32 [65536], P(('grp', 'col', 'row')), parts along dimension 0, may hold values from 0.2 to 1.5
- bound_kind: int32 [65536], P(('grp', 'col', 'row')), parts along dimension 0, may hold values from 0 to 2
- step_size: float32 [64], P('grp'), parts along dimension 0, may hold values from 0.05 to 0.4
- primal_weight: float32 [64], P('grp'), parts along dimension 0, may hold values from 0.5 to 2
Outputs:
- primal_next: float32 [64, 32768], P('grp', ('col', 'row')), parts along dimension 0
- dual_next: float32 [64, 4096], P('grp', ('row', 'col')), parts along dimension 0
- weight_next: float32 [64], P('grp'), parts along dimension 0
There are 2 independent parts, one for each index of `grp`. A program takes and returns all parts, laid end to end along the dimension named above; each array names one. Nothing has to cross between parts.
Inputs may be any that keep to these rules, and one draw needn't show every extreme that they name: `tile_count`: slots at or beyond the count of their cell are not part of the matrix; in every draw some cell uses all 256 slots.
All inputs are finite; a program needn't handle non-finite values.
Results may differ from a plain program's by a relative error of at most 0.0045.
Values may be sent and summed in bfloat16 or wider, within the bound.
No kernel may reach another device: no remote copies, remote signals or barrier semaphores. Data moves between devices by JAX's collectives and lax.ppermute only.
A program may use at most 64 MiB of HBM per device.

v0:
```python
import jax
import jax.numpy as jnp
from jax import lax
from jax.sharding import PartitionSpec as P

ITERS = 2


tile_block = 16
epsilon = 1e-06


def tile_product(tile_values, slot_rows, slot_cols, slot_low, slot_high, source, running, forward):
    first_block = slot_low // tile_block
    last_block = (slot_high + tile_block - 1) // tile_block

    def per_block(block_index, inner):
        first_slot = block_index * tile_block
        tiles_per_block = lax.dynamic_slice_in_dim(tile_values, first_slot, tile_block, 0)
        rows_here = lax.dynamic_slice_in_dim(slot_rows, first_slot, tile_block, 0)
        cols_here = lax.dynamic_slice_in_dim(slot_cols, first_slot, tile_block, 0)
        slot_index_list = first_slot + jnp.arange(tile_block, dtype=jnp.int32)
        live_mask = (slot_index_list >= slot_low) & (slot_index_list < slot_high)
        if forward:
            selected_indices = jnp.take(source, cols_here, axis=1)
            summand_value = jnp.einsum(
                "azy,zly->azl",
                selected_indices,
                tiles_per_block,
                preferred_element_type=jnp.float32,
            )
            target = rows_here
        else:
            selected_indices = jnp.take(source, rows_here, axis=1)
            summand_value = jnp.einsum(
                "hop,opt->hot",
                selected_indices,
                tiles_per_block,
                preferred_element_type=jnp.float32,
            )
            target = cols_here
        summand_value = jnp.where(
            live_mask[None, :, None], summand_value, jnp.zeros_like(summand_value)
        )
        return inner.at[:, target].add(summand_value)

    return lax.fori_loop(first_block, last_block, per_block, running)


def project(values, lower_bound, upper_bound, bound_kind):
    values = jnp.where(bound_kind >= 1, jnp.maximum(values, lower_bound), values)
    return jnp.where(bound_kind == 2, jnp.minimum(values, upper_bound), values)


def body(
    tile_values,
    tile_rows,
    tile_cols,
    tile_count,
    primal_vars,
    dual_vars,
    objective,
    right_side,
    lower_bound,
    upper_bound,
    bound_kind,
    step_size,
    primal_weight,
):
    scenarios = primal_vars.shape[0]
    tile_width = tile_values.shape[-1]
    slot_values = tile_values.reshape(tile_values.shape[2:])
    slot_rows = tile_rows.reshape(-1)
    slot_cols = tile_cols.reshape(-1)
    full_count = tile_count.reshape(())
    row_count = lax.axis_size("row")
    col_count = lax.axis_size("col")
    col_tiles = primal_vars.shape[1] * row_count // tile_width
    row_tiles = dual_vars.shape[1] * col_count // tile_width
    zero_slot = jnp.zeros((), jnp.int32)
    weight = primal_weight
    for sweep_index in range(ITERS):
        primal_step = (step_size / weight)[:, None]
        dual_step = (step_size * weight)[:, None]
        x_panel = lax.all_gather(
            primal_vars.astype(jnp.bfloat16), "row", axis=1, tiled=True
        ).reshape(scenarios, col_tiles, tile_width)
        zero_rows = jnp.zeros((scenarios, row_tiles, tile_width), jnp.float32)
        row_part = tile_product(
            slot_values, slot_rows, slot_cols, zero_slot, full_count, x_panel, zero_rows, True
        )
        row_part = row_part.reshape(scenarios, row_tiles * tile_width)
        row_total = lax.psum_scatter(
            row_part.astype(jnp.bfloat16), "col", scatter_dimension=1, tiled=True
        ).astype(jnp.float32)
        dual_new = jnp.maximum(dual_vars + dual_step * (right_side - row_total), 0.0)
        dual_bar = lax.all_gather(
            (2.0 * dual_new - dual_vars).astype(jnp.bfloat16), "col", axis=1, tiled=True
        )
        dual_move = jnp.sum((dual_new - dual_vars) ** 2, axis=1)
        dual_bar = dual_bar.reshape(scenarios, row_tiles, tile_width)
        zero_cols = jnp.zeros((scenarios, col_tiles, tile_width), jnp.float32)
        col_part = tile_product(
            slot_values, slot_rows, slot_cols, zero_slot, full_count, dual_bar, zero_cols, False
        )
        col_part = col_part.reshape(scenarios, col_tiles * tile_width)
        col_total = lax.psum_scatter(col_part, "row", scatter_dimension=1, tiled=True)
        updated_primal = project(
            primal_vars - primal_step * (objective - col_total),
            lower_bound,
            upper_bound,
            bound_kind,
        )
        primal_move = jnp.sum((updated_primal - primal_vars) ** 2, axis=1)
        primal_total, dual_total = lax.psum((primal_move, dual_move), ("row", "col"))
        weight = jnp.sqrt(
            weight * jnp.sqrt(primal_total + epsilon) / jnp.sqrt(dual_total + epsilon)
        )
        primal_vars, dual_vars = (updated_primal, dual_new)
    return (primal_vars, dual_vars, weight)


def solution(mesh):
    return jax.shard_map(
        body,
        mesh=mesh,
        in_specs=(
            P(("grp", "row"), "col", None, None, None),
            P(("grp", "row"), "col", None),
            P(("grp", "row"), "col", None),
            P(("grp", "row"), "col"),
            P("grp", ("col", "row")),
            P("grp", ("row", "col")),
            P("grp", ("col", "row")),
            P("grp", ("row", "col")),
            P(("grp", "col", "row")),
            P(("grp", "col", "row")),
            P(("grp", "col", "row")),
            P("grp"),
            P("grp"),
        ),
        out_specs=(P("grp", ("col", "row")), P("grp", ("row", "col")), P("grp")),
        check_vma=False,
    )
```

profile of v0, /device:TPU:0, one launch (start us, length us, event | category | flops | bytes accessed | tf_op | source)
XLA Modules:
  0.0 543.4 jit_solution(11975796329456995867)
XLA Ops:
  8.8 17.4 %all_gather.12 = bf16[32,8192]{1,0:T(8,128)(2,1)S(1)} all-gather(bf16[32,2048]{1,0:T(8,128)(2,1)S(1)} %convert_element_type.30), channel_id=1, replica_groups=mesh['grp'=2,'row'=4,'col'=4] {'row'}, dimensions={1}, use_global_device_ids=true | all-gather | bytes 655360 | tf_op jit(solution)/shard_map/all_gather | solution.py:85
  26.4 32.8 %while.40 = (s32[]{:T(128)}, f32[32,8,128]{2,0,1:T(8,128)S(1)}, s32[]{:T(128)}, s32[256]{0:T(256)}, s32[]{:T(128)}, /*index=5*/bf16[256,128,128]{2,1,0:T(8,128)(...) while((s32[]{:T(128)}, f32[32,8,128]{2,0,1:T(8,128)S(1)}, ...), condition=%wide.region_2.4_spmd, body=%wide.region_0.3_spmd.sunk | while | flops 16975060 | bytes 1970871 | solution.py:47
  27.2 1.4 compare_and_fusion.12
  29.2 1.5 fusion.54
  32.6 1.4 compare_and_fusion.12
  34.6 1.5 fusion.54
  38.1 1.4 compare_and_fusion.12
  40.1 1.5 fusion.54
  43.5 1.4 compare_and_fusion.12
  45.5 1.5 fusion.54
  51.0 1.5 fusion.54
  56.5 1.5 fusion.54
  59.9 74.9 %reduce-scatter.5.cloned.1.call-done = bf16[32,256]{1,0:T(8,128)(2,1)} async-done(((bf16[32,1024]{1,0:T(8,128)(2,1)}), bf16[32,256]{1,0:T(8,128)(2,1)}) %reduce-scatter.5.cloned.1.call-update) | async-done | bytes 16400 | tf_op jit(solution)/shard_map/reduce_scatter | solution.py:93
  135.7 5.2 all_gather.13
  141.2 32.0 %while.41 = (s32[]{:T(128)}, f32[32,64,128]{2,0,1:T(8,128)S(1)}, s32[]{:T(128)}, s32[256]{0:T(256)}, s32[]{:T(128)}, /*index=5*/bf16[256,128,128]{2,1,0:T(8,128)...) while((s32[]{:T(128)}, f32[32,64,128]{2,0,1:T(8,128)S(1)}, ...), condition=%wide.region_6.9_spmd, body=%wide.region_4.8_spmd.sunk | while | flops 16975060 | bytes 1970871 | solution.py:47
  142.0 1.4 compare_and_fusion.13
  152.6 1.4 compare_and_fusion.13
  174.3 80.5 %reduce-scatter.7.cloned.1.call-done = f32[32,2048]{1,0:T(8,128)} async-done(((f32[32,8192]{1,0:T(8,128)}), f32[32,2048]{1,0:T(8,128)}) %reduce-scatter.7.cloned.1.call-update) | async-done | bytes 262160 | tf_op jit(solution)/shard_map/reduce_scatter | solution.py:107
  256.1 16.1 %all_gather.14 = bf16[32,8192]{1,0:T(8,128)(2,1)S(1)} all-gather(bf16[32,2048]{1,0:T(8,128)(2,1)S(1)} %convert_element_type.35), channel_id=1, replica_groups=mesh['grp'=2,'row'=4,'col'=4] {'row'}, dimensions={1}, use_global_device_ids=true | all-gather | bytes 655360 | tf_op jit(solution)/shard_map/all_gather | solution.py:85
  272.2 32.8 %while.42 = (s32[]{:T(128)}, f32[32,8,128]{2,0,1:T(8,128)S(1)}, s32[]{:T(128)}, s32[256]{0:T(256)}, s32[]{:T(128)}, /*index=5*/bf16[256,128,128]{2,1,0:T(8,128)(...) while((s32[]{:T(128)}, f32[32,8,128]{2,0,1:T(8,128)S(1)}, ...), condition=%wide.region_14.17_spmd, body=%wide.region_12.16_spmd.sunk | while | flops 16975060 | bytes 1970871 | solution.py:47
  275.0 1.5 fusion.60
  280.5 1.5 fusion.60
  285.9 1.5 fusion.60
  291.4 1.5 fusion.60
  296.9 1.5 fusion.60
  302.3 1.5 fusion.60
  305.7 80.1 %all-reduce.1 = (f32[32]{0:T(128)S(1)}, f32[32]{0:T(128)S(1)}) all-reduce(f32[32]{0:T(128)S(1)} %get-tuple-element.321, f32[32]{0:T(128)S(1)} %get-tuple-element.319), channel_id=1, replica_groups=mesh['grp'=2,'row'=4,'col'=4] {'row','col'}, use_global_device_ids=true, to_apply=%region_11.14 | all-reduce | flops 64 | bytes 512 | tf_op jit(solution)/shard_map/psum | solution.py:115
  386.8 5.2 all_gather.15
  392.2 32.0 %while.43 = (s32[]{:T(128)}, f32[32,64,128]{2,0,1:T(8,128)S(1)}, s32[]{:T(128)}, s32[256]{0:T(256)}, s32[]{:T(128)}, /*index=5*/bf16[256,128,128]{2,1,0:T(8,128)...) while((s32[]{:T(128)}, f32[32,64,128]{2,0,1:T(8,128)S(1)}, ...), condition=%wide.region_18.21_spmd, body=%wide.region_16.20_spmd.sunk | while | flops 16975060 | bytes 1970871 | solution.py:47
  425.3 78.6 %reduce-scatter.11.cloned.1.call-done = f32[32,2048]{1,0:T(8,128)} async-done(((f32[32,8192]{1,0:T(8,128)}), f32[32,2048]{1,0:T(8,128)}) %reduce-scatter.11.cloned.1.call-update) | async-done | bytes 262160 | tf_op jit(solution)/shard_map/reduce_scatter | solution.py:107
  503.9 1.9 multiply_reduce_fusion
  505.8 30.5 %all-reduce = (f32[32]{0:T(128)S(1)}, f32[32]{0:T(128)S(1)}) all-reduce(f32[32]{0:T(128)S(1)} %get-tuple-element.315, f32[32]{0:T(128)S(1)} %get-tuple-element.313), channel_id=1, replica_groups=mesh['grp'=2,'row'=4,'col'=4] {'row','col'}, use_global_device_ids=true, to_apply=%region_23.26 | all-reduce | flops 64 | bytes 512 | tf_op jit(solution)/shard_map/psum | solution.py:115
  (179 shorter events, 111.4 us)
Async XLA Ops:
  7.2 127.6 %reduce-scatter.5.cloned.1.call-start = ((), (), s32[]{:S(2)}) async-start(), calls=%async_computation.4 | async-start | bytes 81920 | tf_op jit(solution)/shard_map/reduce_scatter | solution.py:93
  26.3 33.5 %copy-start.8 = (f32[32]{0:T(128)S(1)}, f32[32]{0:T(128)}, u32[]{:S(2)}) copy-start(f32[32]{0:T(128)} %param.37) | copy-start | bytes 388
  26.3 33.5 %copy-start.9 = (f32[32]{0:T(128)S(1)}, f32[32]{0:T(128)}, u32[]{:S(2)}) copy-start(f32[32]{0:T(128)} %param.36) | copy-start | bytes 388
  26.4 108.4 %copy-start.2 = (f32[32,256]{1,0:T(8,128)S(1)}, f32[32,256]{1,0:T(8,128)}, u32[]{:S(2)}) copy-start(f32[32,256]{1,0:T(8,128)} %param.32) | copy-start | bytes 98308
  26.4 108.4 %copy-start.3 = (f32[32,256]{1,0:T(8,128)S(1)}, f32[32,256]{1,0:T(8,128)}, u32[]{:S(2)}) copy-start(f32[32,256]{1,0:T(8,128)} %param.30) | copy-start | bytes 98308
  59.8 195.0 %reduce-scatter.7.cloned.1.call-start = ((), (), s32[]{:S(2)}) async-start(), calls=%async_computation.5 | async-start | bytes 1310720 | tf_op jit(solution)/shard_map/reduce_scatter | solution.py:107
  141.1 33.2 %copy-start.7 = (s32[2048]{0:T(1024)S(1)}, s32[2048]{0:T(1024)}, u32[]{:S(2)}) copy-start(s32[2048]{0:T(1024)} %param.35) | copy-start | bytes 24580
  141.1 113.7 %copy-start = (f32[32,2048]{1,0:T(8,128)S(1)}, f32[32,2048]{1,0:T(8,128)}, u32[]{:S(2)}) copy-start(f32[32,2048]{1,0:T(8,128)} %param.31) | copy-start | bytes 786436
  141.1 113.7 %copy-start.1 = (f32[32,2048]{1,0:T(8,128)S(1)}, f32[32,2048]{1,0:T(8,128)}, u32[]{:S(2)}) copy-start(f32[32,2048]{1,0:T(8,128)} %param.29) | copy-start | bytes 786436
  141.1 113.7 %copy-start.5 = (f32[2048]{0:T(1024)S(1)}, f32[2048]{0:T(1024)}, u32[]{:S(2)}) copy-start(f32[2048]{0:T(1024)} %param.34) | copy-start | bytes 24580
  141.1 113.7 %copy-start.6 = (f32[2048]{0:T(1024)S(1)}, f32[2048]{0:T(1024)}, u32[]{:S(2)}) copy-start(f32[2048]{0:T(1024)} %param.33) | copy-start | bytes 24580
  174.3 211.6 %reduce-scatter.9.cloned.1.call-start = ((), (), s32[]{:S(2)}) async-start(), calls=%async_computation.6 | async-start | bytes 81920 | tf_op jit(solution)/shard_map/reduce_scatter | solution.py:93
  305.7 198.2 %reduce-scatter.11.cloned.1.call-start = ((), (), s32[]{:S(2)}) async-start(), calls=%async_computation.7 | async-start | bytes 1310720 | tf_op jit(solution)/shard_map/reduce_scatter | solution.py:107
  386.8 5.4 copy-start.4
Sparse Core Ops, SparseCore 0:
  59.9 74.8 reduce-scatter.4
  174.4 80.3 reduce-scatter.6
  305.8 70.5 reduce-scatter.8
  425.4 78.4 reduce-scatter.10
where the time goes:
time: 551 us; the launch traced here: 543 us
  waiting for transfers between devices  234 us (42%)
  blocking collectives  155 us (28%)
  other arithmetic  88.8 us (16%)
  matrix products  33.8 us (6%)
  local copies, waits for them, and re-layouts  16.4 us (3%)
  between operations  14.7 us (3%)
    reduce_scatter x2, waiting for transfers between devices, body(): lax.psum_scatter(col_part, 'row', scatter_dimension=1, tiled=True)  159 us
    psum x2, blocking collectives, body(): lax.psum((primal_move, dual_move), ('row', 'col'))  111 us
    reduce_scatter x2, waiting for transfers between devices, body(): lax.psum_scatter(row_part.astype(jnp.bfloat16), 'col', scatter_dimension=...  74.9 us
    all_gather x2, blocking collectives, body(): lax.all_gather(primal_vars.astype(jnp.bfloat16), 'row', axis=1, tiled=True)  33.4 us
    scatter-add x24, other arithmetic, per_block(): return inner.at[:, target].add(summand_value)  29 us
    select_n x24, other arithmetic, per_block(): return inner.at[:, target].add(summand_value)  18.2 us
    dot_general x12, matrix products, per_block(): jnp.einsum('azy,zly->azl', selected_indices, tiles_per_block, preferred_e...  17.6 us
    and x12, other arithmetic, per_block(): selected_indices = jnp.take(source, cols_here, axis=1)  16.9 us
  transfers between devices with their start and end apart: 4, of which 3 were waited for; matrix products, arithmetic and copies ran while one was open for 0% of the time, Pallas kernels for 0%

commit v1 on v0

v1 whole, which is shorter than its diff:
```python
import functools

import jax
import jax.numpy as jnp
from jax import lax
from jax.experimental import pallas as pl
from jax.experimental.pallas import tpu as pltpu
from jax.sharding import PartitionSpec as P

ITERS = 2
EPSILON = 1e-06
COPIES = 4
VMEM_LIMIT = 40 << 20

SMEM = pl.BlockSpec(memory_space=pltpu.SMEM)
VMEM = pl.BlockSpec(memory_space=pltpu.VMEM)
ANY = pl.BlockSpec(memory_space=pl.ANY)
f32, bf16 = jnp.float32, jnp.bfloat16


def call(kernel, name, out_shape, in_specs, scratch=(), limit=VMEM_LIMIT, cost=None):
    out_specs = jax.tree.map(lambda _: VMEM, out_shape, is_leaf=lambda o: hasattr(o, "shape"))
    return pl.pallas_call(
        kernel,
        out_shape=out_shape,
        in_specs=in_specs,
        out_specs=out_specs,
        scratch_shapes=scratch,
        compiler_params=pltpu.CompilerParams(vmem_limit_bytes=limit),
        cost_estimate=cost,
        name=name,
    )


def pinned(array):
    return pltpu.with_memory_space_constraint(array, pltpu.VMEM)


def densify_kernel(slots, places, rt, rows, cols, count, tiles, out, head, nxt, multi, stage, sem):
    live = jnp.minimum(count[0], slots)
    step = slots // COPIES
    tile = out.shape[1:]

    def copy(i):
        part = pl.ds(i * step, step)
        return pltpu.make_async_copy(tiles.at[part], stage.at[part], sem.at[i])

    for i in range(COPIES):
        copy(i).start()
    zero = jnp.zeros(tile, bf16)

    @pl.loop(0, places, unroll=4)
    def _(p):
        head[p] = -1
        out[p] = zero

    def link(s, found):
        p = cols[s] * rt + rows[s]
        before = head[p]
        nxt[s] = before
        head[p] = s
        second = jnp.logical_and(before >= 0, nxt[jnp.maximum(before, 0)] < 0)
        multi[found] = p
        return found + second.astype(jnp.int32)

    found = lax.fori_loop(0, live, link, jnp.int32(0))
    for i in range(COPIES):
        copy(i).wait()

    def place(s):
        out[cols[s] * rt + rows[s]] = stage[s]

    whole = live // 8

    @pl.loop(0, whole)
    def _(b):
        for i in range(8):
            place(b * 8 + i)

    @pl.loop(whole * 8, live)
    def _(s):
        place(s)

    @pl.loop(0, found)
    def _(m):
        p = multi[m]
        first = head[p]

        def more(state):
            return state[0] >= 0

        def add(state):
            s, total = state
            return nxt[s], total + stage[s].astype(f32)

        _, total = lax.while_loop(more, add, (nxt[first], stage[first].astype(f32)))
        out[p] = total.astype(bf16)


def densify(tiles, rows, cols, count, rt, ct):
    slots, height, width = tiles.shape
    places = rt * ct
    return call(
        functools.partial(densify_kernel, slots, places, rt),
        "densify",
        pltpu.VMEM((places, height, width), bf16),
        [SMEM, SMEM, SMEM, ANY],
        [
            pltpu.SMEM((places,), jnp.int32),
            pltpu.SMEM((slots,), jnp.int32),
            pltpu.SMEM((slots + 1,), jnp.int32),
            pltpu.VMEM(tiles.shape, bf16),
            pltpu.SemaphoreType.DMA((COPIES,)),
        ],
        cost=pl.CostEstimate(flops=0, bytes_accessed=32 << 20, transcendentals=0),
    )(rows, cols, count, tiles)


def columns(k, base, rt, first, n):
    parts = []
    for j in range(first, first + n):
        block = k[pl.ds(base + j * rt, rt)]
        parts.append(block.reshape(rt * block.shape[1], block.shape[2]))
    return jnp.concatenate(parts, axis=1) if n > 1 else parts[0]


def spans(per):
    return [(j, min(2, per - j)) for j in range(0, per, 2)]


def forward(k, x, chunk, rt, per):
    width = k.shape[2]
    total = None
    for j, n in spans(per):
        part = lax.dot_general(
            x[:, j * width : (j + n) * width],
            columns(k, chunk * (per * rt), rt, j, n),
            (((1,), (1,)), ((), ())),
            preferred_element_type=f32,
        )
        total = part if total is None else total + part
    return total


def backward(k, d, chunk, rt, per, store):
    width = k.shape[2]
    for j, n in spans(per):
        block = columns(k, chunk * (per * rt), rt, j, n)
        store(j * width, (j + n) * width, jnp.dot(d, block, preferred_element_type=f32))


def forward_kernel(rt, per, n, has_base, chunks, k, *refs):
    xs, out = refs[:n], refs[-1]
    total = refs[n][...] if has_base else None
    for i in range(n):
        part = forward(k, xs[i], chunks[i], rt, per)
        total = part if total is None else total + part
    out[...] = total.astype(out.dtype)


def forward_part(k, chunks, xs, base, rt, dtype):
    scen, width = xs[0].shape
    per = width // k.shape[2]
    shape = (scen, rt * k.shape[1])
    extra = [] if base is None else [base]
    return call(
        functools.partial(forward_kernel, rt, per, len(xs), base is not None),
        "forward",
        jax.ShapeDtypeStruct(shape, dtype),
        [SMEM] + [VMEM] * (1 + len(xs) + len(extra)),
    )(jnp.stack(chunks), pinned(k), *xs, *extra)


def dual_kernel(rt, per, n_col, n_part, ids, k, step, weight, *refs):
    parts, refs = refs[:n_part], refs[n_part:]
    y, rhs, y_out, bar_out, move_out, send_out = refs
    sigma = step[...] * weight[...]
    total = parts[0][...].astype(f32)
    for part in parts[1:]:
        total = total + part[...].astype(f32)
    width = total.shape[1] // n_col
    bars = []
    for c in range(n_col):
        old = y[c]
        new = jnp.maximum(old + sigma * (rhs[c] - total[:, c * width : (c + 1) * width]), 0.0)
        y_out[c] = new
        bars.append((2.0 * new - old).astype(bf16))
    bar = jnp.concatenate(bars, axis=1)
    bar_out[...] = bar
    mine = ids[0]
    move_out[...] = jnp.sum((y_out[mine] - y[mine]) ** 2, axis=1, keepdims=True)

    def store(low, high, value):
        send_out[:, low:high] = value.astype(send_out.dtype)

    backward(k, bar, ids[1], rt, per, store)


def backward_kernel(rt, per, n, chunks, k, d, *outs):
    bar = d[...]
    for i in range(n):

        def store(low, high, value):
            outs[i][:, low:high] = value.astype(outs[i].dtype)

        backward(k, bar, chunks[i], rt, per, store)


def backward_parts(k, d, chunks, dtypes, rt, per):
    shape = (d.shape[0], per * k.shape[2])
    return call(
        functools.partial(backward_kernel, rt, per, len(chunks)),
        "backward",
        [jax.ShapeDtypeStruct(shape, dtype) for dtype in dtypes],
        [SMEM, VMEM, VMEM],
    )(jnp.stack(chunks), pinned(k), d)


def primal_kernel(n_part, step, weight, x, objective, low, high, kind, dual_move, *refs):
    parts, (x_out, low_out, move_out) = refs[:n_part], refs[n_part:]
    total = parts[0][...].astype(f32)
    for part in parts[1:]:
        total = total + part[...].astype(f32)
    tau = step[...] / weight[...]
    old = x[...]
    new = old - tau * (objective[...] - total)
    new = jnp.where(kind[...] >= 1, jnp.maximum(new, low[...]), new)
    new = jnp.where(kind[...] == 2, jnp.minimum(new, high[...]), new)
    x_out[...] = new
    low_out[...] = new.astype(bf16)
    primal_move = jnp.sum((new - old) ** 2, axis=1, keepdims=True)
    lane = lax.broadcasted_iota(jnp.int32, move_out.shape, 1)
    move_out[...] = jnp.where(lane == 0, primal_move, dual_move[...])


def sum_kernel(*refs):
    parts = [ref[...] for ref in refs[:-1]]
    while len(parts) > 1:
        parts = [a + b for a, b in zip(parts[::2], parts[1::2])]
    refs[-1][...] = parts[0]


def weight_kernel(n_part, weight, *refs):
    parts = [ref[...] for ref in refs[:n_part]]
    while len(parts) > 1:
        parts = [a + b for a, b in zip(parts[::2], parts[1::2])]
    primal, dual = parts[0][:, 0:1], parts[0][:, 1:2]
    refs[n_part][...] = jnp.sqrt(
        weight[...] * jnp.sqrt(primal + EPSILON) / jnp.sqrt(dual + EPSILON)
    )


def swap(array, axis, k):
    n = lax.axis_size(axis)
    return lax.ppermute(array, axis, [(i, i ^ k) for i in range(n)])


def fetch(array, axis, k):
    n = lax.axis_size(axis)
    return lax.ppermute(array, axis, [((i + k) % n, i) for i in range(n)])


def send(array, axis, k):
    n = lax.axis_size(axis)
    return lax.ppermute(array, axis, [(i, (i + k) % n) for i in range(n)])


def body(
    tile_values,
    tile_rows,
    tile_cols,
    tile_count,
    primal_vars,
    dual_vars,
    objective,
    right_side,
    lower_bound,
    upper_bound,
    bound_kind,
    step_size,
    primal_weight,
):
    tiles = tile_values.reshape(tile_values.shape[2:])
    width = tiles.shape[-1]
    n_row, n_col = lax.axis_size("row"), lax.axis_size("col")
    row, col = lax.axis_index("row"), lax.axis_index("col")
    scen, shard = primal_vars.shape
    per = shard // width
    rt = dual_vars.shape[1] * n_col // width
    ct = per * n_row
    line = n_row == 4

    if line:
        chunks = [row, row ^ 1, row ^ 3, row ^ 2]
    else:
        chunks = [(row + i) % n_row for i in range(n_row)]

    def gather(low):
        if line:
            near, far = swap(low, "row", 1), swap(low, "row", 3)
            return [low, near, far, swap(far, "row", 1)]
        return [low] + [fetch(low, "row", i) for i in range(1, n_row)]

    def all_cols(array):
        return [array] + [fetch(array, "col", i) for i in range(1, n_col)]

    low = primal_vars.astype(bf16)
    xs = gather(low)
    k = densify(
        tiles, tile_rows.reshape(-1), tile_cols.reshape(-1), tile_count.reshape(-1), rt, ct
    )
    both = all_cols(jnp.stack([dual_vars, right_side]))
    order = jnp.stack([(i - col) % n_col for i in range(n_col)])
    both = jnp.take(jnp.stack(both), order, axis=0)
    y, rhs = both[:, 0], both[:, 1]
    step = step_size[:, None]
    weight = primal_weight[:, None]
    low_bound, high_bound, kind = lower_bound[None], upper_bound[None], bound_kind[None]
    x = primal_vars
    for _ in range(ITERS):
        base = forward_part(k, chunks[:-1], xs[:-1], None, rt, f32)
        part = forward_part(k, chunks[-1:], xs[-1:], base, rt, bf16)
        parts = all_cols(part)
        first = chunks[-1]
        y, bar, dual_move, far = call(
            functools.partial(dual_kernel, rt, per, n_col, n_col),
            "dual",
            [
                jax.ShapeDtypeStruct(y.shape, f32),
                jax.ShapeDtypeStruct(part.shape, bf16),
                jax.ShapeDtypeStruct((scen, 1), f32),
                jax.ShapeDtypeStruct((scen, shard), bf16),
            ],
            [SMEM] + [VMEM] * (5 + n_col),
        )(jnp.stack([col, first]), pinned(k), step, weight, *parts, y, rhs)
        if line:
            got = swap(far, "row", 1)
            own, near, cross = backward_parts(
                k, bar, [chunks[0], chunks[1], chunks[2]], [f32, bf16, f32], rt, per
            )
            near = swap(near, "row", 1)
            cross = (cross + got.astype(f32)).astype(bf16)
            totals = [own, near, swap(cross, "row", 3)]
        else:
            rest = backward_parts(k, bar, chunks[:-1], [f32] + [bf16] * (n_row - 2), rt, per)
            sent = list(rest[1:]) + [far]
            totals = [rest[0]] + [send(s, "row", i + 1) for i, s in enumerate(sent)]
        x, low, move = call(
            functools.partial(primal_kernel, len(totals)),
            "primal",
            [
                jax.ShapeDtypeStruct(x.shape, f32),
                jax.ShapeDtypeStruct(x.shape, bf16),
                jax.ShapeDtypeStruct((scen, width), f32),
            ],
            [VMEM] * (8 + len(totals)),
        )(step, weight, x, objective, low_bound, high_bound, kind, dual_move, *totals)
        if _ < ITERS - 1:
            xs = gather(low)
        if line and n_col == 4:
            moves = [move] + [swap(move, "row", i) for i in (1, 2, 3)]
            move = call(sum_kernel, "moves", jax.ShapeDtypeStruct(move.shape, f32), [VMEM] * 4)(
                *moves
            )
            moves = [move] + [swap(move, "col", i) for i in (1, 2, 3)]
        else:
            moves = [lax.psum(move, ("row", "col"))]
        weight = call(
            functools.partial(weight_kernel, len(moves)),
            "weight",
            jax.ShapeDtypeStruct((scen, 1), f32),
            [VMEM] * (1 + len(moves)),
        )(weight, *moves)
    dual = lax.dynamic_index_in_dim(y, col, 0, keepdims=False)
    return x, dual, weight.reshape(-1)


def solution(mesh):
    return jax.shard_map(
        body,
        mesh=mesh,
        in_specs=(
            P(("grp", "row"), "col", None, None, None),
            P(("grp", "row"), "col", None),
            P(("grp", "row"), "col", None),
            P(("grp", "row"), "col"),
            P("grp", ("col", "row")),
            P("grp", ("row", "col")),
            P("grp", ("col", "row")),
            P("grp", ("row", "col")),
            P(("grp", "col", "row")),
            P(("grp", "col", "row")),
            P(("grp", "col", "row")),
            P("grp"),
            P("grp"),
        ),
        out_specs=(P("grp", ("col", "row")), P("grp", ("row", "col")), P("grp")),
        check_vma=False,
    )
```

time: 551 us -> 147 us (0.27); the launches traced: 543 us -> 146 us
  waiting for transfers between devices: 234 us -> 28.5 us
  blocking collectives: 155 us -> 0 us
  other arithmetic: 88.8 us -> 5.87 us
  starting transfers between devices: 0.16 us -> 39 us
  Pallas kernels: 0 us -> 35.7 us
  matrix products: 33.8 us -> 0 us
  local copies, waits for them, and re-layouts: 16.4 us -> 34.9 us
  between operations: 14.7 us -> 1.62 us
    reduce_scatter x4 -> x0, waiting for transfers between devices: 234 us -> none  [the longest x2 159 us: body(): lax.psum_scatter(col_part, 'row', scatter_dimension=1, tiled=True)]
    psum x2 -> x0, blocking collectives: 111 us -> none  [body(): lax.psum((primal_move, dual_move), ('row', 'col'))]
    all_gather x4 -> x0, blocking collectives: 43.9 us -> none  [the longest x2 33.4 us: body(): lax.all_gather(primal_vars.astype(jnp.bfloat16), 'row', axis=1, tiled=True)]
    ppermute x0 -> x33, starting transfers between devices: none -> 39 us  [the longest x24 30.2 us: swap(): return lax.ppermute(array, axis, [(i, i ^ k) for i in range(n)])]
    pallas_call x0 -> x15, Pallas kernels: none -> 35.7 us  [the longest x4 16.7 us: forward_part(): call(functools.partial(forward_kernel, rt, per, len(xs), base is not None...]
    dot_general x24 -> x0, matrix products: 33.8 us -> none  [the longest x12 17.6 us: per_block(): jnp.einsum('azy,zly->azl', selected_indices, tiles_per_block, preferred_e...]
    and x24 -> x1, other arithmetic: 33.7 us -> 0.08 us  [body(): both = jnp.take(jnp.stack(both), order, axis=0)]
    unnamed x20 -> x64, local copies, waits for them, and re-layouts: 0.06 us -> 29.5 us
  transfers between devices with their start and end apart: 4 -> 33, of which waited for: 3 -> 16; matrix products, arithmetic and copies ran while one was open for 0% -> 7% of each run, Pallas kernels for 0% -> 18%
where the time goes in v1:
time: 147 us; the launch traced here: 146 us
  starting transfers between devices  39 us (27%)
  Pallas kernels  35.7 us (24%)
  local copies, waits for them, and re-layouts  34.9 us (24%)
  waiting for transfers between devices  28.5 us (19%)
  other arithmetic  5.87 us (4%)
  between operations  1.62 us (1%)
    ppermute x24, starting transfers between devices, swap(): return lax.ppermute(array, axis, [(i, i ^ k) for i in range(n)])  30.2 us
    unnamed x64, local copies, waits for them, and re-layouts  29.5 us
    ppermute x24, waiting for transfers between devices, swap(): return lax.ppermute(array, axis, [(i, i ^ k) for i in range(n)])  25.9 us
    pallas_call x4, Pallas kernels, forward_part(): call(functools.partial(forward_kernel, rt, per, len(xs), base is not None...  16.7 us
    ppermute x9, starting transfers between devices, fetch(): return lax.ppermute(array, axis, [((i + k) % n, i) for i in range(n)])  8.76 us
    pallas_call x2, Pallas kernels, backward_parts(): call(functools.partial(backward_kernel, rt, per, len(chunks)), 'backward'...  7.63 us
    pallas_call x2, Pallas kernels, body(): call(functools.partial(dual_kernel, rt, per, n_col, n_col), 'dual', [jax....  5.45 us
    pallas_call x1, Pallas kernels, densify(): call(functools.partial(densify_kernel, slots, places, rt), 'densify', plt...  4.51 us
  transfers between devices with their start and end apart: 33, of which 16 were waited for; matrix products, arithmetic and copies ran while one was open for 7% of the time, Pallas kernels for 18%

profile of v1, /device:TPU:0, one launch (start us, length us, event | category | flops | bytes accessed | tf_op | source)
XLA Modules:
  0.0 145.6 jit_solution(395539291301683341)
XLA Ops:
  1.4 3.0 %collective-permute-start.7 = (f32[2,32,256]{2,1,0:T(8,128)S(1)}, f32[2,32,256]{2,1,0:T(8,128)S(1)}, u32[]{:S(2)}, u32[]{:S(2)}) collective-permute-start(f32[2,32,256]{2,1,0:T(8,128)S(1)} %get-tuple-element.44), channel_id=1, source_target_pairs={{2,0},{3,1},{0,2},{1,3},{6,4},{7,5},{4,6},{5,7},{10,8},{11,9},{8,1... | collective-permute-start | bytes 196616 | tf_op jit(solution)/shard_map/ppermute | solution.py:260
  5.9 1.6 %collective-permute-start.2 = (bf16[32,2048]{1,0:T(8,128)(2,1)S(1)}, bf16[32,2048]{1,0:T(8,128)(2,1)S(1)}, u32[]{:S(2)}, u32[]{:S(2)}) collective-permute-start(bf16[32,2048]{1,0:T(8,128)(2,1)S(1)} %convert_element_type.15.refs_0_), channel_id=1, source_target_pairs={{0,4},{4,0},{8,12},{12,8},{1,5},{5,1},{9,13},{13,9},{2,6},{6,2},{1... | collective-permute-start | bytes 393224 | tf_op jit(solution)/shard_map/ppermute | solution.py:255
  7.6 2.5 %collective-permute-start = (bf16[32,2048]{1,0:T(8,128)(2,1)S(1)}, bf16[32,2048]{1,0:T(8,128)(2,1)S(1)}, u32[]{:S(2)}, u32[]{:S(2)}) collective-permute-start(bf16[32,2048]{1,0:T(8,128)(2,1)S(1)} %convert_element_type.15.refs_0_), channel_id=1, source_target_pairs={{0,12},{4,8},{8,4},{12,0},{1,13},{5,9},{9,5},{13,1},{2,14},{6,10},... | collective-permute-start | bytes 393224 | tf_op jit(solution)/shard_map/ppermute | solution.py:255
  14.8 4.5 %densify.1.k = bf16[512,128,128]{2,1,0:T(8,128)(2,1)S(1)} custom-call(s32[256]{0:T(256)} %bitcast.50, s32[256]{0:T(256)} %bitcast.51, s32[1]{0:T(128)} %bitcast.37.count, bf16[256,128,128]{2,1,0:T(8,128)(2,1)} %bitcast.44), custom_call_target="tpu_custom_call" | custom-call | bytes 33554432 | tf_op jit(solution)/shard_map/densify/pallas_call | solution.py:103
  19.3 5.8 %copy-done = bf16[512,128,128]{2,1,0:T(8,128)(2,1)} copy-done((bf16[512,128,128]{2,1,0:T(8,128)(2,1)}, bf16[512,128,128]{2,1,0:T(8,128)(2,1)S(1)}, u32[]{:S(2)}) %copy-start) | copy-done | bytes 16777240
  25.7 1.9 %collective-permute-start.1 = (bf16[32,2048]{1,0:T(8,128)(2,1)S(1)}, bf16[32,2048]{1,0:T(8,128)(2,1)S(1)}, u32[]{:S(2)}, u32[]{:S(2)}) collective-permute-start(bf16[32,2048]{1,0:T(8,128)(2,1)S(1)} %collective-permute-done.refs_2_), channel_id=1, source_target_pairs={{0,4},{4,0},{8,12},{12,8},{1,5},{5,1},{9,13},{13,9},{2,6},{6,2},{1... | collective-permute-start | bytes 393224 | tf_op jit(solution)/shard_map/ppermute | solution.py:255
  28.4 5.8 %copy-done.1 = bf16[512,128,128]{2,1,0:T(8,128)(2,1)S(1)} copy-done((bf16[512,128,128]{2,1,0:T(8,128)(2,1)S(1)}, bf16[512,128,128]{2,1,0:T(8,128)(2,1)}, u32[]{:S(2)}) %copy-start.1) | copy-done | bytes 16777240
  34.2 5.5 %forward.4.refs_1_ = f32[32,1024]{1,0:T(8,128)} custom-call(s32[3]{0:T(128)} %pad_add_fusion.1.chunks, bf16[512,128,128]{2,1,0:T(8,128)(2,1)S(1)} %copy-done.1, bf16[32,2048]{1,0:T(8,128)(2,1)} %copy-done.19, bf16[32,2048]{1,0:T(8,128)(2,1)} %copy-done.20, bf16[32,2048]{1,0:T(8,128)(2,1)} %copy-done.21), custom_call_target="tpu_custom_call" | custom-call | tf_op jit(solution)/shard_map/forward/pallas_call | solution.py:166
  40.3 2.9 %forward.5.refs_0_ = bf16[32,1024]{1,0:T(8,128)(2,1)} custom-call(s32[1]{0:T(128)} %bitcast.6.chunks, bf16[512,128,128]{2,1,0:T(8,128)(2,1)S(1)} %copy-done.1, bf16[32,2048]{1,0:T(8,128)(2,1)} %copy-done.25, f32[32,1024]{1,0:T(8,128)} %forward.4.refs_1_), custom_call_target="tpu_custom_call" | custom-call | tf_op jit(solution)/shard_map/forward/pallas_call | solution.py:166
  45.7 1.6 %collective-permute-done.5.refs_3_ = bf16[32,1024]{1,0:T(8,128)(2,1)S(1)} collective-permute-done((bf16[32,1024]{1,0:T(8,128)(2,1)}, bf16[32,1024]{1,0:T(8,128)(2,1)S(1)}, u32[]{:S(2)}, u32[]{:S(2)}) %collective-permute-start.5) | collective-permute-done | bytes 65568 | tf_op jit(solution)/shard_map/ppermute | solution.py:260
  49.1 2.7 %dual.2 = (f32[4,32,256]{2,1,0:T(8,128)}, bf16[32,1024]{1,0:T(8,128)(2,1)}, f32[32,1]{1,0:T(8,128)}, bf16[32,2048]{1,0:T(8,128)(2,1)}) custom-call(s32[2]{0:T(128)} %pad_add_fusion.ids, bf16[512,128,128]{2,1,0:T(8,128)(2,1)S(1)} %copy-done.1, f32[32,1]{1,0:T(8,128)} %copy.30.step, f32[32,1]{1,0:T(8,128)} %copy.28.weight, bf16[32,1024]{1,0:T(8,128)(2,1)} %forward.5.refs_0_, ...), custom_call_target="tpu_custom_call" | custom-call | tf_op jit(solution)/shard_map/dual/pallas_call | solution.py:325
  52.3 3.8 %backward.2 = (f32[32,2048]{1,0:T(8,128)}, bf16[32,2048]{1,0:T(8,128)(2,1)}, f32[32,2048]{1,0:T(8,128)}) custom-call(s32[3]{0:T(128)} %pad_add_fusion.1.chunks, bf16[512,128,128]{2,1,0:T(8,128)(2,1)S(1)} %copy-done.1, bf16[32,1024]{1,0:T(8,128)(2,1)} %get-tuple-element.23.d), custom_call_target="tpu_custom_call" | custom-call | tf_op jit(solution)/shard_map/backward/pallas_call | solution.py:211
  56.1 1.6 %collective-permute-start.9 = (bf16[32,2048]{1,0:T(8,128)(2,1)}, bf16[32,2048]{1,0:T(8,128)(2,1)S(1)}, u32[]{:S(2)}, u32[]{:S(2)}) collective-permute-start(bf16[32,2048]{1,0:T(8,128)(2,1)} %get-tuple-element.25), channel_id=1, source_target_pairs={{0,4},{4,0},{8,12},{12,8},{1,5},{5,1},{9,13},{13,9},{2,6},{6,2},{1... | collective-permute-start | bytes 393224 | tf_op jit(solution)/shard_map/ppermute | solution.py:255
  59.0 5.0 %collective-permute-start.11 = (bf16[32,2048]{1,0:T(8,128)(2,1)S(1)}, bf16[32,2048]{1,0:T(8,128)(2,1)S(1)}, u32[]{:S(2)}, u32[]{:S(2)}) collective-permute-start(bf16[32,2048]{1,0:T(8,128)(2,1)S(1)} %add_convert_fusion.1), channel_id=1, source_target_pairs={{0,12},{4,8},{8,4},{12,0},{1,13},{5,9},{9,5},{13,1},{2,14},{6,10},... | collective-permute-start | bytes 393224 | tf_op jit(solution)/shard_map/ppermute | solution.py:255
  64.1 5.4 %collective-permute-done.11.refs_2_ = bf16[32,2048]{1,0:T(8,128)(2,1)S(1)} collective-permute-done((bf16[32,2048]{1,0:T(8,128)(2,1)S(1)}, bf16[32,2048]{1,0:T(8,128)(2,1)S(1)}, u32[]{:S(2)}, u32[]{:S(2)}) %collective-permute-start.11) | collective-permute-done | bytes 131104 | tf_op jit(solution)/shard_map/ppermute | solution.py:255
  70.7 1.7 %collective-permute-start.18 = (bf16[32,2048]{1,0:T(8,128)(2,1)S(1)}, bf16[32,2048]{1,0:T(8,128)(2,1)S(1)}, u32[]{:S(2)}, u32[]{:S(2)}) collective-permute-start(bf16[32,2048]{1,0:T(8,128)(2,1)S(1)} %get-tuple-element.30.refs_0_), channel_id=1, source_target_pairs={{0,12},{4,8},{8,4},{12,0},{1,13},{5,9},{9,5},{13,1},{2,14},{6,10},... | collective-permute-start | bytes 393224 | tf_op jit(solution)/shard_map/ppermute | solution.py:255
  73.2 5.8 %collective-permute-done.18.refs_2_ = bf16[32,2048]{1,0:T(8,128)(2,1)S(1)} collective-permute-done((bf16[32,2048]{1,0:T(8,128)(2,1)S(1)}, bf16[32,2048]{1,0:T(8,128)(2,1)S(1)}, u32[]{:S(2)}, u32[]{:S(2)}) %collective-permute-start.18) | collective-permute-done | bytes 131104 | tf_op jit(solution)/shard_map/ppermute | solution.py:255
  80.6 5.8 %copy-done.2 = bf16[512,128,128]{2,1,0:T(8,128)(2,1)S(1)} copy-done((bf16[512,128,128]{2,1,0:T(8,128)(2,1)S(1)}, bf16[512,128,128]{2,1,0:T(8,128)(2,1)}, u32[]{:S(2)}) %copy-start.2) | copy-done | bytes 16777240
  86.4 5.5 %forward.6.refs_1_ = f32[32,1024]{1,0:T(8,128)} custom-call(s32[3]{0:T(128)} %pad_add_fusion.1.chunks, bf16[512,128,128]{2,1,0:T(8,128)(2,1)S(1)} %copy-done.2, bf16[32,2048]{1,0:T(8,128)(2,1)} %copy-done.13, bf16[32,2048]{1,0:T(8,128)(2,1)} %copy-done.23, bf16[32,2048]{1,0:T(8,128)(2,1)} %copy-done.22), custom_call_target="tpu_custom_call" | custom-call | tf_op jit(solution)/shard_map/forward/pallas_call | solution.py:166
  92.5 2.9 %forward.7.refs_0_ = bf16[32,1024]{1,0:T(8,128)(2,1)} custom-call(s32[1]{0:T(128)} %bitcast.6.chunks, bf16[512,128,128]{2,1,0:T(8,128)(2,1)S(1)} %copy-done.2, bf16[32,2048]{1,0:T(8,128)(2,1)} %copy-done.24, f32[32,1024]{1,0:T(8,128)} %forward.6.refs_1_), custom_call_target="tpu_custom_call" | custom-call | tf_op jit(solution)/shard_map/forward/pallas_call | solution.py:166
  95.4 2.0 %collective-permute-start.22 = (bf16[32,1024]{1,0:T(8,128)(2,1)}, bf16[32,1024]{1,0:T(8,128)(2,1)S(1)}, u32[]{:S(2)}, u32[]{:S(2)}) collective-permute-start(bf16[32,1024]{1,0:T(8,128)(2,1)} %forward.7.refs_0_), channel_id=1, source_target_pairs={{2,0},{3,1},{0,2},{1,3},{6,4},{7,5},{4,6},{5,7},{10,8},{11,9},{8,1... | collective-permute-start | bytes 196616 | tf_op jit(solution)/shard_map/ppermute | solution.py:260
  97.5 1.4 collective-permute-start.21
  101.1 2.4 %collective-permute-done.13.refs_2_ = f32[32,128]{1,0:T(8,128)S(1)} collective-permute-done((f32[32,128]{1,0:T(8,128)S(1)}, f32[32,128]{1,0:T(8,128)S(1)}, u32[]{:S(2)}, u32[]{:S(2)}) %collective-permute-start.13) | collective-permute-done | bytes 16416 | tf_op jit(solution)/shard_map/ppermute | solution.py:255
  103.8 1.6 %collective-permute-start.16 = (f32[32,128]{1,0:T(8,128)S(1)}, f32[32,128]{1,0:T(8,128)S(1)}, u32[]{:S(2)}, u32[]{:S(2)}) collective-permute-start(f32[32,128]{1,0:T(8,128)S(1)} %moves.2.refs_0_), channel_id=1, source_target_pairs={{0,2},{1,3},{2,0},{3,1},{4,6},{5,7},{6,4},{7,5},{8,10},{9,11},{10,... | collective-permute-start | bytes 49160 | tf_op jit(solution)/shard_map/ppermute | solution.py:255
  105.4 1.7 %collective-permute-done.17.refs_3_ = f32[32,128]{1,0:T(8,128)S(1)} collective-permute-done((f32[32,128]{1,0:T(8,128)S(1)}, f32[32,128]{1,0:T(8,128)S(1)}, u32[]{:S(2)}, u32[]{:S(2)}) %collective-permute-start.17) | collective-permute-done | bytes 16416 | tf_op jit(solution)/shard_map/ppermute | solution.py:255
  109.6 5.8 %copy-done.3 = bf16[512,128,128]{2,1,0:T(8,128)(2,1)S(1)} copy-done((bf16[512,128,128]{2,1,0:T(8,128)(2,1)S(1)}, bf16[512,128,128]{2,1,0:T(8,128)(2,1)}, u32[]{:S(2)}) %copy-start.3) | copy-done | bytes 16777240
  115.4 2.7 %dual.3 = (f32[4,32,256]{2,1,0:T(8,128)}, bf16[32,1024]{1,0:T(8,128)(2,1)}, f32[32,1]{1,0:T(8,128)}, bf16[32,2048]{1,0:T(8,128)(2,1)}) custom-call(s32[2]{0:T(128)} %pad_add_fusion.ids, bf16[512,128,128]{2,1,0:T(8,128)(2,1)S(1)} %copy-done.3, f32[32,1]{1,0:T(8,128)} %copy.30.step, f32[32,1]{1,0:T(8,128)} %copy-done.9, bf16[32,1024]{1,0:T(8,128)(2,1)} %forward.7.refs_0_, ...), custom_call_target="tpu_custom_call" | custom-call | tf_op jit(solution)/shard_map/dual/pallas_call | solution.py:325
  119.2 3.8 %backward.3 = (f32[32,2048]{1,0:T(8,128)}, bf16[32,2048]{1,0:T(8,128)(2,1)}, f32[32,2048]{1,0:T(8,128)}) custom-call(s32[3]{0:T(128)} %pad_add_fusion.1.chunks, bf16[512,128,128]{2,1,0:T(8,128)(2,1)S(1)} %copy-done.3, bf16[32,1024]{1,0:T(8,128)(2,1)} %get-tuple-element.33.d), custom_call_target="tpu_custom_call" | custom-call | tf_op jit(solution)/shard_map/backward/pallas_call | solution.py:211
  125.0 1.4 collective-permute-start.26
  126.4 2.1 %collective-permute-done.24.refs_1_ = bf16[32,2048]{1,0:T(8,128)(2,1)S(1)} collective-permute-done((bf16[32,2048]{1,0:T(8,128)(2,1)}, bf16[32,2048]{1,0:T(8,128)(2,1)S(1)}, u32[]{:S(2)}, u32[]{:S(2)}) %collective-permute-start.24) | collective-permute-done | bytes 131104 | tf_op jit(solution)/shard_map/ppermute | solution.py:255
  128.5 3.5 %collective-permute-done.26.refs_2_ = bf16[32,2048]{1,0:T(8,128)(2,1)S(1)} collective-permute-done((bf16[32,2048]{1,0:T(8,128)(2,1)S(1)}, bf16[32,2048]{1,0:T(8,128)(2,1)S(1)}, u32[]{:S(2)}, u32[]{:S(2)}) %collective-permute-start.26) | collective-permute-done | bytes 131104 | tf_op jit(solution)/shard_map/ppermute | solution.py:255
  133.8 2.2 %collective-permute-start.29 = (f32[32,128]{1,0:T(8,128)S(1)}, f32[32,128]{1,0:T(8,128)S(1)}, u32[]{:S(2)}, u32[]{:S(2)}) collective-permute-start(f32[32,128]{1,0:T(8,128)S(1)} %get-tuple-element.40.refs_0_), channel_id=1, source_target_pairs={{0,12},{4,8},{8,4},{12,0},{1,13},{5,9},{9,5},{13,1},{2,14},{6,10},... | collective-permute-start | bytes 49160 | tf_op jit(solution)/shard_map/ppermute | solution.py:255
  (130 shorter events, 38.2 us)
Async XLA Ops:
  1.4 23.7 %collective-permute-start.7 = (f32[2,32,256]{2,1,0:T(8,128)S(1)}, f32[2,32,256]{2,1,0:T(8,128)S(1)}, u32[]{:S(2)}, u32[]{:S(2)}) collective-permute-start(f32[2,32,256]{2,1,0:T(8,128)S(1)} %get-tuple-element.44), channel_id=1, source_target_pairs={{2,0},{3,1},{0,2},{1,3},{6,4},{7,5},{4,6},{5,7},{10,8},{11,9},{8,1... | collective-permute-start | bytes 196616 | tf_op jit(solution)/shard_map/ppermute | solution.py:260
  4.4 20.7 %collective-permute-start.6 = (f32[2,32,256]{2,1,0:T(8,128)S(1)}, f32[2,32,256]{2,1,0:T(8,128)S(1)}, u32[]{:S(2)}, u32[]{:S(2)}) collective-permute-start(f32[2,32,256]{2,1,0:T(8,128)S(1)} %get-tuple-element.44), channel_id=1, source_target_pairs={{1,0},{2,1},{3,2},{0,3},{5,4},{6,5},{7,6},{4,7},{9,8},{10,9},{11,1... | collective-permute-start | bytes 196616 | tf_op jit(solution)/shard_map/ppermute | solution.py:260
  4.4 20.7 %collective-permute-start.8 = (f32[2,32,256]{2,1,0:T(8,128)S(1)}, f32[2,32,256]{2,1,0:T(8,128)S(1)}, u32[]{:S(2)}, u32[]{:S(2)}) collective-permute-start(f32[2,32,256]{2,1,0:T(8,128)S(1)} %get-tuple-element.44), channel_id=1, source_target_pairs={{3,0},{0,1},{1,2},{2,3},{7,4},{4,5},{5,6},{6,7},{11,8},{8,9},{9,10... | collective-permute-start | bytes 196616 | tf_op jit(solution)/shard_map/ppermute | solution.py:260
  5.9 21.8 %collective-permute-start.2 = (bf16[32,2048]{1,0:T(8,128)(2,1)S(1)}, bf16[32,2048]{1,0:T(8,128)(2,1)S(1)}, u32[]{:S(2)}, u32[]{:S(2)}) collective-permute-start(bf16[32,2048]{1,0:T(8,128)(2,1)S(1)} %convert_element_type.15.refs_0_), channel_id=1, source_target_pairs={{0,4},{4,0},{8,12},{12,8},{1,5},{5,1},{9,13},{13,9},{2,6},{6,2},{1... | collective-permute-start | bytes 393224 | tf_op jit(solution)/shard_map/ppermute | solution.py:255
  7.6 18.2 %collective-permute-start = (bf16[32,2048]{1,0:T(8,128)(2,1)S(1)}, bf16[32,2048]{1,0:T(8,128)(2,1)S(1)}, u32[]{:S(2)}, u32[]{:S(2)}) collective-permute-start(bf16[32,2048]{1,0:T(8,128)(2,1)S(1)} %convert_element_type.15.refs_0_), channel_id=1, source_target_pairs={{0,12},{4,8},{8,4},{12,0},{1,13},{5,9},{9,5},{13,1},{2,14},{6,10},... | collective-permute-start | bytes 393224 | tf_op jit(solution)/shard_map/ppermute | solution.py:255
  25.7 13.9 %collective-permute-start.1 = (bf16[32,2048]{1,0:T(8,128)(2,1)S(1)}, bf16[32,2048]{1,0:T(8,128)(2,1)S(1)}, u32[]{:S(2)}, u32[]{:S(2)}) collective-permute-start(bf16[32,2048]{1,0:T(8,128)(2,1)S(1)} %collective-permute-done.refs_2_), channel_id=1, source_target_pairs={{0,4},{4,0},{8,12},{12,8},{1,5},{5,1},{9,13},{13,9},{2,6},{6,2},{1... | collective-permute-start | bytes 393224 | tf_op jit(solution)/shard_map/ppermute | solution.py:255
  43.2 4.0 %collective-permute-start.5 = (bf16[32,1024]{1,0:T(8,128)(2,1)}, bf16[32,1024]{1,0:T(8,128)(2,1)S(1)}, u32[]{:S(2)}, u32[]{:S(2)}) collective-permute-start(bf16[32,1024]{1,0:T(8,128)(2,1)} %forward.5.refs_0_), channel_id=1, source_target_pairs={{3,0},{0,1},{1,2},{2,3},{7,4},{4,5},{5,6},{6,7},{11,8},{8,9},{9,10... | collective-permute-start | bytes 196616 | tf_op jit(solution)/shard_map/ppermute | solution.py:260
  43.2 5.1 %collective-permute-start.4 = (bf16[32,1024]{1,0:T(8,128)(2,1)}, bf16[32,1024]{1,0:T(8,128)(2,1)S(1)}, u32[]{:S(2)}, u32[]{:S(2)}) collective-permute-start(bf16[32,1024]{1,0:T(8,128)(2,1)} %forward.5.refs_0_), channel_id=1, source_target_pairs={{2,0},{3,1},{0,2},{1,3},{6,4},{7,5},{4,6},{5,7},{10,8},{11,9},{8,1... | collective-permute-start | bytes 196616 | tf_op jit(solution)/shard_map/ppermute | solution.py:260
  44.0 4.3 %collective-permute-start.3 = (bf16[32,1024]{1,0:T(8,128)(2,1)}, bf16[32,1024]{1,0:T(8,128)(2,1)S(1)}, u32[]{:S(2)}, u32[]{:S(2)}) collective-permute-start(bf16[32,1024]{1,0:T(8,128)(2,1)} %forward.5.refs_0_), channel_id=1, source_target_pairs={{1,0},{2,1},{3,2},{0,3},{5,4},{6,5},{7,6},{4,7},{9,8},{10,9},{11,1... | collective-permute-start | bytes 196616 | tf_op jit(solution)/shard_map/ppermute | solution.py:260
  51.8 6.3 %collective-permute-start.10 = (bf16[32,2048]{1,0:T(8,128)(2,1)}, bf16[32,2048]{1,0:T(8,128)(2,1)S(1)}, u32[]{:S(2)}, u32[]{:S(2)}) collective-permute-start(bf16[32,2048]{1,0:T(8,128)(2,1)} %get-tuple-element.27), channel_id=1, source_target_pairs={{0,4},{4,0},{8,12},{12,8},{1,5},{5,1},{9,13},{13,9},{2,6},{6,2},{1... | collective-permute-start | bytes 393224 | tf_op jit(solution)/shard_map/ppermute | solution.py:255
  56.1 8.0 %collective-permute-start.9 = (bf16[32,2048]{1,0:T(8,128)(2,1)}, bf16[32,2048]{1,0:T(8,128)(2,1)S(1)}, u32[]{:S(2)}, u32[]{:S(2)}) collective-permute-start(bf16[32,2048]{1,0:T(8,128)(2,1)} %get-tuple-element.25), channel_id=1, source_target_pairs={{0,4},{4,0},{8,12},{12,8},{1,5},{5,1},{9,13},{13,9},{2,6},{6,2},{1... | collective-permute-start | bytes 393224 | tf_op jit(solution)/shard_map/ppermute | solution.py:255
  59.0 10.4 %collective-permute-start.11 = (bf16[32,2048]{1,0:T(8,128)(2,1)S(1)}, bf16[32,2048]{1,0:T(8,128)(2,1)S(1)}, u32[]{:S(2)}, u32[]{:S(2)}) collective-permute-start(bf16[32,2048]{1,0:T(8,128)(2,1)S(1)} %add_convert_fusion.1), channel_id=1, source_target_pairs={{0,12},{4,8},{8,4},{12,0},{1,13},{5,9},{9,5},{13,1},{2,14},{6,10},... | collective-permute-start | bytes 393224 | tf_op jit(solution)/shard_map/ppermute | solution.py:255
  70.7 8.3 %collective-permute-start.18 = (bf16[32,2048]{1,0:T(8,128)(2,1)S(1)}, bf16[32,2048]{1,0:T(8,128)(2,1)S(1)}, u32[]{:S(2)}, u32[]{:S(2)}) collective-permute-start(bf16[32,2048]{1,0:T(8,128)(2,1)S(1)} %get-tuple-element.30.refs_0_), channel_id=1, source_target_pairs={{0,12},{4,8},{8,4},{12,0},{1,13},{5,9},{9,5},{13,1},{2,14},{6,10},... | collective-permute-start | bytes 393224 | tf_op jit(solution)/shard_map/ppermute | solution.py:255
  72.4 7.6 %collective-permute-start.20 = (bf16[32,2048]{1,0:T(8,128)(2,1)S(1)}, bf16[32,2048]{1,0:T(8,128)(2,1)S(1)}, u32[]{:S(2)}, u32[]{:S(2)}) collective-permute-start(bf16[32,2048]{1,0:T(8,128)(2,1)S(1)} %get-tuple-element.30.refs_0_), channel_id=1, source_target_pairs={{0,4},{4,0},{8,12},{12,8},{1,5},{5,1},{9,13},{13,9},{2,6},{6,2},{1... | collective-permute-start | bytes 393224 | tf_op jit(solution)/shard_map/ppermute | solution.py:255
  79.0 12.8 %collective-permute-start.19 = (bf16[32,2048]{1,0:T(8,128)(2,1)S(1)}, bf16[32,2048]{1,0:T(8,128)(2,1)S(1)}, u32[]{:S(2)}, u32[]{:S(2)}) collective-permute-start(bf16[32,2048]{1,0:T(8,128)(2,1)S(1)} %collective-permute-done.18.refs_2_), channel_id=1, source_target_pairs={{0,4},{4,0},{8,12},{12,8},{1,5},{5,1},{9,13},{13,9},{2,6},{6,2},{1... | collective-permute-start | bytes 393224 | tf_op jit(solution)/shard_map/ppermute | solution.py:255
  79.0 20.8 %collective-permute-start.14 = (f32[32,128]{1,0:T(8,128)S(1)}, f32[32,128]{1,0:T(8,128)S(1)}, u32[]{:S(2)}, u32[]{:S(2)}) collective-permute-start(f32[32,128]{1,0:T(8,128)S(1)} %get-tuple-element.28.refs_0_), channel_id=1, source_target_pairs={{0,12},{4,8},{8,4},{12,0},{1,13},{5,9},{9,5},{13,1},{2,14},{6,10},... | collective-permute-start | bytes 49160 | tf_op jit(solution)/shard_map/ppermute | solution.py:255
  95.4 13.5 %collective-permute-start.23 = (bf16[32,1024]{1,0:T(8,128)(2,1)}, bf16[32,1024]{1,0:T(8,128)(2,1)S(1)}, u32[]{:S(2)}, u32[]{:S(2)}) collective-permute-start(bf16[32,1024]{1,0:T(8,128)(2,1)} %forward.7.refs_0_), channel_id=1, source_target_pairs={{3,0},{0,1},{1,2},{2,3},{7,4},{4,5},{5,6},{6,7},{11,8},{8,9},{9,10... | collective-permute-start | bytes 196616 | tf_op jit(solution)/shard_map/ppermute | solution.py:260
  95.4 13.5 %collective-permute-start.22 = (bf16[32,1024]{1,0:T(8,128)(2,1)}, bf16[32,1024]{1,0:T(8,128)(2,1)S(1)}, u32[]{:S(2)}, u32[]{:S(2)}) collective-permute-start(bf16[32,1024]{1,0:T(8,128)(2,1)} %forward.7.refs_0_), channel_id=1, source_target_pairs={{2,0},{3,1},{0,2},{1,3},{6,4},{7,5},{4,6},{5,7},{10,8},{11,9},{8,1... | collective-permute-start | bytes 196616 | tf_op jit(solution)/shard_map/ppermute | solution.py:260
  97.5 11.5 %collective-permute-start.21 = (bf16[32,1024]{1,0:T(8,128)(2,1)}, bf16[32,1024]{1,0:T(8,128)(2,1)S(1)}, u32[]{:S(2)}, u32[]{:S(2)}) collective-permute-start(bf16[32,1024]{1,0:T(8,128)(2,1)} %forward.7.refs_0_), channel_id=1, source_target_pairs={{1,0},{2,1},{3,2},{0,3},{5,4},{6,5},{7,6},{4,7},{9,8},{10,9},{11,1... | collective-permute-start | bytes 196616 | tf_op jit(solution)/shard_map/ppermute | solution.py:260
  98.9 4.6 %collective-permute-start.13 = (f32[32,128]{1,0:T(8,128)S(1)}, f32[32,128]{1,0:T(8,128)S(1)}, u32[]{:S(2)}, u32[]{:S(2)}) collective-permute-start(f32[32,128]{1,0:T(8,128)S(1)} %get-tuple-element.28.refs_0_), channel_id=1, source_target_pairs={{0,8},{4,12},{8,0},{12,4},{1,9},{5,13},{9,1},{13,5},{2,10},{6,14},... | collective-permute-start | bytes 49160 | tf_op jit(solution)/shard_map/ppermute | solution.py:255
  99.9 3.9 %collective-permute-start.12 = (f32[32,128]{1,0:T(8,128)S(1)}, f32[32,128]{1,0:T(8,128)S(1)}, u32[]{:S(2)}, u32[]{:S(2)}) collective-permute-start(f32[32,128]{1,0:T(8,128)S(1)} %get-tuple-element.28.refs_0_), channel_id=1, source_target_pairs={{0,4},{4,0},{8,12},{12,8},{1,5},{5,1},{9,13},{13,9},{2,6},{6,2},{1... | collective-permute-start | bytes 49160 | tf_op jit(solution)/shard_map/ppermute | solution.py:255
  103.7 3.4 %collective-permute-start.17 = (f32[32,128]{1,0:T(8,128)S(1)}, f32[32,128]{1,0:T(8,128)S(1)}, u32[]{:S(2)}, u32[]{:S(2)}) collective-permute-start(f32[32,128]{1,0:T(8,128)S(1)} %moves.2.refs_0_), channel_id=1, source_target_pairs={{0,3},{1,2},{2,1},{3,0},{4,7},{5,6},{6,5},{7,4},{8,11},{9,10},{10,... | collective-permute-start | bytes 49160 | tf_op jit(solution)/shard_map/ppermute | solution.py:255
  103.8 3.8 %collective-permute-start.16 = (f32[32,128]{1,0:T(8,128)S(1)}, f32[32,128]{1,0:T(8,128)S(1)}, u32[]{:S(2)}, u32[]{:S(2)}) collective-permute-start(f32[32,128]{1,0:T(8,128)S(1)} %moves.2.refs_0_), channel_id=1, source_target_pairs={{0,2},{1,3},{2,0},{3,1},{4,6},{5,7},{6,4},{7,5},{8,10},{9,11},{10,... | collective-permute-start | bytes 49160 | tf_op jit(solution)/shard_map/ppermute | solution.py:255
  118.1 5.8 %collective-permute-start.25 = (bf16[32,2048]{1,0:T(8,128)(2,1)}, bf16[32,2048]{1,0:T(8,128)(2,1)S(1)}, u32[]{:S(2)}, u32[]{:S(2)}) collective-permute-start(bf16[32,2048]{1,0:T(8,128)(2,1)} %get-tuple-element.37), channel_id=1, source_target_pairs={{0,4},{4,0},{8,12},{12,8},{1,5},{5,1},{9,13},{13,9},{2,6},{6,2},{1... | collective-permute-start | bytes 393224 | tf_op jit(solution)/shard_map/ppermute | solution.py:255
  123.0 5.5 %collective-permute-start.24 = (bf16[32,2048]{1,0:T(8,128)(2,1)}, bf16[32,2048]{1,0:T(8,128)(2,1)S(1)}, u32[]{:S(2)}, u32[]{:S(2)}) collective-permute-start(bf16[32,2048]{1,0:T(8,128)(2,1)} %get-tuple-element.35), channel_id=1, source_target_pairs={{0,4},{4,0},{8,12},{12,8},{1,5},{5,1},{9,13},{13,9},{2,6},{6,2},{1... | collective-permute-start | bytes 393224 | tf_op jit(solution)/shard_map/ppermute | solution.py:255
  125.0 7.0 %collective-permute-start.26 = (bf16[32,2048]{1,0:T(8,128)(2,1)S(1)}, bf16[32,2048]{1,0:T(8,128)(2,1)S(1)}, u32[]{:S(2)}, u32[]{:S(2)}) collective-permute-start(bf16[32,2048]{1,0:T(8,128)(2,1)S(1)} %add_convert_fusion), channel_id=1, source_target_pairs={{0,12},{4,8},{8,4},{12,0},{1,13},{5,9},{9,5},{13,1},{2,14},{6,10},... | collective-permute-start | bytes 393224 | tf_op jit(solution)/shard_map/ppermute | solution.py:255
  133.8 5.5 %collective-permute-start.29 = (f32[32,128]{1,0:T(8,128)S(1)}, f32[32,128]{1,0:T(8,128)S(1)}, u32[]{:S(2)}, u32[]{:S(2)}) collective-permute-start(f32[32,128]{1,0:T(8,128)S(1)} %get-tuple-element.40.refs_0_), channel_id=1, source_target_pairs={{0,12},{4,8},{8,4},{12,0},{1,13},{5,9},{9,5},{13,1},{2,14},{6,10},... | collective-permute-start | bytes 49160 | tf_op jit(solution)/shard_map/ppermute | solution.py:255
  136.0 4.6 %collective-permute-start.28 = (f32[32,128]{1,0:T(8,128)S(1)}, f32[32,128]{1,0:T(8,128)S(1)}, u32[]{:S(2)}, u32[]{:S(2)}) collective-permute-start(f32[32,128]{1,0:T(8,128)S(1)} %get-tuple-element.40.refs_0_), channel_id=1, source_target_pairs={{0,8},{4,12},{8,0},{12,4},{1,9},{5,13},{9,1},{13,5},{2,10},{6,14},... | collective-permute-start | bytes 49160 | tf_op jit(solution)/shard_map/ppermute | solution.py:255
  137.2 3.7 %collective-permute-start.27 = (f32[32,128]{1,0:T(8,128)S(1)}, f32[32,128]{1,0:T(8,128)S(1)}, u32[]{:S(2)}, u32[]{:S(2)}) collective-permute-start(f32[32,128]{1,0:T(8,128)S(1)} %get-tuple-element.40.refs_0_), channel_id=1, source_target_pairs={{0,4},{4,0},{8,12},{12,8},{1,5},{5,1},{9,13},{13,9},{2,6},{6,2},{1... | collective-permute-start | bytes 49160 | tf_op jit(solution)/shard_map/ppermute | solution.py:255
  141.0 3.3 %collective-permute-start.32 = (f32[32,128]{1,0:T(8,128)S(1)}, f32[32,128]{1,0:T(8,128)S(1)}, u32[]{:S(2)}, u32[]{:S(2)}) collective-permute-start(f32[32,128]{1,0:T(8,128)S(1)} %moves.3.refs_0_), channel_id=1, source_target_pairs={{0,3},{1,2},{2,1},{3,0},{4,7},{5,6},{6,5},{7,4},{8,11},{9,10},{10,... | collective-permute-start | bytes 49160 | tf_op jit(solution)/shard_map/ppermute | solution.py:255
  141.1 3.8 %collective-permute-start.31 = (f32[32,128]{1,0:T(8,128)S(1)}, f32[32,128]{1,0:T(8,128)S(1)}, u32[]{:S(2)}, u32[]{:S(2)}) collective-permute-start(f32[32,128]{1,0:T(8,128)S(1)} %moves.3.refs_0_), channel_id=1, source_target_pairs={{0,2},{1,3},{2,0},{3,1},{4,6},{5,7},{6,4},{7,5},{8,10},{9,11},{10,... | collective-permute-start | bytes 49160 | tf_op jit(solution)/shard_map/ppermute | solution.py:255
  142.4 2.5 %collective-permute-start.30 = (f32[32,128]{1,0:T(8,128)S(1)}, f32[32,128]{1,0:T(8,128)S(1)}, u32[]{:S(2)}, u32[]{:S(2)}) collective-permute-start(f32[32,128]{1,0:T(8,128)S(1)} %moves.3.refs_0_), channel_id=1, source_target_pairs={{0,1},{1,0},{2,3},{3,2},{4,5},{5,4},{6,7},{7,6},{8,9},{9,8},{10,11... | collective-permute-start | bytes 49160 | tf_op jit(solution)/shard_map/ppermute | solution.py:255
  (33 other events, 275.6 us)

commit v2 on v1

v2 whole, which is shorter than its diff:
```python
import functools

import jax
import jax.numpy as jnp
from jax import lax
from jax.experimental import pallas as pl
from jax.experimental.pallas import tpu as pltpu
from jax.sharding import PartitionSpec as P

ITERS = 2
EPSILON = 1e-06
COPIES = 4
GROUP = 8

SMEM = pl.BlockSpec(memory_space=pltpu.SMEM)
VMEM = pl.BlockSpec(memory_space=pltpu.VMEM)
ANY = pl.BlockSpec(memory_space=pl.ANY)
f32, bf16 = jnp.float32, jnp.bfloat16


def shape(dims, dtype):
    return pltpu.VMEM(dims, dtype)


def call(kernel, name, out_shape, args, specs=None, scratch=(), limit=8 << 20, cost=None):
    specs = specs or [VMEM] * len(args)
    out_specs = jax.tree.map(lambda _: VMEM, out_shape, is_leaf=lambda o: hasattr(o, "shape"))
    args = [
        pltpu.with_memory_space_constraint(a, pltpu.VMEM) if spec is VMEM else a
        for a, spec in zip(args, specs)
    ]
    return pl.pallas_call(
        kernel,
        out_shape=out_shape,
        in_specs=specs,
        out_specs=out_specs,
        scratch_shapes=scratch,
        compiler_params=pltpu.CompilerParams(vmem_limit_bytes=limit),
        cost_estimate=cost,
        name=name,
    )(*args)


def swap(array, axis, k):
    return lax.ppermute(array, axis, [(i, i ^ k) for i in range(lax.axis_size(axis))])


def partners(n):
    return list(range(n - 1, 0, -1))


def everyone(array, axis):
    got = {k: swap(array, axis, k) for k in partners(lax.axis_size(axis))}
    return [array] + [got[k] for k in sorted(got)]


def diagonal(n):
    return lax.broadcasted_iota(jnp.int32, (n, n), 0) == lax.broadcasted_iota(jnp.int32, (n, n), 1)


def to_column(line):
    n = line.shape[1]
    return jnp.sum(jnp.where(diagonal(n), line, 0.0), axis=1, keepdims=True)


def to_line(column):
    n = column.shape[0]
    return jnp.sum(jnp.where(diagonal(n), column, 0.0), axis=0, keepdims=True)


def tree_sum(parts):
    while len(parts) > 1:
        parts = [a + b for a, b in zip(parts[::2], parts[1::2])]
    return parts[0]


def pack_columns(columns, lanes):
    lane = lax.broadcasted_iota(jnp.int32, (columns[0].shape[0], lanes), 1)
    out = jnp.zeros(lane.shape, f32)
    for i, rest in enumerate(columns):
        for j in range(3):
            piece = rest.astype(bf16).astype(f32)
            out = jnp.where(lane == 3 * i + j, piece, out)
            rest = rest - piece
    return out.astype(bf16)


def unpack_columns(packed, n):
    packed = packed.astype(f32)
    pick = lambda i: packed[:, i : i + 1]
    return [pick(3 * i) + (pick(3 * i + 1) + pick(3 * i + 2)) for i in range(n)]


def densify_kernel(slots, places, rt, rows, cols, count, tiles, out, head, nxt, multi, stage, sem):
    live = jnp.minimum(count[0], slots)
    step = slots // COPIES
    zero = jnp.zeros(out.shape[1:], bf16)

    def copy(i):
        part = pl.ds(i * step, step)
        return pltpu.make_async_copy(tiles.at[part], stage.at[part], sem.at[i])

    for i in range(COPIES):
        copy(i).start()

    @pl.loop(0, places, unroll=16)
    def _(p):
        head[p] = -1

    def link(s, found):
        p = cols[s] * rt + rows[s]
        before = head[p]
        nxt[s] = before
        head[p] = s
        multi[found] = p
        return found + (before >= 0).astype(jnp.int32)

    clear = max(1, places // slots)

    def link_group(g, found):
        for i in range(GROUP):
            found = link(g * GROUP + i, found)
        for i in range(GROUP * clear):
            out[g * GROUP * clear + i] = zero
        return found

    groups = live // GROUP
    found = lax.fori_loop(0, groups, link_group, jnp.int32(0))
    found = lax.fori_loop(groups * GROUP, live, link, found)
    cleared = groups * (GROUP * clear)
    rest = (places - cleared) // GROUP

    @pl.loop(0, rest)
    def _(g):
        for i in range(GROUP):
            out[cleared + g * GROUP + i] = zero

    @pl.loop(cleared + rest * GROUP, places)
    def _(p):
        out[p] = zero

    def place(s):
        out[cols[s] * rt + rows[s]] = stage[s]

    for i in range(COPIES):
        copy(i).wait()
        here = jnp.clip(live - i * step, 0, step)
        whole = here // GROUP

        @pl.loop(0, whole)
        def _(g):
            for j in range(GROUP):
                place(i * step + g * GROUP + j)

        @pl.loop(i * step + whole * GROUP, i * step + here)
        def _(s):
            place(s)

    @pl.loop(0, found)
    def _(m):
        p = multi[m]
        first = head[p]

        @pl.when(first >= 0)
        def _():
            head[p] = -1
            second = nxt[first]

            def more(state):
                return state[0] >= 0

            def add(state):
                s, total = state
                return nxt[s], total + stage[s].astype(f32)

            pair = stage[first].astype(f32) + stage[second].astype(f32)
            _, total = lax.while_loop(more, add, (nxt[second], pair))
            out[p] = total.astype(bf16)


def densify(tiles, rows, cols, count, rt, ct):
    slots, height, width = tiles.shape
    places = rt * ct
    return call(
        functools.partial(densify_kernel, slots, places, rt),
        "densify",
        shape((places, height, width), bf16),
        [rows, cols, count, pltpu.with_memory_space_constraint(tiles, pltpu.HBM)],
        [SMEM, SMEM, SMEM, ANY],
        [
            pltpu.SMEM((places,), jnp.int32),
            pltpu.SMEM((slots,), jnp.int32),
            pltpu.SMEM((slots + 1,), jnp.int32),
            pltpu.VMEM(tiles.shape, bf16),
            pltpu.SemaphoreType.DMA((COPIES,)),
        ],
        limit=16 << 20,
        cost=pl.CostEstimate(flops=0, bytes_accessed=32 << 20, transcendentals=0),
    )


def columns(k, base, rt, first, n):
    parts = []
    for j in range(first, first + n):
        block = k[pl.ds(base + j * rt, rt)]
        parts.append(block.reshape(rt * block.shape[1], block.shape[2]))
    return jnp.concatenate(parts, axis=1) if n > 1 else parts[0]


def spans(per):
    return [(j, min(2, per - j)) for j in range(0, per, 2)]


def forward(k, x, chunk, rt, per):
    width = k.shape[2]
    total = None
    for j, n in spans(per):
        part = lax.dot_general(
            x[:, j * width : (j + n) * width],
            columns(k, chunk * (per * rt), rt, j, n),
            (((1,), (1,)), ((), ())),
            preferred_element_type=f32,
        )
        total = part if total is None else total + part
    return total


def backward(k, d, chunk, rt, per, store):
    width = k.shape[2]
    for j, n in spans(per):
        block = columns(k, chunk * (per * rt), rt, j, n)
        store(j * width, (j + n) * width, jnp.dot(d, block, preferred_element_type=f32))


def stack_kernel(y, rhs, both):
    both[0] = y[...]
    both[1] = rhs[...]


def cost(k, per, rt):
    chunk = per * rt * k.shape[1] * k.shape[2]
    return pl.CostEstimate(flops=64 * chunk, bytes_accessed=2 * chunk, transcendentals=0)


def forward_kernel(rt, per, i, has_base, n_move, k, x, *refs):
    total = forward(k, x, lax.axis_index("row") ^ i, rt, per)
    if has_base:
        total = total + refs[0][...]
    out, rows = refs[-1], total.shape[1]
    out[:, :rows] = total.astype(out.dtype)
    if n_move:
        shard = per * k.shape[2]
        moves = [unpack_columns(ref[:, shard:], 2) for ref in refs[has_base : has_base + n_move]]
        moves = [tree_sum([m[j] for m in moves]) for j in range(2)]
        out[:, rows:] = pack_columns(moves, out.shape[1] - rows)


def forward_parts(k, xs, rt, per, order, packed):
    scen, rows = xs[0].shape[0], rt * k.shape[1]
    base = []
    for i in order:
        last = i == order[-1]
        moves = xs if last and packed else []
        extra = k.shape[2] if moves else 0
        base = [
            call(
                functools.partial(forward_kernel, rt, per, i, len(base), len(moves)),
                "forward",
                shape((scen, rows + extra), bf16 if last else f32),
                [k, xs[i], *base, *moves],
                cost=cost(k, per, rt),
            )
        ]
    return base[0]


def new_weight(weight, primal, dual):
    return jnp.sqrt(weight * jnp.sqrt(primal + EPSILON) / jnp.sqrt(dual + EPSILON))


def dual_kernel(rt, per, n_col, packed, has_y, first, k, step, weight, *refs):
    row, col = lax.axis_index("row"), lax.axis_index("col")
    parts, both, refs = refs[:n_col], refs[n_col : 2 * n_col], refs[2 * n_col :]
    y_out, bar_out, move_out, send_out, weight_out = refs[has_y:]
    w = to_column(weight[...])
    if packed:
        moves = [unpack_columns(part[:, bar_out.shape[1] :], 2) for part in parts]
        w = new_weight(w, *[tree_sum([m[j] for m in moves]) for j in range(2)])
    weight_out[...] = to_line(w)
    sigma = to_column(step[...]) * w
    width = y_out.shape[-1]
    for c in range(n_col):
        here = pl.ds(pl.multiple_of((col ^ c) * width, width), width)
        total = tree_sum([part[:, here].astype(f32) for part in parts])
        old = refs[0][c] if has_y else both[c][0]
        new = jnp.maximum(old + sigma * (both[c][1] - total), 0.0)
        if c == 0:
            move_out[...] = jnp.sum((new - old) ** 2, axis=1, keepdims=True)
        if len(y_out.shape) == 3:
            y_out[c] = new
        elif c == 0:
            y_out[...] = new
        bar_out[:, here] = (2.0 * new - old).astype(bf16)

    def store(low, high, value):
        send_out[:, low:high] = value.astype(send_out.dtype)

    backward(k, bar_out[...], row ^ first, rt, per, store)


def backward_kernel(rt, per, i, k, d, out):
    def store(low, high, value):
        out[:, low:high] = value.astype(out.dtype)

    backward(k, d[...], lax.axis_index("row") ^ i, rt, per, store)


def backward_part(k, d, i, dtype, rt, per):
    return call(
        functools.partial(backward_kernel, rt, per, i),
        "backward",
        shape((d.shape[0], per * k.shape[2]), dtype),
        [k, d],
        cost=cost(k, per, rt),
    )


def primal_kernel(n_part, step, weight, x, objective, low, high, kind, dual_move, *refs):
    parts, outs = refs[:n_part], refs[n_part:]
    total = parts[0][...].astype(f32)
    for part in parts[1:]:
        total = total + part[...].astype(f32)
    tau = to_column(step[...]) / to_column(weight[...])
    old = x[...]
    new = old - tau * (objective[...] - total)
    new = jnp.where(kind[...] >= 1, jnp.maximum(new, low[...]), new)
    new = jnp.where(kind[...] == 2, jnp.minimum(new, high[...]), new)
    outs[0][...] = new
    primal_move = jnp.sum((new - old) ** 2, axis=1, keepdims=True)
    width = new.shape[1]
    if outs[1].dtype == bf16:
        outs[1][:, :width] = new.astype(bf16)
        moves = [primal_move, dual_move[...]]
        outs[1][:, width:] = pack_columns(moves, outs[1].shape[1] - width)
    else:
        lane = lax.broadcasted_iota(jnp.int32, outs[1].shape, 1)
        outs[1][...] = jnp.where(lane == 0, primal_move, dual_move[...])


def sum_kernel(*refs):
    refs[-1][...] = tree_sum([ref[...] for ref in refs[:-1]])


def weight_kernel(weight, *refs):
    total = tree_sum([ref[...] for ref in refs[:-1]])
    w = new_weight(to_column(weight[...]), total[:, 0:1], total[:, 1:2])
    refs[-1][...] = to_line(w)


def body(
    tile_values,
    tile_rows,
    tile_cols,
    tile_count,
    primal_vars,
    dual_vars,
    objective,
    right_side,
    lower_bound,
    upper_bound,
    bound_kind,
    step_size,
    primal_weight,
):
    tiles = tile_values.reshape(tile_values.shape[2:])
    width = tiles.shape[-1]
    n_row, n_col = lax.axis_size("row"), lax.axis_size("col")
    scen, shard = primal_vars.shape
    per = shard // width
    rt = dual_vars.shape[1] * n_col // width
    ct = per * n_row
    order = [0, 1] + partners(n_row)[:-1]

    xs = everyone(primal_vars.astype(bf16), "row")
    k = densify(
        tiles, tile_rows.reshape(-1), tile_cols.reshape(-1), tile_count.reshape(-1), rt, ct
    )
    y, rhs, k = lax.optimization_barrier((dual_vars, right_side, k))
    both = call(stack_kernel, "stack", shape((2,) + y.shape, f32), [y, rhs])
    both = everyone(both, "col")
    step = step_size[None]
    weight = primal_weight[None]
    low_bound, high_bound, kind = lower_bound[None], upper_bound[None], bound_kind[None]
    x, y, packed = primal_vars, [], False
    for sweep in range(ITERS):
        last = sweep == ITERS - 1
        part = forward_parts(k, xs, rt, per, order, packed)
        first, *others = partners(n_row)
        y, bar, dual_move, sent, weight = call(
            functools.partial(dual_kernel, rt, per, n_col, packed, len(y), first),
            "dual",
            [
                shape(dual_vars.shape if last else (n_col,) + dual_vars.shape, f32),
                shape((scen, rt * width), bf16),
                shape((scen, 1), f32),
                shape((scen, shard), bf16),
                shape((1, scen), f32),
            ],
            [k, step, weight, *everyone(part, "col"), *both, *y],
            cost=cost(k, per, rt),
        )
        totals = [swap(sent, "row", first)]
        for i in others:
            sent = backward_part(k, bar, i, bf16, rt, per)
            totals.append(swap(sent, "row", i))
            sent, bar = lax.optimization_barrier((sent, bar))
        totals.insert(0, backward_part(k, bar, 0, f32, rt, per))
        x, low = call(
            functools.partial(primal_kernel, len(totals)),
            "primal",
            [
                shape(x.shape, f32),
                shape((scen, width), f32) if last else shape((scen, shard + width), bf16),
            ],
            [step, weight, x, objective, low_bound, high_bound, kind, dual_move, *totals],
        )
        y, packed = [y], True
        if not last:
            xs = everyone(low, "row")
    move = call(sum_kernel, "moves", shape(low.shape, f32), everyone(low, "row"))
    weight = call(
        weight_kernel, "weight", shape((1, scen), f32), [weight, *everyone(move, "col")]
    )
    return x, y[0], weight.reshape(-1)


def solution(mesh):
    return jax.shard_map(
        body,
        mesh=mesh,
        in_specs=(
            P(("grp", "row"), "col", None, None, None),
            P(("grp", "row"), "col", None),
            P(("grp", "row"), "col", None),
            P(("grp", "row"), "col"),
            P("grp", ("col", "row")),
            P("grp", ("row", "col")),
            P("grp", ("col", "row")),
            P("grp", ("row", "col")),
            P(("grp", "col", "row")),
            P(("grp", "col", "row")),
            P(("grp", "col", "row")),
            P("grp"),
            P("grp"),
        ),
        out_specs=(P("grp", ("col", "row")), P("grp", ("row", "col")), P("grp")),
        check_vma=False,
    )
```

time: 147 us -> 94.7 us (0.64)
  local copies, waits for them, and re-layouts: 34.9 us -> 3.25 us
  Pallas kernels: 35.7 us -> 22.4 us
  starting transfers between devices: 39 us -> 33.3 us
  other arithmetic: 5.87 us -> 0.98 us
  waiting for transfers between devices: 28.5 us -> 33.2 us
    unnamed x64 -> x25, local copies, waits for them, and re-layouts: 29.5 us -> 3.25 us
    pallas_call x15 -> x22, Pallas kernels: 35.7 us -> 22.4 us  [call(): pl.pallas_call(kernel, out_shape=out_shape, in_specs=specs, out_specs=out...]
    ppermute x33 -> x27, starting transfers between devices: 39 us -> 33.3 us  [swap(): lax.ppermute(array, axis, [(i, i ^ k) for i in range(lax.axis_size(axis))])]
    ppermute x33 -> x27, waiting for transfers between devices: 28.5 us -> 33.2 us  [swap(): lax.ppermute(array, axis, [(i, i ^ k) for i in range(lax.axis_size(axis))])]
    broadcast_in_dim x2 -> x0, local copies, waits for them, and re-layouts: 2.68 us -> none  [the longest x1 1.34 us: body(): step = step_size[:, None]]
    squeeze x2 -> x0, local copies, waits for them, and re-layouts: 2.09 us -> none  [the longest x1 1.37 us: body(): dual = lax.dynamic_index_in_dim(y, col, 0, keepdims=False)]
    another operation x4 -> x0, other arithmetic: 2.05 us -> none  [the longest x2 0.8 us: body(): both = jnp.take(jnp.stack(both), order, axis=0)]
    convert_element_type x3 -> x1, other arithmetic: 2.94 us -> 0.98 us  [body(): xs = everyone(primal_vars.astype(bf16), 'row')]
  transfers between devices with their start and end apart: 33 -> 27, of which waited for: 16 -> 15; matrix products, arithmetic and copies ran while one was open for 7% -> 1% of each run, Pallas kernels for 18% -> 17%
where the time goes in v2:
time: 94.7 us
  starting transfers between devices  33.3 us (35%)
  waiting for transfers between devices  33.2 us (35%)
  Pallas kernels  22.4 us (24%)
  local copies, waits for them, and re-layouts  3.25 us (3%)
  between operations  1.56 us (2%)
  other arithmetic  0.98 us (1%)
    ppermute x27, starting transfers between devices, swap(): lax.ppermute(array, axis, [(i, i ^ k) for i in range(lax.axis_size(axis))])  33.3 us
    ppermute x27, waiting for transfers between devices, swap(): lax.ppermute(array, axis, [(i, i ^ k) for i in range(lax.axis_size(axis))])  33.2 us
    pallas_call x22, Pallas kernels, call(): pl.pallas_call(kernel, out_shape=out_shape, in_specs=specs, out_specs=out...  22.4 us
    unnamed x25, local copies, waits for them, and re-layouts  3.25 us
  transfers between devices with their start and end apart: 27, of which 15 were waited for; matrix products, arithmetic and copies ran while one was open for 1% of the time, Pallas kernels for 17%

profile of v2, /device:TPU:0, one launch (start us, length us, event | category | flops | bytes accessed | tf_op | source)
XLA Modules:
  0.0 94.7 jit_solution(1136616642549609537)
XLA Ops:
  1.6 3.1 %collective-permute-start.2 = (bf16[32,2048]{1,0:T(8,128)(2,1)S(1)}, bf16[32,2048]{1,0:T(8,128)(2,1)S(1)}, u32[]{:S(2)}, u32[]{:S(2)}) collective-permute-start(bf16[32,2048]{1,0:T(8,128)(2,1)S(1)} %convert_element_type.3.x), channel_id=1, source_target_pairs={{0,4},{4,0},{8,12},{12,8},{1,5},{5,1},{9,13},{13,9},{2,6},{6,2},{1... | collective-permute-start | bytes 393224 | tf_op jit(solution)/shard_map/ppermute | solution.py:45
  4.7 2.5 %collective-permute-start.1 = (bf16[32,2048]{1,0:T(8,128)(2,1)S(1)}, bf16[32,2048]{1,0:T(8,128)(2,1)S(1)}, u32[]{:S(2)}, u32[]{:S(2)}) collective-permute-start(bf16[32,2048]{1,0:T(8,128)(2,1)S(1)} %convert_element_type.3.x), channel_id=1, source_target_pairs={{0,12},{4,8},{8,4},{12,0},{1,13},{5,9},{9,5},{13,1},{2,14},{6,10},... | collective-permute-start | bytes 393224 | tf_op jit(solution)/shard_map/ppermute | solution.py:45
  9.3 4.1 %densify.1.k = bf16[512,128,128]{2,1,0:T(8,128)(2,1)S(1)} custom-call(s32[256]{0:T(256)S(1)} %bitcast.22, s32[256]{0:T(256)S(1)} %bitcast.23, s32[1]{0:T(128)} %bitcast.10.count, bf16[256,128,128]{2,1,0:T(8,128)(2,1)} %bitcast.25), custom_call_target="tpu_custom_call" | custom-call | bytes 33554432 | tf_op jit(solution)/shard_map/densify/pallas_call | solution.py:32
  14.2 3.6 %collective-permute-start.7 = (f32[2,32,256]{2,1,0:T(8,128)S(1)}, f32[2,32,256]{2,1,0:T(8,128)S(1)}, u32[]{:S(2)}, u32[]{:S(2)}) collective-permute-start(f32[2,32,256]{2,1,0:T(8,128)S(1)} %stack.1.refs_4_), channel_id=1, source_target_pairs={{0,2},{1,3},{2,0},{3,1},{4,6},{5,7},{6,4},{7,5},{8,10},{9,11},{10,... | collective-permute-start | bytes 196616 | tf_op jit(solution)/shard_map/ppermute | solution.py:45
  17.8 1.3 %forward.8.refs_0_ = f32[32,1024]{1,0:T(8,128)S(1)} custom-call(bf16[512,128,128]{2,1,0:T(8,128)(2,1)S(1)} %densify.1.k, bf16[32,2048]{1,0:T(8,128)(2,1)S(1)} %convert_element_type.3.x), custom_call_target="tpu_custom_call" | custom-call | flops 134217728 | bytes 4194304 | tf_op jit(solution)/shard_map/forward/pallas_call | solution.py:32
  19.2 1.3 %forward.9.refs_0_ = f32[32,1024]{1,0:T(8,128)S(1)} custom-call(bf16[512,128,128]{2,1,0:T(8,128)(2,1)S(1)} %densify.1.k, bf16[32,2048]{1,0:T(8,128)(2,1)S(1)} %collective-permute-done.2.x, f32[32,1024]{1,0:T(8,128)S(1)} %forward.8.refs_0_), custom_call_target="tpu_custom_call" | custom-call | flops 134217728 | bytes 4194304 | tf_op jit(solution)/shard_map/forward/pallas_call | solution.py:32
  20.6 1.3 %forward.10.refs_0_ = f32[32,1024]{1,0:T(8,128)S(1)} custom-call(bf16[512,128,128]{2,1,0:T(8,128)(2,1)S(1)} %densify.1.k, bf16[32,2048]{1,0:T(8,128)(2,1)S(1)} %collective-permute-done.1.x, f32[32,1024]{1,0:T(8,128)S(1)} %forward.9.refs_0_), custom_call_target="tpu_custom_call" | custom-call | flops 134217728 | bytes 4194304 | tf_op jit(solution)/shard_map/forward/pallas_call | solution.py:32
  21.9 1.3 %forward.11.refs_0_ = bf16[32,1024]{1,0:T(8,128)(2,1)S(1)} custom-call(bf16[512,128,128]{2,1,0:T(8,128)(2,1)S(1)} %densify.1.k, bf16[32,2048]{1,0:T(8,128)(2,1)S(1)} %collective-permute-done.x, f32[32,1024]{1,0:T(8,128)S(1)} %forward.10.refs_0_), custom_call_target="tpu_custom_call" | custom-call | flops 134217728 | bytes 4194304 | tf_op jit(solution)/shard_map/forward/pallas_call | solution.py:32
  23.2 1.4 %collective-permute-start.5 = (bf16[32,1024]{1,0:T(8,128)(2,1)S(1)}, bf16[32,1024]{1,0:T(8,128)(2,1)S(1)}, u32[]{:S(2)}, u32[]{:S(2)}) collective-permute-start(bf16[32,1024]{1,0:T(8,128)(2,1)S(1)} %forward.11.refs_0_), channel_id=1, source_target_pairs={{0,3},{1,2},{2,1},{3,0},{4,7},{5,6},{6,5},{7,4},{8,11},{9,10},{10,... | collective-permute-start | bytes 196616 | tf_op jit(solution)/shard_map/ppermute | solution.py:45
  25.4 1.7 %collective-permute-done.5.refs_3_ = bf16[32,1024]{1,0:T(8,128)(2,1)S(1)} collective-permute-done((bf16[32,1024]{1,0:T(8,128)(2,1)S(1)}, bf16[32,1024]{1,0:T(8,128)(2,1)S(1)}, u32[]{:S(2)}, u32[]{:S(2)}) %collective-permute-start.5) | collective-permute-done | bytes 65568 | tf_op jit(solution)/shard_map/ppermute | solution.py:45
  27.2 2.0 %collective-permute-done.4.refs_2_ = bf16[32,1024]{1,0:T(8,128)(2,1)S(1)} collective-permute-done((bf16[32,1024]{1,0:T(8,128)(2,1)S(1)}, bf16[32,1024]{1,0:T(8,128)(2,1)S(1)}, u32[]{:S(2)}, u32[]{:S(2)}) %collective-permute-start.4) | collective-permute-done | bytes 65568 | tf_op jit(solution)/shard_map/ppermute | solution.py:45
  31.0 2.9 %collective-permute-start.10 = (bf16[32,2048]{1,0:T(8,128)(2,1)S(1)}, bf16[32,2048]{1,0:T(8,128)(2,1)S(1)}, u32[]{:S(2)}, u32[]{:S(2)}) collective-permute-start(bf16[32,2048]{1,0:T(8,128)(2,1)S(1)} %backward.6), channel_id=1, source_target_pairs={{0,8},{4,12},{8,0},{12,4},{1,9},{5,13},{9,1},{13,5},{2,10},{6,14},... | collective-permute-start | bytes 393224 | tf_op jit(solution)/shard_map/ppermute | solution.py:45
  34.8 1.5 %collective-permute-start.9 = (bf16[32,2048]{1,0:T(8,128)(2,1)S(1)}, bf16[32,2048]{1,0:T(8,128)(2,1)S(1)}, u32[]{:S(2)}, u32[]{:S(2)}) collective-permute-start(bf16[32,2048]{1,0:T(8,128)(2,1)S(1)} %get-tuple-element.32), channel_id=1, source_target_pairs={{0,12},{4,8},{8,4},{12,0},{1,13},{5,9},{9,5},{13,1},{2,14},{6,10},... | collective-permute-start | bytes 393224 | tf_op jit(solution)/shard_map/ppermute | solution.py:45
  37.1 7.2 %collective-permute-done.11.refs_3_ = bf16[32,2048]{1,0:T(8,128)(2,1)S(1)} collective-permute-done((bf16[32,2048]{1,0:T(8,128)(2,1)S(1)}, bf16[32,2048]{1,0:T(8,128)(2,1)S(1)}, u32[]{:S(2)}, u32[]{:S(2)}) %collective-permute-start.11) | collective-permute-done | bytes 131104 | tf_op jit(solution)/shard_map/ppermute | solution.py:45
  45.4 1.8 %collective-permute-start.13 = (bf16[32,2176]{1,0:T(8,128)(2,1)S(1)}, bf16[32,2176]{1,0:T(8,128)(2,1)S(1)}, u32[]{:S(2)}, u32[]{:S(2)}) collective-permute-start(bf16[32,2176]{1,0:T(8,128)(2,1)S(1)} %get-tuple-element.33.x.refs_1_), channel_id=1, source_target_pairs={{0,12},{4,8},{8,4},{12,0},{1,13},{5,9},{9,5},{13,1},{2,14},{6,10},... | collective-permute-start | bytes 417800 | tf_op jit(solution)/shard_map/ppermute | solution.py:45
  48.3 1.3 %forward.12.refs_0_ = f32[32,1024]{1,0:T(8,128)S(1)} custom-call(bf16[512,128,128]{2,1,0:T(8,128)(2,1)S(1)} %densify.1.k, bf16[32,2176]{1,0:T(8,128)(2,1)S(1)} %get-tuple-element.33.x.refs_1_), custom_call_target="tpu_custom_call" | custom-call | flops 134217728 | bytes 4194304 | tf_op jit(solution)/shard_map/forward/pallas_call | solution.py:32
  49.6 3.1 %collective-permute-done.14.x.refs_2_ = bf16[32,2176]{1,0:T(8,128)(2,1)S(1)} collective-permute-done((bf16[32,2176]{1,0:T(8,128)(2,1)S(1)}, bf16[32,2176]{1,0:T(8,128)(2,1)S(1)}, u32[]{:S(2)}, u32[]{:S(2)}) %collective-permute-start.14) | collective-permute-done | bytes 139296 | tf_op jit(solution)/shard_map/ppermute | solution.py:45
  52.7 1.3 %forward.13.refs_0_ = f32[32,1024]{1,0:T(8,128)S(1)} custom-call(bf16[512,128,128]{2,1,0:T(8,128)(2,1)S(1)} %densify.1.k, bf16[32,2176]{1,0:T(8,128)(2,1)S(1)} %collective-permute-done.14.x.refs_2_, f32[32,1024]{1,0:T(8,128)S(1)} %forward.12.refs_0_), custom_call_target="tpu_custom_call" | custom-call | flops 134217728 | bytes 4194304 | tf_op jit(solution)/shard_map/forward/pallas_call | solution.py:32
  54.0 1.3 %forward.14.refs_0_ = f32[32,1024]{1,0:T(8,128)S(1)} custom-call(bf16[512,128,128]{2,1,0:T(8,128)(2,1)S(1)} %densify.1.k, bf16[32,2176]{1,0:T(8,128)(2,1)S(1)} %collective-permute-done.13.x.refs_4_, f32[32,1024]{1,0:T(8,128)S(1)} %forward.13.refs_0_), custom_call_target="tpu_custom_call" | custom-call | flops 134217728 | bytes 4194304 | tf_op jit(solution)/shard_map/forward/pallas_call | solution.py:32
  55.4 5.2 %collective-permute-done.12.x.refs_3_ = bf16[32,2176]{1,0:T(8,128)(2,1)S(1)} collective-permute-done((bf16[32,2176]{1,0:T(8,128)(2,1)S(1)}, bf16[32,2176]{1,0:T(8,128)(2,1)S(1)}, u32[]{:S(2)}, u32[]{:S(2)}) %collective-permute-start.12) | collective-permute-done | bytes 139296 | tf_op jit(solution)/shard_map/ppermute | solution.py:45
  60.5 1.3 %forward.15.refs_0_ = bf16[32,1152]{1,0:T(8,128)(2,1)S(1)} custom-call(bf16[512,128,128]{2,1,0:T(8,128)(2,1)S(1)} %densify.1.k, bf16[32,2176]{1,0:T(8,128)(2,1)S(1)} %collective-permute-done.12.x.refs_3_, f32[32,1024]{1,0:T(8,128)S(1)} %forward.14.refs_0_, bf16[32,2176]{1,0:T(8,128)(2,1)S(1)} %get-tuple-element.33.x.refs_1_, ...), custom_call_target="tpu_custom_call" | custom-call | flops 134217728 | bytes 4194304 | tf_op jit(solution)/shard_map/forward/pallas_call | solution.py:32
  63.8 2.5 %collective-permute-done.17.refs_3_ = bf16[32,1152]{1,0:T(8,128)(2,1)S(1)} collective-permute-done((bf16[32,1152]{1,0:T(8,128)(2,1)S(1)}, bf16[32,1152]{1,0:T(8,128)(2,1)S(1)}, u32[]{:S(2)}, u32[]{:S(2)}) %collective-permute-start.17) | collective-permute-done | bytes 73760 | tf_op jit(solution)/shard_map/ppermute | solution.py:45
  67.1 1.2 %dual.3 = (f32[32,256]{1,0:T(8,128)S(1)}, bf16[32,1024]{1,0:T(8,128)(2,1)S(1)}, f32[32,1]{1,0:T(8,128)S(1)}, bf16[32,2048]{1,0:T(8,128)(2,1)S(1)}, f32[1,32]{1,0:T(1,128)S(1)}) custom-call(bf16[512,128,128]{2,1,0:T(8,128)(2,1)S(1)} %densify.1.k, f32[1,32]{1,0:T(1,128)S(1)} %bitcast.20, f32[1,32]{1,0:T(1,128)S(1)} %get-tuple-element.27.weight, ...), custom_call_target="tpu_custom_call" | custom-call | flops 134217728 | bytes 4194304 | tf_op jit(solution)/shard_map/dual/pallas_call | solution.py:32
  70.4 1.6 %collective-permute-start.20 = (bf16[32,2048]{1,0:T(8,128)(2,1)S(1)}, bf16[32,2048]{1,0:T(8,128)(2,1)S(1)}, u32[]{:S(2)}, u32[]{:S(2)}) collective-permute-start(bf16[32,2048]{1,0:T(8,128)(2,1)S(1)} %backward.10), channel_id=1, source_target_pairs={{0,4},{4,0},{8,12},{12,8},{1,5},{5,1},{9,13},{13,9},{2,6},{6,2},{1... | collective-permute-start | bytes 393224 | tf_op jit(solution)/shard_map/ppermute | solution.py:45
  72.0 2.3 %collective-permute-start.18 = (bf16[32,2048]{1,0:T(8,128)(2,1)S(1)}, bf16[32,2048]{1,0:T(8,128)(2,1)S(1)}, u32[]{:S(2)}, u32[]{:S(2)}) collective-permute-start(bf16[32,2048]{1,0:T(8,128)(2,1)S(1)} %get-tuple-element.41), channel_id=1, source_target_pairs={{0,12},{4,8},{8,4},{12,0},{1,13},{5,9},{9,5},{13,1},{2,14},{6,10},... | collective-permute-start | bytes 393224 | tf_op jit(solution)/shard_map/ppermute | solution.py:45
  75.1 1.3 %collective-permute-done.20.refs_3_ = bf16[32,2048]{1,0:T(8,128)(2,1)S(1)} collective-permute-done((bf16[32,2048]{1,0:T(8,128)(2,1)S(1)}, bf16[32,2048]{1,0:T(8,128)(2,1)S(1)}, u32[]{:S(2)}, u32[]{:S(2)}) %collective-permute-start.20) | collective-permute-done | bytes 131104 | tf_op jit(solution)/shard_map/ppermute | solution.py:45
  76.4 2.8 %collective-permute-done.19.refs_2_ = bf16[32,2048]{1,0:T(8,128)(2,1)S(1)} collective-permute-done((bf16[32,2048]{1,0:T(8,128)(2,1)S(1)}, bf16[32,2048]{1,0:T(8,128)(2,1)S(1)}, u32[]{:S(2)}, u32[]{:S(2)}) %collective-permute-start.19) | collective-permute-done | bytes 131104 | tf_op jit(solution)/shard_map/ppermute | solution.py:45
  79.2 2.1 %collective-permute-done.18.refs_1_ = bf16[32,2048]{1,0:T(8,128)(2,1)S(1)} collective-permute-done((bf16[32,2048]{1,0:T(8,128)(2,1)S(1)}, bf16[32,2048]{1,0:T(8,128)(2,1)S(1)}, u32[]{:S(2)}, u32[]{:S(2)}) %collective-permute-start.18) | collective-permute-done | bytes 131104 | tf_op jit(solution)/shard_map/ppermute | solution.py:45
  81.6 2.4 %collective-permute-start.23 = (f32[32,128]{1,0:T(8,128)S(1)}, f32[32,128]{1,0:T(8,128)S(1)}, u32[]{:S(2)}, u32[]{:S(2)}) collective-permute-start(f32[32,128]{1,0:T(8,128)S(1)} %get-tuple-element.44.refs_0_), channel_id=1, source_target_pairs={{0,12},{4,8},{8,4},{12,0},{1,13},{5,9},{9,5},{13,1},{2,14},{6,10},... | collective-permute-start | bytes 49160 | tf_op jit(solution)/shard_map/ppermute | solution.py:45
  84.0 2.3 %collective-permute-start.22 = (f32[32,128]{1,0:T(8,128)S(1)}, f32[32,128]{1,0:T(8,128)S(1)}, u32[]{:S(2)}, u32[]{:S(2)}) collective-permute-start(f32[32,128]{1,0:T(8,128)S(1)} %get-tuple-element.44.refs_0_), channel_id=1, source_target_pairs={{0,8},{4,12},{8,0},{12,4},{1,9},{5,13},{9,1},{13,5},{2,10},{6,14},... | collective-permute-start | bytes 49160 | tf_op jit(solution)/shard_map/ppermute | solution.py:45
  87.3 1.4 %collective-permute-done.22.refs_2_ = f32[32,128]{1,0:T(8,128)S(1)} collective-permute-done((f32[32,128]{1,0:T(8,128)S(1)}, f32[32,128]{1,0:T(8,128)S(1)}, u32[]{:S(2)}, u32[]{:S(2)}) %collective-permute-start.22) | collective-permute-done | bytes 16416 | tf_op jit(solution)/shard_map/ppermute | solution.py:45
  88.8 1.3 %collective-permute-done.21.refs_1_ = f32[32,128]{1,0:T(8,128)S(1)} collective-permute-done((f32[32,128]{1,0:T(8,128)S(1)}, f32[32,128]{1,0:T(8,128)S(1)}, u32[]{:S(2)}, u32[]{:S(2)}) %collective-permute-start.21) | collective-permute-done | bytes 16416 | tf_op jit(solution)/shard_map/ppermute | solution.py:45
  (70 shorter events, 21.1 us)
Async XLA Ops:
  1.6 17.5 %collective-permute-start.2 = (bf16[32,2048]{1,0:T(8,128)(2,1)S(1)}, bf16[32,2048]{1,0:T(8,128)(2,1)S(1)}, u32[]{:S(2)}, u32[]{:S(2)}) collective-permute-start(bf16[32,2048]{1,0:T(8,128)(2,1)S(1)} %convert_element_type.3.x), channel_id=1, source_target_pairs={{0,4},{4,0},{8,12},{12,8},{1,5},{5,1},{9,13},{13,9},{2,6},{6,2},{1... | collective-permute-start | bytes 393224 | tf_op jit(solution)/shard_map/ppermute | solution.py:45
  4.7 15.8 %collective-permute-start.1 = (bf16[32,2048]{1,0:T(8,128)(2,1)S(1)}, bf16[32,2048]{1,0:T(8,128)(2,1)S(1)}, u32[]{:S(2)}, u32[]{:S(2)}) collective-permute-start(bf16[32,2048]{1,0:T(8,128)(2,1)S(1)} %convert_element_type.3.x), channel_id=1, source_target_pairs={{0,12},{4,8},{8,4},{12,0},{1,13},{5,9},{9,5},{13,1},{2,14},{6,10},... | collective-permute-start | bytes 393224 | tf_op jit(solution)/shard_map/ppermute | solution.py:45
  7.2 14.7 %collective-permute-start = (bf16[32,2048]{1,0:T(8,128)(2,1)S(1)}, bf16[32,2048]{1,0:T(8,128)(2,1)S(1)}, u32[]{:S(2)}, u32[]{:S(2)}) collective-permute-start(bf16[32,2048]{1,0:T(8,128)(2,1)S(1)} %convert_element_type.3.x), channel_id=1, source_target_pairs={{0,8},{4,12},{8,0},{12,4},{1,9},{5,13},{9,1},{13,5},{2,10},{6,14},... | collective-permute-start | bytes 393224 | tf_op jit(solution)/shard_map/ppermute | solution.py:45
  13.4 12.0 %collective-permute-start.8 = (f32[2,32,256]{2,1,0:T(8,128)S(1)}, f32[2,32,256]{2,1,0:T(8,128)S(1)}, u32[]{:S(2)}, u32[]{:S(2)}) collective-permute-start(f32[2,32,256]{2,1,0:T(8,128)S(1)} %stack.1.refs_4_), channel_id=1, source_target_pairs={{0,3},{1,2},{2,1},{3,0},{4,7},{5,6},{6,5},{7,4},{8,11},{9,10},{10,... | collective-permute-start | bytes 196616 | tf_op jit(solution)/shard_map/ppermute | solution.py:45
  14.2 11.3 %collective-permute-start.7 = (f32[2,32,256]{2,1,0:T(8,128)S(1)}, f32[2,32,256]{2,1,0:T(8,128)S(1)}, u32[]{:S(2)}, u32[]{:S(2)}) collective-permute-start(f32[2,32,256]{2,1,0:T(8,128)S(1)} %stack.1.refs_4_), channel_id=1, source_target_pairs={{0,2},{1,3},{2,0},{3,1},{4,6},{5,7},{6,4},{7,5},{8,10},{9,11},{10,... | collective-permute-start | bytes 196616 | tf_op jit(solution)/shard_map/ppermute | solution.py:45
  19.1 6.3 %collective-permute-start.6 = (f32[2,32,256]{2,1,0:T(8,128)S(1)}, f32[2,32,256]{2,1,0:T(8,128)S(1)}, u32[]{:S(2)}, u32[]{:S(2)}) collective-permute-start(f32[2,32,256]{2,1,0:T(8,128)S(1)} %stack.1.refs_4_), channel_id=1, source_target_pairs={{0,1},{1,0},{2,3},{3,2},{4,5},{5,4},{6,7},{7,6},{8,9},{9,8},{10,11... | collective-permute-start | bytes 196616 | tf_op jit(solution)/shard_map/ppermute | solution.py:45
  23.2 3.9 %collective-permute-start.5 = (bf16[32,1024]{1,0:T(8,128)(2,1)S(1)}, bf16[32,1024]{1,0:T(8,128)(2,1)S(1)}, u32[]{:S(2)}, u32[]{:S(2)}) collective-permute-start(bf16[32,1024]{1,0:T(8,128)(2,1)S(1)} %forward.11.refs_0_), channel_id=1, source_target_pairs={{0,3},{1,2},{2,1},{3,0},{4,7},{5,6},{6,5},{7,4},{8,11},{9,10},{10,... | collective-permute-start | bytes 196616 | tf_op jit(solution)/shard_map/ppermute | solution.py:45
  24.7 4.5 %collective-permute-start.4 = (bf16[32,1024]{1,0:T(8,128)(2,1)S(1)}, bf16[32,1024]{1,0:T(8,128)(2,1)S(1)}, u32[]{:S(2)}, u32[]{:S(2)}) collective-permute-start(bf16[32,1024]{1,0:T(8,128)(2,1)S(1)} %forward.11.refs_0_), channel_id=1, source_target_pairs={{0,2},{1,3},{2,0},{3,1},{4,6},{5,7},{6,4},{7,5},{8,10},{9,11},{10,... | collective-permute-start | bytes 196616 | tf_op jit(solution)/shard_map/ppermute | solution.py:45
  25.4 3.8 %collective-permute-start.3 = (bf16[32,1024]{1,0:T(8,128)(2,1)S(1)}, bf16[32,1024]{1,0:T(8,128)(2,1)S(1)}, u32[]{:S(2)}, u32[]{:S(2)}) collective-permute-start(bf16[32,1024]{1,0:T(8,128)(2,1)S(1)} %forward.11.refs_0_), channel_id=1, source_target_pairs={{0,1},{1,0},{2,3},{3,2},{4,5},{5,4},{6,7},{7,6},{8,9},{9,8},{10,11... | collective-permute-start | bytes 196616 | tf_op jit(solution)/shard_map/ppermute | solution.py:45
  31.0 13.4 %copy-start = (f32[32,2048]{1,0:T(8,128)S(1)}, f32[32,2048]{1,0:T(8,128)}, u32[]{:S(2)}) copy-start(f32[32,2048]{1,0:T(8,128)} %x.1) | copy-start | bytes 786436
  31.0 13.4 %copy-start.1 = (f32[32,2048]{1,0:T(8,128)S(1)}, f32[32,2048]{1,0:T(8,128)}, u32[]{:S(2)}) copy-start(f32[32,2048]{1,0:T(8,128)} %objective.3) | copy-start | bytes 786436
  31.0 13.4 %copy-start.2 = (f32[2048]{0:T(1024)S(1)}, f32[2048]{0:T(1024)}, u32[]{:S(2)}) copy-start(f32[2048]{0:T(1024)} %param.21) | copy-start | bytes 24580
  31.0 13.4 %copy-start.3 = (f32[2048]{0:T(1024)S(1)}, f32[2048]{0:T(1024)}, u32[]{:S(2)}) copy-start(f32[2048]{0:T(1024)} %param.22) | copy-start | bytes 24580
  31.0 13.4 %copy-start.4 = (s32[2048]{0:T(1024)S(1)}, s32[2048]{0:T(1024)}, u32[]{:S(2)}) copy-start(s32[2048]{0:T(1024)} %param.23) | copy-start | bytes 24580
  31.0 13.3 %collective-permute-start.10 = (bf16[32,2048]{1,0:T(8,128)(2,1)S(1)}, bf16[32,2048]{1,0:T(8,128)(2,1)S(1)}, u32[]{:S(2)}, u32[]{:S(2)}) collective-permute-start(bf16[32,2048]{1,0:T(8,128)(2,1)S(1)} %backward.6), channel_id=1, source_target_pairs={{0,8},{4,12},{8,0},{12,4},{1,9},{5,13},{9,1},{13,5},{2,10},{6,14},... | collective-permute-start | bytes 393224 | tf_op jit(solution)/shard_map/ppermute | solution.py:45
  34.8 9.6 %collective-permute-start.11 = (bf16[32,2048]{1,0:T(8,128)(2,1)S(1)}, bf16[32,2048]{1,0:T(8,128)(2,1)S(1)}, u32[]{:S(2)}, u32[]{:S(2)}) collective-permute-start(bf16[32,2048]{1,0:T(8,128)(2,1)S(1)} %backward.7), channel_id=1, source_target_pairs={{0,4},{4,0},{8,12},{12,8},{1,5},{5,1},{9,13},{13,9},{2,6},{6,2},{1... | collective-permute-start | bytes 393224 | tf_op jit(solution)/shard_map/ppermute | solution.py:45
  34.8 9.6 %collective-permute-start.9 = (bf16[32,2048]{1,0:T(8,128)(2,1)S(1)}, bf16[32,2048]{1,0:T(8,128)(2,1)S(1)}, u32[]{:S(2)}, u32[]{:S(2)}) collective-permute-start(bf16[32,2048]{1,0:T(8,128)(2,1)S(1)} %get-tuple-element.32), channel_id=1, source_target_pairs={{0,12},{4,8},{8,4},{12,0},{1,13},{5,9},{9,5},{13,1},{2,14},{6,10},... | collective-permute-start | bytes 393224 | tf_op jit(solution)/shard_map/ppermute | solution.py:45
  44.7 8.0 %collective-permute-start.14 = (bf16[32,2176]{1,0:T(8,128)(2,1)S(1)}, bf16[32,2176]{1,0:T(8,128)(2,1)S(1)}, u32[]{:S(2)}, u32[]{:S(2)}) collective-permute-start(bf16[32,2176]{1,0:T(8,128)(2,1)S(1)} %get-tuple-element.33.x.refs_1_), channel_id=1, source_target_pairs={{0,4},{4,0},{8,12},{12,8},{1,5},{5,1},{9,13},{13,9},{2,6},{6,2},{1... | collective-permute-start | bytes 417800 | tf_op jit(solution)/shard_map/ppermute | solution.py:45
  45.4 8.7 %collective-permute-start.13 = (bf16[32,2176]{1,0:T(8,128)(2,1)S(1)}, bf16[32,2176]{1,0:T(8,128)(2,1)S(1)}, u32[]{:S(2)}, u32[]{:S(2)}) collective-permute-start(bf16[32,2176]{1,0:T(8,128)(2,1)S(1)} %get-tuple-element.33.x.refs_1_), channel_id=1, source_target_pairs={{0,12},{4,8},{8,4},{12,0},{1,13},{5,9},{9,5},{13,1},{2,14},{6,10},... | collective-permute-start | bytes 417800 | tf_op jit(solution)/shard_map/ppermute | solution.py:45
  47.2 13.4 %collective-permute-start.12 = (bf16[32,2176]{1,0:T(8,128)(2,1)S(1)}, bf16[32,2176]{1,0:T(8,128)(2,1)S(1)}, u32[]{:S(2)}, u32[]{:S(2)}) collective-permute-start(bf16[32,2176]{1,0:T(8,128)(2,1)S(1)} %get-tuple-element.33.x.refs_1_), channel_id=1, source_target_pairs={{0,8},{4,12},{8,0},{12,4},{1,9},{5,13},{9,1},{13,5},{2,10},{6,14},... | collective-permute-start | bytes 417800 | tf_op jit(solution)/shard_map/ppermute | solution.py:45
  61.8 4.4 %collective-permute-start.17 = (bf16[32,1152]{1,0:T(8,128)(2,1)S(1)}, bf16[32,1152]{1,0:T(8,128)(2,1)S(1)}, u32[]{:S(2)}, u32[]{:S(2)}) collective-permute-start(bf16[32,1152]{1,0:T(8,128)(2,1)S(1)} %forward.15.refs_0_), channel_id=1, source_target_pairs={{0,3},{1,2},{2,1},{3,0},{4,7},{5,6},{6,5},{7,4},{8,11},{9,10},{10,... | collective-permute-start | bytes 221192 | tf_op jit(solution)/shard_map/ppermute | solution.py:45
  61.9 5.2 %collective-permute-start.16 = (bf16[32,1152]{1,0:T(8,128)(2,1)S(1)}, bf16[32,1152]{1,0:T(8,128)(2,1)S(1)}, u32[]{:S(2)}, u32[]{:S(2)}) collective-permute-start(bf16[32,1152]{1,0:T(8,128)(2,1)S(1)} %forward.15.refs_0_), channel_id=1, source_target_pairs={{0,2},{1,3},{2,0},{3,1},{4,6},{5,7},{6,4},{7,5},{8,10},{9,11},{10,... | collective-permute-start | bytes 221192 | tf_op jit(solution)/shard_map/ppermute | solution.py:45
  62.9 4.2 %collective-permute-start.15 = (bf16[32,1152]{1,0:T(8,128)(2,1)S(1)}, bf16[32,1152]{1,0:T(8,128)(2,1)S(1)}, u32[]{:S(2)}, u32[]{:S(2)}) collective-permute-start(bf16[32,1152]{1,0:T(8,128)(2,1)S(1)} %forward.15.refs_0_), channel_id=1, source_target_pairs={{0,1},{1,0},{2,3},{3,2},{4,5},{5,4},{6,7},{7,6},{8,9},{9,8},{10,11... | collective-permute-start | bytes 221192 | tf_op jit(solution)/shard_map/ppermute | solution.py:45
  69.1 10.1 %collective-permute-start.19 = (bf16[32,2048]{1,0:T(8,128)(2,1)S(1)}, bf16[32,2048]{1,0:T(8,128)(2,1)S(1)}, u32[]{:S(2)}, u32[]{:S(2)}) collective-permute-start(bf16[32,2048]{1,0:T(8,128)(2,1)S(1)} %backward.9), channel_id=1, source_target_pairs={{0,8},{4,12},{8,0},{12,4},{1,9},{5,13},{9,1},{13,5},{2,10},{6,14},... | collective-permute-start | bytes 393224 | tf_op jit(solution)/shard_map/ppermute | solution.py:45
  70.4 6.1 %collective-permute-start.20 = (bf16[32,2048]{1,0:T(8,128)(2,1)S(1)}, bf16[32,2048]{1,0:T(8,128)(2,1)S(1)}, u32[]{:S(2)}, u32[]{:S(2)}) collective-permute-start(bf16[32,2048]{1,0:T(8,128)(2,1)S(1)} %backward.10), channel_id=1, source_target_pairs={{0,4},{4,0},{8,12},{12,8},{1,5},{5,1},{9,13},{13,9},{2,6},{6,2},{1... | collective-permute-start | bytes 393224 | tf_op jit(solution)/shard_map/ppermute | solution.py:45
  72.0 9.3 %collective-permute-start.18 = (bf16[32,2048]{1,0:T(8,128)(2,1)S(1)}, bf16[32,2048]{1,0:T(8,128)(2,1)S(1)}, u32[]{:S(2)}, u32[]{:S(2)}) collective-permute-start(bf16[32,2048]{1,0:T(8,128)(2,1)S(1)} %get-tuple-element.41), channel_id=1, source_target_pairs={{0,12},{4,8},{8,4},{12,0},{1,13},{5,9},{9,5},{13,1},{2,14},{6,10},... | collective-permute-start | bytes 393224 | tf_op jit(solution)/shard_map/ppermute | solution.py:45
  81.6 5.7 %collective-permute-start.23 = (f32[32,128]{1,0:T(8,128)S(1)}, f32[32,128]{1,0:T(8,128)S(1)}, u32[]{:S(2)}, u32[]{:S(2)}) collective-permute-start(f32[32,128]{1,0:T(8,128)S(1)} %get-tuple-element.44.refs_0_), channel_id=1, source_target_pairs={{0,12},{4,8},{8,4},{12,0},{1,13},{5,9},{9,5},{13,1},{2,14},{6,10},... | collective-permute-start | bytes 49160 | tf_op jit(solution)/shard_map/ppermute | solution.py:45
  84.0 4.7 %collective-permute-start.22 = (f32[32,128]{1,0:T(8,128)S(1)}, f32[32,128]{1,0:T(8,128)S(1)}, u32[]{:S(2)}, u32[]{:S(2)}) collective-permute-start(f32[32,128]{1,0:T(8,128)S(1)} %get-tuple-element.44.refs_0_), channel_id=1, source_target_pairs={{0,8},{4,12},{8,0},{12,4},{1,9},{5,13},{9,1},{13,5},{2,10},{6,14},... | collective-permute-start | bytes 49160 | tf_op jit(solution)/shard_map/ppermute | solution.py:45
  86.3 3.7 %collective-permute-start.21 = (f32[32,128]{1,0:T(8,128)S(1)}, f32[32,128]{1,0:T(8,128)S(1)}, u32[]{:S(2)}, u32[]{:S(2)}) collective-permute-start(f32[32,128]{1,0:T(8,128)S(1)} %get-tuple-element.44.refs_0_), channel_id=1, source_target_pairs={{0,4},{4,0},{8,12},{12,8},{1,5},{5,1},{9,13},{13,9},{2,6},{6,2},{1... | collective-permute-start | bytes 49160 | tf_op jit(solution)/shard_map/ppermute | solution.py:45
  90.1 3.2 %collective-permute-start.26 = (f32[32,128]{1,0:T(8,128)S(1)}, f32[32,128]{1,0:T(8,128)S(1)}, u32[]{:S(2)}, u32[]{:S(2)}) collective-permute-start(f32[32,128]{1,0:T(8,128)S(1)} %moves.1.refs_0_), channel_id=1, source_target_pairs={{0,3},{1,2},{2,1},{3,0},{4,7},{5,6},{6,5},{7,4},{8,11},{9,10},{10,... | collective-permute-start | bytes 49160 | tf_op jit(solution)/shard_map/ppermute | solution.py:45
  90.2 3.8 %collective-permute-start.25 = (f32[32,128]{1,0:T(8,128)S(1)}, f32[32,128]{1,0:T(8,128)S(1)}, u32[]{:S(2)}, u32[]{:S(2)}) collective-permute-start(f32[32,128]{1,0:T(8,128)S(1)} %moves.1.refs_0_), channel_id=1, source_target_pairs={{0,2},{1,3},{2,0},{3,1},{4,6},{5,7},{6,4},{7,5},{8,10},{9,11},{10,... | collective-permute-start | bytes 49160 | tf_op jit(solution)/shard_map/ppermute | solution.py:45
  90.9 3.1 %collective-permute-start.24 = (f32[32,128]{1,0:T(8,128)S(1)}, f32[32,128]{1,0:T(8,128)S(1)}, u32[]{:S(2)}, u32[]{:S(2)}) collective-permute-start(f32[32,128]{1,0:T(8,128)S(1)} %moves.1.refs_0_), channel_id=1, source_target_pairs={{0,1},{1,0},{2,3},{3,2},{4,5},{5,4},{6,7},{7,6},{8,9},{9,8},{10,11... | collective-permute-start | bytes 49160 | tf_op jit(solution)/shard_map/ppermute | solution.py:45
  (6 other events, 44.2 us)

commit v3 on v2

--- a/solution.py
+++ b/solution.py
@@ -11,6 +11,7 @@
 EPSILON = 1e-06
 COPIES = 4
 GROUP = 8
+PIECES = 2
 
 SMEM = pl.BlockSpec(memory_space=pltpu.SMEM)
 VMEM = pl.BlockSpec(memory_space=pltpu.VMEM)
@@ -45,12 +46,12 @@
     return lax.ppermute(array, axis, [(i, i ^ k) for i in range(lax.axis_size(axis))])
 
 
-def partners(n):
-    return list(range(n - 1, 0, -1))
-
-
-def everyone(array, axis):
-    got = {k: swap(array, axis, k) for k in partners(lax.axis_size(axis))}
+def partners(n, first=(2, 1, 3)):
+    return [i for i in (*first, *range(4, n)) if i < n]
+
+
+def everyone(array, axis, first=(2, 1, 3)):
+    got = {k: swap(array, axis, k) for k in partners(lax.axis_size(axis), first)}
     return [array] + [got[k] for k in sorted(got)]
 
 
@@ -91,8 +92,10 @@
     return [pick(3 * i) + (pick(3 * i + 1) + pick(3 * i + 2)) for i in range(n)]
 
 
-def densify_kernel(slots, places, rt, rows, cols, count, tiles, out, head, nxt, multi, stage, sem):
-    live = jnp.minimum(count[0], slots)
+def densify_kernel(
+    slots, places, rt, count, rows_in, cols_in, tiles, out, *scratch
+):
+    rows, cols, head, nxt, multi, stage, sem = scratch
     step = slots // COPIES
     zero = jnp.zeros(out.shape[1:], bf16)
 
@@ -102,13 +105,21 @@
 
     for i in range(COPIES):
         copy(i).start()
+    pairs = [(rows_in, rows), (cols_in, cols)]
+    small = [pltpu.make_async_copy(*pair, sem.at[COPIES + i]) for i, pair in enumerate(pairs)]
+    for one in small:
+        one.start()
 
     @pl.loop(0, places, unroll=16)
     def _(p):
         head[p] = -1
 
+    for one in small:
+        one.wait()
+    live = jnp.minimum(count[0, 0], slots)
+
     def link(s, found):
-        p = cols[s] * rt + rows[s]
+        p = cols[0, 0, s] * rt + rows[0, 0, s]
         before = head[p]
         nxt[s] = before
         head[p] = s
@@ -140,7 +151,7 @@
         out[p] = zero
 
     def place(s):
-        out[cols[s] * rt + rows[s]] = stage[s]
+        out[cols[0, 0, s] * rt + rows[0, 0, s]] = stage[s]
 
     for i in range(COPIES):
         copy(i).wait()
@@ -181,18 +192,21 @@
 def densify(tiles, rows, cols, count, rt, ct):
     slots, height, width = tiles.shape
     places = rt * ct
+    hbm = [pltpu.with_memory_space_constraint(a, pltpu.HBM) for a in (rows, cols, tiles)]
     return call(
         functools.partial(densify_kernel, slots, places, rt),
         "densify",
         shape((places, height, width), bf16),
-        [rows, cols, count, pltpu.with_memory_space_constraint(tiles, pltpu.HBM)],
-        [SMEM, SMEM, SMEM, ANY],
+        [pltpu.with_memory_space_constraint(count, pltpu.SMEM), *hbm],
+        [SMEM] + [ANY] * 3,
         [
+            pltpu.SMEM(rows.shape, jnp.int32),
+            pltpu.SMEM(cols.shape, jnp.int32),
             pltpu.SMEM((places,), jnp.int32),
             pltpu.SMEM((slots,), jnp.int32),
             pltpu.SMEM((slots + 1,), jnp.int32),
             pltpu.VMEM(tiles.shape, bf16),
-            pltpu.SemaphoreType.DMA((COPIES,)),
+            pltpu.SemaphoreType.DMA((COPIES + 2,)),
         ],
         limit=16 << 20,
         cost=pl.CostEstimate(flops=0, bytes_accessed=32 << 20, transcendentals=0),
@@ -211,13 +225,13 @@
     return [(j, min(2, per - j)) for j in range(0, per, 2)]
 
 
-def forward(k, x, chunk, rt, per):
+def forward(k, x, chunk, start, rt, per):
     width = k.shape[2]
     total = None
-    for j, n in spans(per):
+    for j, n in spans(x.shape[1] // width):
         part = lax.dot_general(
             x[:, j * width : (j + n) * width],
-            columns(k, chunk * (per * rt), rt, j, n),
+            columns(k, chunk * (per * rt), rt, start + j, n),
             (((1,), (1,)), ((), ())),
             preferred_element_type=f32,
         )
@@ -225,50 +239,81 @@
     return total
 
 
-def backward(k, d, chunk, rt, per, store):
+def backward(k, d, chunk, start, rt, per, out):
     width = k.shape[2]
-    for j, n in spans(per):
-        block = columns(k, chunk * (per * rt), rt, j, n)
-        store(j * width, (j + n) * width, jnp.dot(d, block, preferred_element_type=f32))
-
-
-def stack_kernel(y, rhs, both):
-    both[0] = y[...]
-    both[1] = rhs[...]
-
-
-def cost(k, per, rt):
-    chunk = per * rt * k.shape[1] * k.shape[2]
-    return pl.CostEstimate(flops=64 * chunk, bytes_accessed=2 * chunk, transcendentals=0)
-
-
-def forward_kernel(rt, per, i, has_base, n_move, k, x, *refs):
-    total = forward(k, x, lax.axis_index("row") ^ i, rt, per)
+    for j in range(out.shape[1] // width):
+        block = columns(k, chunk * (per * rt), rt, start + j, 1)
+        part = jnp.dot(d, block, preferred_element_type=f32)
+        out[:, j * width : (j + 1) * width] = part.astype(out.dtype)
+
+
+def cost(k, tile_cols, rt):
+    size = tile_cols * rt * k.shape[1] * k.shape[2]
+    return pl.CostEstimate(flops=64 * size, bytes_accessed=2 * size, transcendentals=0)
+
+
+def start_kernel(x, y, rhs, low, both, held, sem):
+    pairs = [(x, held), (y, both.at[0]), (rhs, both.at[1])]
+    copies = [pltpu.make_async_copy(*pair, sem.at[i]) for i, pair in enumerate(pairs)]
+    for copy in copies:
+        copy.start()
+    for copy in copies:
+        copy.wait()
+    low[...] = held[...].astype(bf16)
+
+
+def start(x, y, rhs):
+    hbm = [pltpu.with_memory_space_constraint(a, pltpu.HBM) for a in (x, y, rhs)]
+    return call(
+        start_kernel,
+        "start",
+        [shape(x.shape, bf16), shape((2,) + y.shape, f32)],
+        hbm,
+        [ANY] * 3,
+        [pltpu.VMEM(x.shape, f32), pltpu.SemaphoreType.DMA((3,))],
+    )
+
+
+def add_kernel(total, part, out):
+    out[...] = total[...] + part[...].astype(f32)
+
+
+def add(total, part):
+    size = total.size
+    cost = pl.CostEstimate(flops=size, bytes_accessed=10 * size, transcendentals=0)
+    return call(add_kernel, "add", shape(total.shape, f32), [total, part], cost=cost)
+
+
+def forward_kernel(rt, per, i, start, n, has_base, n_move, k, x, *refs):
+    total = forward(k, x.at[:, : n * k.shape[2]], lax.axis_index("row") ^ i, start, rt, per)
     if has_base:
         total = total + refs[0][...]
     out, rows = refs[-1], total.shape[1]
     out[:, :rows] = total.astype(out.dtype)
     if n_move:
-        shard = per * k.shape[2]
-        moves = [unpack_columns(ref[:, shard:], 2) for ref in refs[has_base : has_base + n_move]]
+        extra = n * k.shape[2]
+        moves = [unpack_columns(ref[:, extra:], 2) for ref in refs[has_base : has_base + n_move]]
         moves = [tree_sum([m[j] for m in moves]) for j in range(2)]
         out[:, rows:] = pack_columns(moves, out.shape[1] - rows)
 
 
-def forward_parts(k, xs, rt, per, order, packed):
-    scen, rows = xs[0].shape[0], rt * k.shape[1]
+def forward_parts(k, pieces, rt, per, packed):
+    scen, rows = pieces[0][0].shape[0], rt * k.shape[1]
+    n_row, n = len(pieces[0]), per // len(pieces)
+    order = [(0, p) for p in range(len(pieces))]
+    order += [(i, p) for p in range(len(pieces)) for i in range(1, n_row)]
     base = []
-    for i in order:
-        last = i == order[-1]
-        moves = xs if last and packed else []
+    for i, p in order:
+        last = (i, p) == order[-1]
+        moves = pieces[-1] if last and packed else []
         extra = k.shape[2] if moves else 0
         base = [
             call(
-                functools.partial(forward_kernel, rt, per, i, len(base), len(moves)),
+                functools.partial(forward_kernel, rt, per, i, p * n, n, len(base), len(moves)),
                 "forward",
                 shape((scen, rows + extra), bf16 if last else f32),
-                [k, xs[i], *base, *moves],
-                cost=cost(k, per, rt),
+                [k, pieces[p][i], *base, *moves],
+                cost=cost(k, n, rt),
             )
         ]
     return base[0]
@@ -295,56 +340,57 @@
         old = refs[0][c] if has_y else both[c][0]
         new = jnp.maximum(old + sigma * (both[c][1] - total), 0.0)
         if c == 0:
-            move_out[...] = jnp.sum((new - old) ** 2, axis=1, keepdims=True)
+            move_out[:, 0:1] = jnp.zeros((old.shape[0], 1), f32)
+            move_out[:, 1:2] = jnp.sum((new - old) ** 2, axis=1, keepdims=True)
         if len(y_out.shape) == 3:
             y_out[c] = new
         elif c == 0:
             y_out[...] = new
         bar_out[:, here] = (2.0 * new - old).astype(bf16)
 
-    def store(low, high, value):
-        send_out[:, low:high] = value.astype(send_out.dtype)
-
-    backward(k, bar_out[...], row ^ first, rt, per, store)
-
-
-def backward_kernel(rt, per, i, k, d, out):
-    def store(low, high, value):
-        out[:, low:high] = value.astype(out.dtype)
-
-    backward(k, d[...], lax.axis_index("row") ^ i, rt, per, store)
-
-
-def backward_part(k, d, i, dtype, rt, per):
+    backward(k, bar_out[...], row ^ first, 0, rt, per, send_out)
+
+
+def backward_kernel(rt, per, i, start, k, d, out):
+    backward(k, d[...], lax.axis_index("row") ^ i, start, rt, per, out)
+
+
+def backward_part(k, d, i, start, n, dtype, rt, per):
     return call(
-        functools.partial(backward_kernel, rt, per, i),
+        functools.partial(backward_kernel, rt, per, i, start),
         "backward",
-        shape((d.shape[0], per * k.shape[2]), dtype),
+        shape((d.shape[0], n * k.shape[2]), dtype),
         [k, d],
-        cost=cost(k, per, rt),
+        cost=cost(k, n, rt),
     )
 
 
-def primal_kernel(n_part, step, weight, x, objective, low, high, kind, dual_move, *refs):
-    parts, outs = refs[:n_part], refs[n_part:]
-    total = parts[0][...].astype(f32)
-    for part in parts[1:]:
-        total = total + part[...].astype(f32)
+def primal_kernel(n_part, n_x, start, mode, step, weight, objective, low, high, kind, moved, *refs):
+    parts, xs, outs = refs[:n_part], refs[n_part : n_part + n_x], refs[n_part + n_x :]
+    total = tree_sum([part[...].astype(f32) for part in parts])
+    width = total.shape[1]
+    here = slice(start, start + width)
     tau = to_column(step[...]) / to_column(weight[...])
-    old = x[...]
-    new = old - tau * (objective[...] - total)
-    new = jnp.where(kind[...] >= 1, jnp.maximum(new, low[...]), new)
-    new = jnp.where(kind[...] == 2, jnp.minimum(new, high[...]), new)
+    old = jnp.concatenate([x[...] for x in xs], axis=1) if n_x > 1 else xs[0][...]
+    if old.shape[1] > width:
+        old = old[:, here]
+    new = old - tau * (objective[:, here] - total)
+    bound = kind[:, here]
+    new = jnp.where(bound >= 1, jnp.maximum(new, low[:, here]), new)
+    new = jnp.where(bound == 2, jnp.minimum(new, high[:, here]), new)
     outs[0][...] = new
-    primal_move = jnp.sum((new - old) ** 2, axis=1, keepdims=True)
-    width = new.shape[1]
-    if outs[1].dtype == bf16:
-        outs[1][:, :width] = new.astype(bf16)
-        moves = [primal_move, dual_move[...]]
-        outs[1][:, width:] = pack_columns(moves, outs[1].shape[1] - width)
+    primal_move = jnp.sum((new - old) ** 2, axis=1, keepdims=True) + moved[:, 0:1]
+    dual_move = moved[:, 1:2]
+    if mode == "last":
+        outs[1][0:1] = to_line(primal_move)
+        outs[1][1:2] = to_line(dual_move)
+        return
+    outs[1][:, :width] = new.astype(bf16)
+    if mode == "packed":
+        outs[1][:, width:] = pack_columns([primal_move, dual_move], outs[1].shape[1] - width)
     else:
-        lane = lax.broadcasted_iota(jnp.int32, outs[1].shape, 1)
-        outs[1][...] = jnp.where(lane == 0, primal_move, dual_move[...])
+        outs[2][:, 0:1] = primal_move
+        outs[2][:, 1:2] = dual_move
 
 
 def sum_kernel(*refs):
@@ -353,8 +399,7 @@
 
 def weight_kernel(weight, *refs):
     total = tree_sum([ref[...] for ref in refs[:-1]])
-    w = new_weight(to_column(weight[...]), total[:, 0:1], total[:, 1:2])
-    refs[-1][...] = to_line(w)
+    refs[-1][...] = new_weight(weight[...], total[0:1], total[1:2])
 
 
 def body(
@@ -379,59 +424,77 @@
     per = shard // width
     rt = dual_vars.shape[1] * n_col // width
     ct = per * n_row
-    order = [0, 1] + partners(n_row)[:-1]
-
-    xs = everyone(primal_vars.astype(bf16), "row")
-    k = densify(
-        tiles, tile_rows.reshape(-1), tile_cols.reshape(-1), tile_count.reshape(-1), rt, ct
-    )
-    y, rhs, k = lax.optimization_barrier((dual_vars, right_side, k))
-    both = call(stack_kernel, "stack", shape((2,) + y.shape, f32), [y, rhs])
-    both = everyone(both, "col")
+    n_piece = PIECES if per % PIECES == 0 else 1
+
+    low, both = start(primal_vars, dual_vars, right_side)
+    chunks = [everyone(low, "row")]
+    both = everyone(both, "col", (1, 3, 2))
+    k = densify(tiles, tile_rows, tile_cols, tile_count, rt, ct)
+    k, both = lax.optimization_barrier((k, both))
     step = step_size[None]
     weight = primal_weight[None]
     low_bound, high_bound, kind = lower_bound[None], upper_bound[None], bound_kind[None]
-    x, y, packed = primal_vars, [], False
+    xs, y, packed = [primal_vars], [], False
     for sweep in range(ITERS):
         last = sweep == ITERS - 1
-        part = forward_parts(k, xs, rt, per, order, packed)
+        pieces = 1 if last else n_piece
+        n = per // pieces
+        part = forward_parts(k, chunks, rt, per, packed)
         first, *others = partners(n_row)
-        y, bar, dual_move, sent, weight = call(
+        y, bar, moved, sent, weight = call(
             functools.partial(dual_kernel, rt, per, n_col, packed, len(y), first),
             "dual",
             [
                 shape(dual_vars.shape if last else (n_col,) + dual_vars.shape, f32),
                 shape((scen, rt * width), bf16),
-                shape((scen, 1), f32),
-                shape((scen, shard), bf16),
+                shape((scen, 2), f32),
+                shape((scen, n * width), bf16),
                 shape((1, scen), f32),
             ],
-            [k, step, weight, *everyone(part, "col"), *both, *y],
-            cost=cost(k, per, rt),
+            [k, step, weight, *everyone(part, "col", (1, 3, 2)), *both, *y],
+            cost=cost(k, n, rt),
         )
-        totals = [swap(sent, "row", first)]
-        for i in others:
-            sent = backward_part(k, bar, i, bf16, rt, per)
-            totals.append(swap(sent, "row", i))
-            sent, bar = lax.optimization_barrier((sent, bar))
-        totals.insert(0, backward_part(k, bar, 0, f32, rt, per))
-        x, low = call(
-            functools.partial(primal_kernel, len(totals)),
-            "primal",
-            [
-                shape(x.shape, f32),
-                shape((scen, width), f32) if last else shape((scen, shard + width), bf16),
-            ],
-            [step, weight, x, objective, low_bound, high_bound, kind, dual_move, *totals],
-        )
-        y, packed = [y], True
-        if not last:
-            xs = everyone(low, "row")
-    move = call(sum_kernel, "moves", shape(low.shape, f32), everyone(low, "row"))
+        totals = []
+        for p in range(pieces):
+            got = {}
+            for i in partners(n_row):
+                if p or i != first:
+                    sent = backward_part(k, bar, i, p * n, n, bf16, rt, per)
+                got[i] = swap(sent, "row", i)
+                sent, bar = lax.optimization_barrier((sent, bar))
+            totals.append(list(got.values()))
+        for p in range(pieces):
+            total = backward_part(k, bar, 0, p * n, n, f32, rt, per)
+            for part in totals[p][:-1]:
+                total = add(total, part)
+            totals[p] = [total, totals[p][-1]]
+        new, chunks = [], []
+        for p in range(pieces):
+            mode = "last" if last else "packed" if p == pieces - 1 else "plain"
+            extra = width if mode == "packed" else 0
+            outs = [shape((scen, n * width), f32)]
+            if last:
+                outs.append(shape((2, scen), f32))
+            else:
+                outs.append(shape((scen, n * width + extra), bf16))
+            if mode == "plain":
+                outs.append(shape((scen, 2), f32))
+            x, low, *more = call(
+                functools.partial(primal_kernel, len(totals[p]), len(xs), p * n * width, mode),
+                "primal",
+                outs,
+                [step, weight, objective, low_bound, high_bound, kind, moved, *totals[p], *xs],
+            )
+            moved = more[0] if more else moved
+            new.append(x)
+            if not last:
+                chunks.append(everyone(low, "row"))
+        xs, y, packed = new, [y], True
+    move = call(sum_kernel, "moves", shape(low.shape, f32), everyone(low, "row", (1, 2, 3)))
     weight = call(
-        weight_kernel, "weight", shape((1, scen), f32), [weight, *everyone(move, "col")]
+        weight_kernel, "weight", shape((1, scen), f32), [weight, *everyone(move, "col", (1, 2, 3))]
     )
-    return x, y[0], weight.reshape(-1)
+    return xs[0], y[0], weight.reshape(-1)
 
 
 def solution(mesh):

time: 94.7 us -> 91.1 us (0.962)
  waiting for transfers between devices: 33.2 us -> 21.8 us
  starting transfers between devices: 33.3 us -> 42.8 us
  local copies, waits for them, and re-layouts: 3.25 us -> 1.9 us
  other arithmetic: 0.98 us -> 0 us
    ppermute x27 -> x33, waiting for transfers between devices: 33.2 us -> 21.8 us  [swap(): lax.ppermute(array, axis, [(i, i ^ k) for i in range(lax.axis_size(axis))])]
    ppermute x27 -> x33, starting transfers between devices: 33.3 us -> 42.8 us  [swap(): lax.ppermute(array, axis, [(i, i ^ k) for i in range(lax.axis_size(axis))])]
    unnamed x25 -> x17, local copies, waits for them, and re-layouts: 3.25 us -> 1.9 us
    convert_element_type x1 -> x0, other arithmetic: 0.98 us -> none  [body(): xs = everyone(primal_vars.astype(bf16), 'row')]
    pallas_call x22 -> x37, Pallas kernels: 22.4 us -> 23.1 us  [call(): pl.pallas_call(kernel, out_shape=out_shape, in_specs=specs, out_specs=out...]
  transfers between devices with their start and end apart: 27 -> 33, of which waited for: 15 -> 12; matrix products, arithmetic and copies ran while one was open for 1% -> 1% of each run, Pallas kernels for 17% -> 20%
where the time goes in v3:
time: 91.1 us; the launch traced here: 91.2 us
  starting transfers between devices  42.8 us (47%)
  Pallas kernels  23.1 us (25%)
  waiting for transfers between devices  21.8 us (24%)
  local copies, waits for them, and re-layouts  1.9 us (2%)
  between operations  1.69 us (2%)
    ppermute x33, starting transfers between devices, swap(): lax.ppermute(array, axis, [(i, i ^ k) for i in range(lax.axis_size(axis))])  42.8 us
    pallas_call x37, Pallas kernels, call(): pl.pallas_call(kernel, out_shape=out_shape, in_specs=specs, out_specs=out...  23.1 us
    ppermute x33, waiting for transfers between devices, swap(): lax.ppermute(array, axis, [(i, i ^ k) for i in range(lax.axis_size(axis))])  21.8 us
    unnamed x17, local copies, waits for them, and re-layouts  1.9 us
  transfers between devices with their start and end apart: 33, of which 12 were waited for; matrix products, arithmetic and copies ran while one was open for 1% of the time, Pallas kernels for 20%

profile of v3, /device:TPU:0, one launch (start us, length us, event | category | flops | bytes accessed | tf_op | source)
XLA Modules:
  0.0 91.2 jit_solution(4748269763127886538)
XLA Ops:
  2.2 2.6 %collective-permute-start.5 = (bf16[32,2048]{1,0:T(8,128)(2,1)S(1)}, bf16[32,2048]{1,0:T(8,128)(2,1)S(1)}, u32[]{:S(2)}, u32[]{:S(2)}) collective-permute-start(bf16[32,2048]{1,0:T(8,128)(2,1)S(1)} %get-tuple-element.38.x), channel_id=1, source_target_pairs={{0,4},{4,0},{8,12},{12,8},{1,5},{5,1},{9,13},{13,9},{2,6},{6,2},{1... | collective-permute-start | bytes 393224 | tf_op jit(solution)/shard_map/ppermute | solution.py:46
  4.8 2.6 %collective-permute-start.4 = (bf16[32,2048]{1,0:T(8,128)(2,1)S(1)}, bf16[32,2048]{1,0:T(8,128)(2,1)S(1)}, u32[]{:S(2)}, u32[]{:S(2)}) collective-permute-start(bf16[32,2048]{1,0:T(8,128)(2,1)S(1)} %get-tuple-element.38.x), channel_id=1, source_target_pairs={{0,8},{4,12},{8,0},{12,4},{1,9},{5,13},{9,1},{13,5},{2,10},{6,14},... | collective-permute-start | bytes 393224 | tf_op jit(solution)/shard_map/ppermute | solution.py:46
  7.4 1.7 %collective-permute-start.1 = (f32[2,32,256]{2,1,0:T(8,128)S(1)}, f32[2,32,256]{2,1,0:T(8,128)S(1)}, u32[]{:S(2)}, u32[]{:S(2)}) collective-permute-start(f32[2,32,256]{2,1,0:T(8,128)S(1)} %get-tuple-element.39.refs_4_), channel_id=1, source_target_pairs={{0,2},{1,3},{2,0},{3,1},{4,6},{5,7},{6,4},{7,5},{8,10},{9,11},{10,... | collective-permute-start | bytes 196616 | tf_op jit(solution)/shard_map/ppermute | solution.py:46
  9.8 3.6 %densify.1.k = bf16[512,128,128]{2,1,0:T(8,128)(2,1)S(1)} custom-call(s32[1,1]{1,0:T(1,128)S(6)} %copy.19.count, s32[1,1,256]{2,1,0:T(1,128)} %rows_in.1, s32[1,1,256]{2,1,0:T(1,128)} %cols_in.1, bf16[256,128,128]{2,1,0:T(8,128)(2,1)} %bitcast.23), custom_call_target="tpu_custom_call" | custom-call | bytes 33554432 | tf_op jit(solution)/shard_map/densify/pallas_call | solution.py:33
  13.4 1.3 %forward.12.refs_0_ = f32[32,1024]{1,0:T(8,128)S(1)} custom-call(bf16[512,128,128]{2,1,0:T(8,128)(2,1)S(1)} %densify.1.k, bf16[32,2048]{1,0:T(8,128)(2,1)S(1)} %get-tuple-element.38.x), custom_call_target="tpu_custom_call" | custom-call | flops 134217728 | bytes 4194304 | tf_op jit(solution)/shard_map/forward/pallas_call | solution.py:33
  14.8 1.3 %forward.13.refs_0_ = f32[32,1024]{1,0:T(8,128)S(1)} custom-call(bf16[512,128,128]{2,1,0:T(8,128)(2,1)S(1)} %densify.1.k, bf16[32,2048]{1,0:T(8,128)(2,1)S(1)} %collective-permute-done.5.x, f32[32,1024]{1,0:T(8,128)S(1)} %forward.12.refs_0_), custom_call_target="tpu_custom_call" | custom-call | flops 134217728 | bytes 4194304 | tf_op jit(solution)/shard_map/forward/pallas_call | solution.py:33
  16.1 1.6 %collective-permute-done.4.x = bf16[32,2048]{1,0:T(8,128)(2,1)S(1)} collective-permute-done((bf16[32,2048]{1,0:T(8,128)(2,1)S(1)}, bf16[32,2048]{1,0:T(8,128)(2,1)S(1)}, u32[]{:S(2)}, u32[]{:S(2)}) %collective-permute-start.4) | collective-permute-done | bytes 131104 | tf_op jit(solution)/shard_map/ppermute | solution.py:46
  17.7 1.3 %forward.14.refs_0_ = f32[32,1024]{1,0:T(8,128)S(1)} custom-call(bf16[512,128,128]{2,1,0:T(8,128)(2,1)S(1)} %densify.1.k, bf16[32,2048]{1,0:T(8,128)(2,1)S(1)} %collective-permute-done.4.x, f32[32,1024]{1,0:T(8,128)S(1)} %forward.13.refs_0_), custom_call_target="tpu_custom_call" | custom-call | flops 134217728 | bytes 4194304 | tf_op jit(solution)/shard_map/forward/pallas_call | solution.py:33
  19.0 1.3 %forward.15.refs_0_ = bf16[32,1024]{1,0:T(8,128)(2,1)S(1)} custom-call(bf16[512,128,128]{2,1,0:T(8,128)(2,1)S(1)} %densify.1.k, bf16[32,2048]{1,0:T(8,128)(2,1)S(1)} %collective-permute-done.3.x, f32[32,1024]{1,0:T(8,128)S(1)} %forward.14.refs_0_), custom_call_target="tpu_custom_call" | custom-call | flops 134217728 | bytes 4194304 | tf_op jit(solution)/shard_map/forward/pallas_call | solution.py:33
  20.4 1.7 %collective-permute-start.6 = (bf16[32,1024]{1,0:T(8,128)(2,1)S(1)}, bf16[32,1024]{1,0:T(8,128)(2,1)S(1)}, u32[]{:S(2)}, u32[]{:S(2)}) collective-permute-start(bf16[32,1024]{1,0:T(8,128)(2,1)S(1)} %forward.15.refs_0_), channel_id=1, source_target_pairs={{0,1},{1,0},{2,3},{3,2},{4,5},{5,4},{6,7},{7,6},{8,9},{9,8},{10,11... | collective-permute-start | bytes 196616 | tf_op jit(solution)/shard_map/ppermute | solution.py:46
  22.0 1.4 %collective-permute-start.8 = (bf16[32,1024]{1,0:T(8,128)(2,1)S(1)}, bf16[32,1024]{1,0:T(8,128)(2,1)S(1)}, u32[]{:S(2)}, u32[]{:S(2)}) collective-permute-start(bf16[32,1024]{1,0:T(8,128)(2,1)S(1)} %forward.15.refs_0_), channel_id=1, source_target_pairs={{0,3},{1,2},{2,1},{3,0},{4,7},{5,6},{6,5},{7,4},{8,11},{9,10},{10,... | collective-permute-start | bytes 196616 | tf_op jit(solution)/shard_map/ppermute | solution.py:46
  23.5 3.3 %collective-permute-done.7.refs_2_ = bf16[32,1024]{1,0:T(8,128)(2,1)S(1)} collective-permute-done((bf16[32,1024]{1,0:T(8,128)(2,1)S(1)}, bf16[32,1024]{1,0:T(8,128)(2,1)S(1)}, u32[]{:S(2)}, u32[]{:S(2)}) %collective-permute-start.7) | collective-permute-done | bytes 65568 | tf_op jit(solution)/shard_map/ppermute | solution.py:46
  27.4 2.2 %collective-permute-start.9 = (bf16[32,1024]{1,0:T(8,128)(2,1)S(1)}, bf16[32,1024]{1,0:T(8,128)(2,1)S(1)}, u32[]{:S(2)}, u32[]{:S(2)}) collective-permute-start(bf16[32,1024]{1,0:T(8,128)(2,1)S(1)} %get-tuple-element.45), channel_id=1, source_target_pairs={{0,8},{4,12},{8,0},{12,4},{1,9},{5,13},{9,1},{13,5},{2,10},{6,14},... | collective-permute-start | bytes 196616 | tf_op jit(solution)/shard_map/ppermute | solution.py:46
  30.0 3.4 %collective-permute-start.10 = (bf16[32,1024]{1,0:T(8,128)(2,1)S(1)}, bf16[32,1024]{1,0:T(8,128)(2,1)S(1)}, u32[]{:S(2)}, u32[]{:S(2)}) collective-permute-start(bf16[32,1024]{1,0:T(8,128)(2,1)S(1)} %backward.10), channel_id=1, source_target_pairs={{0,4},{4,0},{8,12},{12,8},{1,5},{5,1},{9,13},{13,9},{2,6},{6,2},{1... | collective-permute-start | bytes 196616 | tf_op jit(solution)/shard_map/ppermute | solution.py:46
  34.3 1.5 %collective-permute-start.12 = (bf16[32,1024]{1,0:T(8,128)(2,1)S(1)}, bf16[32,1024]{1,0:T(8,128)(2,1)S(1)}, u32[]{:S(2)}, u32[]{:S(2)}) collective-permute-start(bf16[32,1024]{1,0:T(8,128)(2,1)S(1)} %backward.12), channel_id=1, source_target_pairs={{0,8},{4,12},{8,0},{12,4},{1,9},{5,13},{9,1},{13,5},{2,10},{6,14},... | collective-permute-start | bytes 196616 | tf_op jit(solution)/shard_map/ppermute | solution.py:46
  36.3 3.0 %collective-permute-start.13 = (bf16[32,1024]{1,0:T(8,128)(2,1)S(1)}, bf16[32,1024]{1,0:T(8,128)(2,1)S(1)}, u32[]{:S(2)}, u32[]{:S(2)}) collective-permute-start(bf16[32,1024]{1,0:T(8,128)(2,1)S(1)} %backward.13), channel_id=1, source_target_pairs={{0,4},{4,0},{8,12},{12,8},{1,5},{5,1},{9,13},{13,9},{2,6},{6,2},{1... | collective-permute-start | bytes 196616 | tf_op jit(solution)/shard_map/ppermute | solution.py:46
  41.1 3.8 %collective-permute-start.19 = (bf16[32,1024]{1,0:T(8,128)(2,1)S(1)}, bf16[32,1024]{1,0:T(8,128)(2,1)S(1)}, u32[]{:S(2)}, u32[]{:S(2)}) collective-permute-start(bf16[32,1024]{1,0:T(8,128)(2,1)S(1)} %get-tuple-element.55.x), channel_id=1, source_target_pairs={{0,8},{4,12},{8,0},{12,4},{1,9},{5,13},{9,1},{13,5},{2,10},{6,14},... | collective-permute-start | bytes 196616 | tf_op jit(solution)/shard_map/ppermute | solution.py:46
  47.2 2.5 %collective-permute-start.16 = (bf16[32,1152]{1,0:T(8,128)(2,1)S(1)}, bf16[32,1152]{1,0:T(8,128)(2,1)S(1)}, u32[]{:S(2)}, u32[]{:S(2)}) collective-permute-start(bf16[32,1152]{1,0:T(8,128)(2,1)S(1)} %get-tuple-element.54.x.refs_1_), channel_id=1, source_target_pairs={{0,8},{4,12},{8,0},{12,4},{1,9},{5,13},{9,1},{13,5},{2,10},{6,14},... | collective-permute-start | bytes 221192 | tf_op jit(solution)/shard_map/ppermute | solution.py:46
  55.0 1.4 %collective-permute-done.16.x.refs_3_ = bf16[32,1152]{1,0:T(8,128)(2,1)S(1)} collective-permute-done((bf16[32,1152]{1,0:T(8,128)(2,1)S(1)}, bf16[32,1152]{1,0:T(8,128)(2,1)S(1)}, u32[]{:S(2)}, u32[]{:S(2)}) %collective-permute-start.16) | collective-permute-done | bytes 73760 | tf_op jit(solution)/shard_map/ppermute | solution.py:46
  58.6 1.2 %collective-permute-start.23 = (bf16[32,1152]{1,0:T(8,128)(2,1)S(1)}, bf16[32,1152]{1,0:T(8,128)(2,1)S(1)}, u32[]{:S(2)}, u32[]{:S(2)}) collective-permute-start(bf16[32,1152]{1,0:T(8,128)(2,1)S(1)} %forward.23.refs_0_), channel_id=1, source_target_pairs={{0,3},{1,2},{2,1},{3,0},{4,7},{5,6},{6,5},{7,4},{8,11},{9,10},{10,... | collective-permute-start | bytes 221192 | tf_op jit(solution)/shard_map/ppermute | solution.py:46
  59.8 3.3 %collective-permute-done.22.refs_2_ = bf16[32,1152]{1,0:T(8,128)(2,1)S(1)} collective-permute-done((bf16[32,1152]{1,0:T(8,128)(2,1)S(1)}, bf16[32,1152]{1,0:T(8,128)(2,1)S(1)}, u32[]{:S(2)}, u32[]{:S(2)}) %collective-permute-start.22) | collective-permute-done | bytes 73760 | tf_op jit(solution)/shard_map/ppermute | solution.py:46
  63.8 1.0 %dual.3 = (f32[32,256]{1,0:T(8,128)S(1)}, bf16[32,1024]{1,0:T(8,128)(2,1)S(1)}, f32[32,2]{1,0:T(8,128)S(1)}, bf16[32,2048]{1,0:T(8,128)(2,1)S(1)}, f32[1,32]{1,0:T(1,128)S(1)}) custom-call(bf16[512,128,128]{2,1,0:T(8,128)(2,1)S(1)} %densify.1.k, f32[1,32]{1,0:T(1,128)S(1)} %bitcast.20, f32[1,32]{1,0:T(1,128)S(1)} %get-tuple-element.43.weight, ...), custom_call_target="tpu_custom_call" | custom-call | flops 134217728 | bytes 4194304 | tf_op jit(solution)/shard_map/dual/pallas_call | solution.py:33
  64.8 1.3 %collective-permute-start.24 = (bf16[32,2048]{1,0:T(8,128)(2,1)S(1)}, bf16[32,2048]{1,0:T(8,128)(2,1)S(1)}, u32[]{:S(2)}, u32[]{:S(2)}) collective-permute-start(bf16[32,2048]{1,0:T(8,128)(2,1)S(1)} %get-tuple-element.59), channel_id=1, source_target_pairs={{0,8},{4,12},{8,0},{12,4},{1,9},{5,13},{9,1},{13,5},{2,10},{6,14},... | collective-permute-start | bytes 393224 | tf_op jit(solution)/shard_map/ppermute | solution.py:46
  66.9 1.4 %collective-permute-start.25 = (bf16[32,2048]{1,0:T(8,128)(2,1)S(1)}, bf16[32,2048]{1,0:T(8,128)(2,1)S(1)}, u32[]{:S(2)}, u32[]{:S(2)}) collective-permute-start(bf16[32,2048]{1,0:T(8,128)(2,1)S(1)} %backward.17), channel_id=1, source_target_pairs={{0,4},{4,0},{8,12},{12,8},{1,5},{5,1},{9,13},{13,9},{2,6},{6,2},{1... | collective-permute-start | bytes 393224 | tf_op jit(solution)/shard_map/ppermute | solution.py:46
  69.0 1.8 %collective-permute-start.26 = (bf16[32,2048]{1,0:T(8,128)(2,1)S(1)}, bf16[32,2048]{1,0:T(8,128)(2,1)S(1)}, u32[]{:S(2)}, u32[]{:S(2)}) collective-permute-start(bf16[32,2048]{1,0:T(8,128)(2,1)S(1)} %backward.18), channel_id=1, source_target_pairs={{0,12},{4,8},{8,4},{12,0},{1,13},{5,9},{9,5},{13,1},{2,14},{6,10},... | collective-permute-start | bytes 393224 | tf_op jit(solution)/shard_map/ppermute | solution.py:46
  71.5 3.7 %collective-permute-done.24.part = bf16[32,2048]{1,0:T(8,128)(2,1)S(1)} collective-permute-done((bf16[32,2048]{1,0:T(8,128)(2,1)S(1)}, bf16[32,2048]{1,0:T(8,128)(2,1)S(1)}, u32[]{:S(2)}, u32[]{:S(2)}) %collective-permute-start.24) | collective-permute-done | bytes 131104 | tf_op jit(solution)/shard_map/ppermute | solution.py:46
  75.2 2.6 %collective-permute-done.25.part = bf16[32,2048]{1,0:T(8,128)(2,1)S(1)} collective-permute-done((bf16[32,2048]{1,0:T(8,128)(2,1)S(1)}, bf16[32,2048]{1,0:T(8,128)(2,1)S(1)}, u32[]{:S(2)}, u32[]{:S(2)}) %collective-permute-start.25) | collective-permute-done | bytes 131104 | tf_op jit(solution)/shard_map/ppermute | solution.py:46
  78.2 2.7 %collective-permute-start.27 = (f32[2,32]{1,0:T(2,128)S(1)}, f32[2,32]{1,0:T(2,128)S(1)}, u32[]{:S(2)}, u32[]{:S(2)}) collective-permute-start(f32[2,32]{1,0:T(2,128)S(1)} %get-tuple-element.68.refs_0_), channel_id=1, source_target_pairs={{0,4},{4,0},{8,12},{12,8},{1,5},{5,1},{9,13},{13,9},{2,6},{6,2},{1... | collective-permute-start | bytes 776 | tf_op jit(solution)/shard_map/ppermute | solution.py:46
  81.6 1.8 %collective-permute-start.29 = (f32[2,32]{1,0:T(2,128)S(1)}, f32[2,32]{1,0:T(2,128)S(1)}, u32[]{:S(2)}, u32[]{:S(2)}) collective-permute-start(f32[2,32]{1,0:T(2,128)S(1)} %get-tuple-element.68.refs_0_), channel_id=1, source_target_pairs={{0,12},{4,8},{8,4},{12,0},{1,13},{5,9},{9,5},{13,1},{2,14},{6,10},... | collective-permute-start | bytes 776 | tf_op jit(solution)/shard_map/ppermute | solution.py:46
  83.4 2.0 %collective-permute-done.28.refs_2_ = f32[2,32]{1,0:T(2,128)S(1)} collective-permute-done((f32[2,32]{1,0:T(2,128)S(1)}, f32[2,32]{1,0:T(2,128)S(1)}, u32[]{:S(2)}, u32[]{:S(2)}) %collective-permute-start.28) | collective-permute-done | bytes 288 | tf_op jit(solution)/shard_map/ppermute | solution.py:46
  85.4 1.6 %collective-permute-done.29.refs_3_ = f32[2,32]{1,0:T(2,128)S(1)} collective-permute-done((f32[2,32]{1,0:T(2,128)S(1)}, f32[2,32]{1,0:T(2,128)S(1)}, u32[]{:S(2)}, u32[]{:S(2)}) %collective-permute-start.29) | collective-permute-done | bytes 288 | tf_op jit(solution)/shard_map/ppermute | solution.py:46
  87.6 1.2 %collective-permute-start.32 = (f32[2,32]{1,0:T(2,128)S(1)}, f32[2,32]{1,0:T(2,128)S(1)}, u32[]{:S(2)}, u32[]{:S(2)}) collective-permute-start(f32[2,32]{1,0:T(2,128)S(1)} %moves.1.refs_0_), channel_id=1, source_target_pairs={{0,3},{1,2},{2,1},{3,0},{4,7},{5,6},{6,5},{7,4},{8,11},{9,10},{10,... | collective-permute-start | bytes 776 | tf_op jit(solution)/shard_map/ppermute | solution.py:46
  (88 shorter events, 22.1 us)
Async XLA Ops:
  1.6 7.5 %collective-permute-start = (f32[2,32,256]{2,1,0:T(8,128)S(1)}, f32[2,32,256]{2,1,0:T(8,128)S(1)}, u32[]{:S(2)}, u32[]{:S(2)}) collective-permute-start(f32[2,32,256]{2,1,0:T(8,128)S(1)} %get-tuple-element.39.refs_4_), channel_id=1, source_target_pairs={{0,1},{1,0},{2,3},{3,2},{4,5},{5,4},{6,7},{7,6},{8,9},{9,8},{10,11... | collective-permute-start | bytes 196616 | tf_op jit(solution)/shard_map/ppermute | solution.py:46
  2.2 12.6 %collective-permute-start.5 = (bf16[32,2048]{1,0:T(8,128)(2,1)S(1)}, bf16[32,2048]{1,0:T(8,128)(2,1)S(1)}, u32[]{:S(2)}, u32[]{:S(2)}) collective-permute-start(bf16[32,2048]{1,0:T(8,128)(2,1)S(1)} %get-tuple-element.38.x), channel_id=1, source_target_pairs={{0,4},{4,0},{8,12},{12,8},{1,5},{5,1},{9,13},{13,9},{2,6},{6,2},{1... | collective-permute-start | bytes 393224 | tf_op jit(solution)/shard_map/ppermute | solution.py:46
  4.8 12.9 %collective-permute-start.4 = (bf16[32,2048]{1,0:T(8,128)(2,1)S(1)}, bf16[32,2048]{1,0:T(8,128)(2,1)S(1)}, u32[]{:S(2)}, u32[]{:S(2)}) collective-permute-start(bf16[32,2048]{1,0:T(8,128)(2,1)S(1)} %get-tuple-element.38.x), channel_id=1, source_target_pairs={{0,8},{4,12},{8,0},{12,4},{1,9},{5,13},{9,1},{13,5},{2,10},{6,14},... | collective-permute-start | bytes 393224 | tf_op jit(solution)/shard_map/ppermute | solution.py:46
  7.4 11.6 %collective-permute-start.3 = (bf16[32,2048]{1,0:T(8,128)(2,1)S(1)}, bf16[32,2048]{1,0:T(8,128)(2,1)S(1)}, u32[]{:S(2)}, u32[]{:S(2)}) collective-permute-start(bf16[32,2048]{1,0:T(8,128)(2,1)S(1)} %get-tuple-element.38.x), channel_id=1, source_target_pairs={{0,12},{4,8},{8,4},{12,0},{1,13},{5,9},{9,5},{13,1},{2,14},{6,10},... | collective-permute-start | bytes 393224 | tf_op jit(solution)/shard_map/ppermute | solution.py:46
  7.4 6.0 %collective-permute-start.1 = (f32[2,32,256]{2,1,0:T(8,128)S(1)}, f32[2,32,256]{2,1,0:T(8,128)S(1)}, u32[]{:S(2)}, u32[]{:S(2)}) collective-permute-start(f32[2,32,256]{2,1,0:T(8,128)S(1)} %get-tuple-element.39.refs_4_), channel_id=1, source_target_pairs={{0,2},{1,3},{2,0},{3,1},{4,6},{5,7},{6,4},{7,5},{8,10},{9,11},{10,... | collective-permute-start | bytes 196616 | tf_op jit(solution)/shard_map/ppermute | solution.py:46
  9.1 4.3 %collective-permute-start.2 = (f32[2,32,256]{2,1,0:T(8,128)S(1)}, f32[2,32,256]{2,1,0:T(8,128)S(1)}, u32[]{:S(2)}, u32[]{:S(2)}) collective-permute-start(f32[2,32,256]{2,1,0:T(8,128)S(1)} %get-tuple-element.39.refs_4_), channel_id=1, source_target_pairs={{0,3},{1,2},{2,1},{3,0},{4,7},{5,6},{6,5},{7,4},{8,11},{9,10},{10,... | collective-permute-start | bytes 196616 | tf_op jit(solution)/shard_map/ppermute | solution.py:46
  20.4 3.1 %collective-permute-start.6 = (bf16[32,1024]{1,0:T(8,128)(2,1)S(1)}, bf16[32,1024]{1,0:T(8,128)(2,1)S(1)}, u32[]{:S(2)}, u32[]{:S(2)}) collective-permute-start(bf16[32,1024]{1,0:T(8,128)(2,1)S(1)} %forward.15.refs_0_), channel_id=1, source_target_pairs={{0,1},{1,0},{2,3},{3,2},{4,5},{5,4},{6,7},{7,6},{8,9},{9,8},{10,11... | collective-permute-start | bytes 196616 | tf_op jit(solution)/shard_map/ppermute | solution.py:46
  22.0 4.8 %collective-permute-start.7 = (bf16[32,1024]{1,0:T(8,128)(2,1)S(1)}, bf16[32,1024]{1,0:T(8,128)(2,1)S(1)}, u32[]{:S(2)}, u32[]{:S(2)}) collective-permute-start(bf16[32,1024]{1,0:T(8,128)(2,1)S(1)} %forward.15.refs_0_), channel_id=1, source_target_pairs={{0,2},{1,3},{2,0},{3,1},{4,6},{5,7},{6,4},{7,5},{8,10},{9,11},{10,... | collective-permute-start | bytes 196616 | tf_op jit(solution)/shard_map/ppermute | solution.py:46
  22.0 4.8 %collective-permute-start.8 = (bf16[32,1024]{1,0:T(8,128)(2,1)S(1)}, bf16[32,1024]{1,0:T(8,128)(2,1)S(1)}, u32[]{:S(2)}, u32[]{:S(2)}) collective-permute-start(bf16[32,1024]{1,0:T(8,128)(2,1)S(1)} %forward.15.refs_0_), channel_id=1, source_target_pairs={{0,3},{1,2},{2,1},{3,0},{4,7},{5,6},{6,5},{7,4},{8,11},{9,10},{10,... | collective-permute-start | bytes 196616 | tf_op jit(solution)/shard_map/ppermute | solution.py:46
  27.4 12.3 %collective-permute-start.9 = (bf16[32,1024]{1,0:T(8,128)(2,1)S(1)}, bf16[32,1024]{1,0:T(8,128)(2,1)S(1)}, u32[]{:S(2)}, u32[]{:S(2)}) collective-permute-start(bf16[32,1024]{1,0:T(8,128)(2,1)S(1)} %get-tuple-element.45), channel_id=1, source_target_pairs={{0,8},{4,12},{8,0},{12,4},{1,9},{5,13},{9,1},{13,5},{2,10},{6,14},... | collective-permute-start | bytes 196616 | tf_op jit(solution)/shard_map/ppermute | solution.py:46
  30.0 10.2 %collective-permute-start.10 = (bf16[32,1024]{1,0:T(8,128)(2,1)S(1)}, bf16[32,1024]{1,0:T(8,128)(2,1)S(1)}, u32[]{:S(2)}, u32[]{:S(2)}) collective-permute-start(bf16[32,1024]{1,0:T(8,128)(2,1)S(1)} %backward.10), channel_id=1, source_target_pairs={{0,4},{4,0},{8,12},{12,8},{1,5},{5,1},{9,13},{13,9},{2,6},{6,2},{1... | collective-permute-start | bytes 196616 | tf_op jit(solution)/shard_map/ppermute | solution.py:46
  33.8 6.9 %collective-permute-start.11 = (bf16[32,1024]{1,0:T(8,128)(2,1)S(1)}, bf16[32,1024]{1,0:T(8,128)(2,1)S(1)}, u32[]{:S(2)}, u32[]{:S(2)}) collective-permute-start(bf16[32,1024]{1,0:T(8,128)(2,1)S(1)} %backward.11), channel_id=1, source_target_pairs={{0,12},{4,8},{8,4},{12,0},{1,13},{5,9},{9,5},{13,1},{2,14},{6,10},... | collective-permute-start | bytes 196616 | tf_op jit(solution)/shard_map/ppermute | solution.py:46
  34.3 11.0 %collective-permute-start.12 = (bf16[32,1024]{1,0:T(8,128)(2,1)S(1)}, bf16[32,1024]{1,0:T(8,128)(2,1)S(1)}, u32[]{:S(2)}, u32[]{:S(2)}) collective-permute-start(bf16[32,1024]{1,0:T(8,128)(2,1)S(1)} %backward.12), channel_id=1, source_target_pairs={{0,8},{4,12},{8,0},{12,4},{1,9},{5,13},{9,1},{13,5},{2,10},{6,14},... | collective-permute-start | bytes 196616 | tf_op jit(solution)/shard_map/ppermute | solution.py:46
  36.3 9.1 %collective-permute-start.13 = (bf16[32,1024]{1,0:T(8,128)(2,1)S(1)}, bf16[32,1024]{1,0:T(8,128)(2,1)S(1)}, u32[]{:S(2)}, u32[]{:S(2)}) collective-permute-start(bf16[32,1024]{1,0:T(8,128)(2,1)S(1)} %backward.13), channel_id=1, source_target_pairs={{0,4},{4,0},{8,12},{12,8},{1,5},{5,1},{9,13},{13,9},{2,6},{6,2},{1... | collective-permute-start | bytes 196616 | tf_op jit(solution)/shard_map/ppermute | solution.py:46
  39.6 6.2 %collective-permute-start.14 = (bf16[32,1024]{1,0:T(8,128)(2,1)S(1)}, bf16[32,1024]{1,0:T(8,128)(2,1)S(1)}, u32[]{:S(2)}, u32[]{:S(2)}) collective-permute-start(bf16[32,1024]{1,0:T(8,128)(2,1)S(1)} %backward.14), channel_id=1, source_target_pairs={{0,12},{4,8},{8,4},{12,0},{1,13},{5,9},{9,5},{13,1},{2,14},{6,10},... | collective-permute-start | bytes 196616 | tf_op jit(solution)/shard_map/ppermute | solution.py:46
  40.9 8.8 %collective-permute-start.20 = (bf16[32,1024]{1,0:T(8,128)(2,1)S(1)}, bf16[32,1024]{1,0:T(8,128)(2,1)S(1)}, u32[]{:S(2)}, u32[]{:S(2)}) collective-permute-start(bf16[32,1024]{1,0:T(8,128)(2,1)S(1)} %get-tuple-element.55.x), channel_id=1, source_target_pairs={{0,4},{4,0},{8,12},{12,8},{1,5},{5,1},{9,13},{13,9},{2,6},{6,2},{1... | collective-permute-start | bytes 196616 | tf_op jit(solution)/shard_map/ppermute | solution.py:46
  41.1 11.8 %collective-permute-start.19 = (bf16[32,1024]{1,0:T(8,128)(2,1)S(1)}, bf16[32,1024]{1,0:T(8,128)(2,1)S(1)}, u32[]{:S(2)}, u32[]{:S(2)}) collective-permute-start(bf16[32,1024]{1,0:T(8,128)(2,1)S(1)} %get-tuple-element.55.x), channel_id=1, source_target_pairs={{0,8},{4,12},{8,0},{12,4},{1,9},{5,13},{9,1},{13,5},{2,10},{6,14},... | collective-permute-start | bytes 196616 | tf_op jit(solution)/shard_map/ppermute | solution.py:46
  46.2 8.1 %collective-permute-start.17 = (bf16[32,1152]{1,0:T(8,128)(2,1)S(1)}, bf16[32,1152]{1,0:T(8,128)(2,1)S(1)}, u32[]{:S(2)}, u32[]{:S(2)}) collective-permute-start(bf16[32,1152]{1,0:T(8,128)(2,1)S(1)} %get-tuple-element.54.x.refs_1_), channel_id=1, source_target_pairs={{0,4},{4,0},{8,12},{12,8},{1,5},{5,1},{9,13},{13,9},{2,6},{6,2},{1... | collective-permute-start | bytes 221192 | tf_op jit(solution)/shard_map/ppermute | solution.py:46
  46.8 6.8 %collective-permute-start.18 = (bf16[32,1024]{1,0:T(8,128)(2,1)S(1)}, bf16[32,1024]{1,0:T(8,128)(2,1)S(1)}, u32[]{:S(2)}, u32[]{:S(2)}) collective-permute-start(bf16[32,1024]{1,0:T(8,128)(2,1)S(1)} %get-tuple-element.55.x), channel_id=1, source_target_pairs={{0,12},{4,8},{8,4},{12,0},{1,13},{5,9},{9,5},{13,1},{2,14},{6,10},... | collective-permute-start | bytes 196616 | tf_op jit(solution)/shard_map/ppermute | solution.py:46
  47.2 9.2 %collective-permute-start.16 = (bf16[32,1152]{1,0:T(8,128)(2,1)S(1)}, bf16[32,1152]{1,0:T(8,128)(2,1)S(1)}, u32[]{:S(2)}, u32[]{:S(2)}) collective-permute-start(bf16[32,1152]{1,0:T(8,128)(2,1)S(1)} %get-tuple-element.54.x.refs_1_), channel_id=1, source_target_pairs={{0,8},{4,12},{8,0},{12,4},{1,9},{5,13},{9,1},{13,5},{2,10},{6,14},... | collective-permute-start | bytes 221192 | tf_op jit(solution)/shard_map/ppermute | solution.py:46
  49.8 7.4 %collective-permute-start.15 = (bf16[32,1152]{1,0:T(8,128)(2,1)S(1)}, bf16[32,1152]{1,0:T(8,128)(2,1)S(1)}, u32[]{:S(2)}, u32[]{:S(2)}) collective-permute-start(bf16[32,1152]{1,0:T(8,128)(2,1)S(1)} %get-tuple-element.54.x.refs_1_), channel_id=1, source_target_pairs={{0,12},{4,8},{8,4},{12,0},{1,13},{5,9},{9,5},{13,1},{2,14},{6,10},... | collective-permute-start | bytes 221192 | tf_op jit(solution)/shard_map/ppermute | solution.py:46
  58.0 5.1 %collective-permute-start.22 = (bf16[32,1152]{1,0:T(8,128)(2,1)S(1)}, bf16[32,1152]{1,0:T(8,128)(2,1)S(1)}, u32[]{:S(2)}, u32[]{:S(2)}) collective-permute-start(bf16[32,1152]{1,0:T(8,128)(2,1)S(1)} %forward.23.refs_0_), channel_id=1, source_target_pairs={{0,2},{1,3},{2,0},{3,1},{4,6},{5,7},{6,4},{7,5},{8,10},{9,11},{10,... | collective-permute-start | bytes 221192 | tf_op jit(solution)/shard_map/ppermute | solution.py:46
  58.6 5.2 %collective-permute-start.23 = (bf16[32,1152]{1,0:T(8,128)(2,1)S(1)}, bf16[32,1152]{1,0:T(8,128)(2,1)S(1)}, u32[]{:S(2)}, u32[]{:S(2)}) collective-permute-start(bf16[32,1152]{1,0:T(8,128)(2,1)S(1)} %forward.23.refs_0_), channel_id=1, source_target_pairs={{0,3},{1,2},{2,1},{3,0},{4,7},{5,6},{6,5},{7,4},{8,11},{9,10},{10,... | collective-permute-start | bytes 221192 | tf_op jit(solution)/shard_map/ppermute | solution.py:46
  64.8 10.3 %collective-permute-start.24 = (bf16[32,2048]{1,0:T(8,128)(2,1)S(1)}, bf16[32,2048]{1,0:T(8,128)(2,1)S(1)}, u32[]{:S(2)}, u32[]{:S(2)}) collective-permute-start(bf16[32,2048]{1,0:T(8,128)(2,1)S(1)} %get-tuple-element.59), channel_id=1, source_target_pairs={{0,8},{4,12},{8,0},{12,4},{1,9},{5,13},{9,1},{13,5},{2,10},{6,14},... | collective-permute-start | bytes 393224 | tf_op jit(solution)/shard_map/ppermute | solution.py:46
  66.9 10.9 %collective-permute-start.25 = (bf16[32,2048]{1,0:T(8,128)(2,1)S(1)}, bf16[32,2048]{1,0:T(8,128)(2,1)S(1)}, u32[]{:S(2)}, u32[]{:S(2)}) collective-permute-start(bf16[32,2048]{1,0:T(8,128)(2,1)S(1)} %backward.17), channel_id=1, source_target_pairs={{0,4},{4,0},{8,12},{12,8},{1,5},{5,1},{9,13},{13,9},{2,6},{6,2},{1... | collective-permute-start | bytes 393224 | tf_op jit(solution)/shard_map/ppermute | solution.py:46
  69.0 8.9 %collective-permute-start.26 = (bf16[32,2048]{1,0:T(8,128)(2,1)S(1)}, bf16[32,2048]{1,0:T(8,128)(2,1)S(1)}, u32[]{:S(2)}, u32[]{:S(2)}) collective-permute-start(bf16[32,2048]{1,0:T(8,128)(2,1)S(1)} %backward.18), channel_id=1, source_target_pairs={{0,12},{4,8},{8,4},{12,0},{1,13},{5,9},{9,5},{13,1},{2,14},{6,10},... | collective-permute-start | bytes 393224 | tf_op jit(solution)/shard_map/ppermute | solution.py:46
  78.2 5.2 %collective-permute-start.27 = (f32[2,32]{1,0:T(2,128)S(1)}, f32[2,32]{1,0:T(2,128)S(1)}, u32[]{:S(2)}, u32[]{:S(2)}) collective-permute-start(f32[2,32]{1,0:T(2,128)S(1)} %get-tuple-element.68.refs_0_), channel_id=1, source_target_pairs={{0,4},{4,0},{8,12},{12,8},{1,5},{5,1},{9,13},{13,9},{2,6},{6,2},{1... | collective-permute-start | bytes 776 | tf_op jit(solution)/shard_map/ppermute | solution.py:46
  81.0 4.5 %collective-permute-start.28 = (f32[2,32]{1,0:T(2,128)S(1)}, f32[2,32]{1,0:T(2,128)S(1)}, u32[]{:S(2)}, u32[]{:S(2)}) collective-permute-start(f32[2,32]{1,0:T(2,128)S(1)} %get-tuple-element.68.refs_0_), channel_id=1, source_target_pairs={{0,8},{4,12},{8,0},{12,4},{1,9},{5,13},{9,1},{13,5},{2,10},{6,14},... | collective-permute-start | bytes 776 | tf_op jit(solution)/shard_map/ppermute | solution.py:46
  81.6 5.4 %collective-permute-start.29 = (f32[2,32]{1,0:T(2,128)S(1)}, f32[2,32]{1,0:T(2,128)S(1)}, u32[]{:S(2)}, u32[]{:S(2)}) collective-permute-start(f32[2,32]{1,0:T(2,128)S(1)} %get-tuple-element.68.refs_0_), channel_id=1, source_target_pairs={{0,12},{4,8},{8,4},{12,0},{1,13},{5,9},{9,5},{13,1},{2,14},{6,10},... | collective-permute-start | bytes 776 | tf_op jit(solution)/shard_map/ppermute | solution.py:46
  87.0 3.2 %collective-permute-start.30 = (f32[2,32]{1,0:T(2,128)S(1)}, f32[2,32]{1,0:T(2,128)S(1)}, u32[]{:S(2)}, u32[]{:S(2)}) collective-permute-start(f32[2,32]{1,0:T(2,128)S(1)} %moves.1.refs_0_), channel_id=1, source_target_pairs={{0,1},{1,0},{2,3},{3,2},{4,5},{5,4},{6,7},{7,6},{8,9},{9,8},{10,11... | collective-permute-start | bytes 776 | tf_op jit(solution)/shard_map/ppermute | solution.py:46
  87.0 3.6 %collective-permute-start.31 = (f32[2,32]{1,0:T(2,128)S(1)}, f32[2,32]{1,0:T(2,128)S(1)}, u32[]{:S(2)}, u32[]{:S(2)}) collective-permute-start(f32[2,32]{1,0:T(2,128)S(1)} %moves.1.refs_0_), channel_id=1, source_target_pairs={{0,2},{1,3},{2,0},{3,1},{4,6},{5,7},{6,4},{7,5},{8,10},{9,11},{10,... | collective-permute-start | bytes 776 | tf_op jit(solution)/shard_map/ppermute | solution.py:46
  87.6 3.0 %collective-permute-start.32 = (f32[2,32]{1,0:T(2,128)S(1)}, f32[2,32]{1,0:T(2,128)S(1)}, u32[]{:S(2)}, u32[]{:S(2)}) collective-permute-start(f32[2,32]{1,0:T(2,128)S(1)} %moves.1.refs_0_), channel_id=1, source_target_pairs={{0,3},{1,2},{2,1},{3,0},{4,7},{5,6},{6,5},{7,4},{8,11},{9,10},{10,... | collective-permute-start | bytes 776 | tf_op jit(solution)/shard_map/ppermute | solution.py:46
  (8 other events, 45.7 us)

commit v4 on v3

--- a/solution.py
+++ b/solution.py
@@ -11,7 +11,6 @@
 EPSILON = 1e-06
 COPIES = 4
 GROUP = 8
-PIECES = 2
 
 SMEM = pl.BlockSpec(memory_space=pltpu.SMEM)
 VMEM = pl.BlockSpec(memory_space=pltpu.VMEM)
@@ -23,7 +22,7 @@
     return pltpu.VMEM(dims, dtype)
 
 
-def call(kernel, name, out_shape, args, specs=None, scratch=(), limit=8 << 20, cost=None):
+def call(kernel, name, out_shape, args, specs=None, scratch=(), limit=8 << 20, cost=None, aliases={}):
     specs = specs or [VMEM] * len(args)
     out_specs = jax.tree.map(lambda _: VMEM, out_shape, is_leaf=lambda o: hasattr(o, "shape"))
     args = [
@@ -38,6 +37,7 @@
         scratch_shapes=scratch,
         compiler_params=pltpu.CompilerParams(vmem_limit_bytes=limit),
         cost_estimate=cost,
+        input_output_aliases=aliases,
         name=name,
     )(*args)
 
@@ -93,7 +93,7 @@
 
 
 def densify_kernel(
-    slots, places, rt, count, rows_in, cols_in, tiles, out, *scratch
+    slots, places, rt, clean, count, rows_in, cols_in, tiles, _, out, *scratch
 ):
     rows, cols, head, nxt, multi, stage, sem = scratch
     step = slots // COPIES
@@ -126,19 +126,19 @@
         multi[found] = p
         return found + (before >= 0).astype(jnp.int32)
 
-    clear = max(1, places // slots)
+    clear = max(1, (places - clean) // slots)
 
     def link_group(g, found):
         for i in range(GROUP):
             found = link(g * GROUP + i, found)
         for i in range(GROUP * clear):
-            out[g * GROUP * clear + i] = zero
+            out[clean + g * GROUP * clear + i] = zero
         return found
 
     groups = live // GROUP
     found = lax.fori_loop(0, groups, link_group, jnp.int32(0))
     found = lax.fori_loop(groups * GROUP, live, link, found)
-    cleared = groups * (GROUP * clear)
+    cleared = clean + groups * (GROUP * clear)
     rest = (places - cleared) // GROUP
 
     @pl.loop(0, rest)
@@ -189,16 +189,16 @@
             out[p] = total.astype(bf16)
 
 
-def densify(tiles, rows, cols, count, rt, ct):
+def densify(tiles, rows, cols, count, k, clean, rt):
     slots, height, width = tiles.shape
-    places = rt * ct
+    places = k.shape[0]
     hbm = [pltpu.with_memory_space_constraint(a, pltpu.HBM) for a in (rows, cols, tiles)]
     return call(
-        functools.partial(densify_kernel, slots, places, rt),
+        functools.partial(densify_kernel, slots, places, rt, clean),
         "densify",
         shape((places, height, width), bf16),
-        [pltpu.with_memory_space_constraint(count, pltpu.SMEM), *hbm],
-        [SMEM] + [ANY] * 3,
+        [pltpu.with_memory_space_constraint(count, pltpu.SMEM), *hbm, k],
+        [SMEM] + [ANY] * 3 + [VMEM],
         [
             pltpu.SMEM(rows.shape, jnp.int32),
             pltpu.SMEM(cols.shape, jnp.int32),
@@ -209,6 +209,7 @@
             pltpu.SemaphoreType.DMA((COPIES + 2,)),
         ],
         limit=16 << 20,
+        aliases={4: 0},
         cost=pl.CostEstimate(flops=0, bytes_accessed=32 << 20, transcendentals=0),
     )
 
@@ -252,22 +253,28 @@
     return pl.CostEstimate(flops=64 * size, bytes_accessed=2 * size, transcendentals=0)
 
 
-def start_kernel(x, y, rhs, low, both, held, sem):
+def start_kernel(clear, x, y, rhs, low, both, k, held, sem):
     pairs = [(x, held), (y, both.at[0]), (rhs, both.at[1])]
     copies = [pltpu.make_async_copy(*pair, sem.at[i]) for i, pair in enumerate(pairs)]
     for copy in copies:
         copy.start()
+    zero = jnp.zeros(k.shape[1:], bf16)
+
+    @pl.loop(0, clear, unroll=8)
+    def _(p):
+        k[p] = zero
+
     for copy in copies:
         copy.wait()
     low[...] = held[...].astype(bf16)
 
 
-def start(x, y, rhs):
+def start(x, y, rhs, k_dims, clear):
     hbm = [pltpu.with_memory_space_constraint(a, pltpu.HBM) for a in (x, y, rhs)]
     return call(
-        start_kernel,
+        functools.partial(start_kernel, clear),
         "start",
-        [shape(x.shape, bf16), shape((2,) + y.shape, f32)],
+        [shape(x.shape, bf16), shape((2,) + y.shape, f32), shape(k_dims, bf16)],
         hbm,
         [ANY] * 3,
         [pltpu.VMEM(x.shape, f32), pltpu.SemaphoreType.DMA((3,))],
@@ -275,13 +282,13 @@
 
 
 def add_kernel(total, part, out):
-    out[...] = total[...] + part[...].astype(f32)
-
-
-def add(total, part):
+    out[...] = (total[...] + part[...].astype(f32)).astype(out.dtype)
+
+
+def add(total, part, dtype=f32):
     size = total.size
     cost = pl.CostEstimate(flops=size, bytes_accessed=10 * size, transcendentals=0)
-    return call(add_kernel, "add", shape(total.shape, f32), [total, part], cost=cost)
+    return call(add_kernel, "add", shape(total.shape, dtype), [total, part], cost=cost)
 
 
 def forward_kernel(rt, per, i, start, n, has_base, n_move, k, x, *refs):
@@ -297,14 +304,12 @@
         out[:, rows:] = pack_columns(moves, out.shape[1] - rows)
 
 
-def forward_parts(k, pieces, rt, per, packed):
+def forward_parts(k, pieces, rt, per, n, packed, order, base=()):
     scen, rows = pieces[0][0].shape[0], rt * k.shape[1]
-    n_row, n = len(pieces[0]), per // len(pieces)
-    order = [(0, p) for p in range(len(pieces))]
-    order += [(i, p) for p in range(len(pieces)) for i in range(1, n_row)]
-    base = []
+    n_row = len(pieces[0])
+    base = list(base)
     for i, p in order:
-        last = (i, p) == order[-1]
+        last = (i, p) == (n_row - 1, len(pieces) - 1)
         moves = pieces[-1] if last and packed else []
         extra = k.shape[2] if moves else 0
         base = [
@@ -323,7 +328,7 @@
     return jnp.sqrt(weight * jnp.sqrt(primal + EPSILON) / jnp.sqrt(dual + EPSILON))
 
 
-def dual_kernel(rt, per, n_col, packed, has_y, first, k, step, weight, *refs):
+def dual_kernel(rt, per, n_col, packed, has_y, first, start, k, step, weight, *refs):
     row, col = lax.axis_index("row"), lax.axis_index("col")
     parts, both, refs = refs[:n_col], refs[n_col : 2 * n_col], refs[2 * n_col :]
     y_out, bar_out, move_out, send_out, weight_out = refs[has_y:]
@@ -348,7 +353,7 @@
             y_out[...] = new
         bar_out[:, here] = (2.0 * new - old).astype(bf16)
 
-    backward(k, bar_out[...], row ^ first, 0, rt, per, send_out)
+    backward(k, bar_out[...], row ^ first, start, rt, per, send_out)
 
 
 def backward_kernel(rt, per, i, start, k, d, out):
@@ -365,9 +370,13 @@
     )
 
 
-def primal_kernel(n_part, n_x, start, mode, step, weight, objective, low, high, kind, moved, *refs):
-    parts, xs, outs = refs[:n_part], refs[n_part : n_part + n_x], refs[n_part + n_x :]
-    total = tree_sum([part[...].astype(f32) for part in parts])
+def primal_kernel(n_parts, n_x, start, mode, step, weight, objective, low, high, kind, moved, *refs):
+    refs = list(refs)
+    pieces = []
+    for n in n_parts:
+        pieces.append(tree_sum([refs.pop(0)[...].astype(f32) for _ in range(n)]))
+    total = jnp.concatenate(pieces, axis=1) if len(pieces) > 1 else pieces[0]
+    xs, outs = refs[:n_x], refs[n_x:]
     width = total.shape[1]
     here = slice(start, start + width)
     tau = to_column(step[...]) / to_column(weight[...])
@@ -423,26 +432,39 @@
     scen, shard = primal_vars.shape
     per = shard // width
     rt = dual_vars.shape[1] * n_col // width
-    ct = per * n_row
-    n_piece = PIECES if per % PIECES == 0 else 1
-
-    low, both = start(primal_vars, dual_vars, right_side)
+    line = n_row == 4 and per % 2 == 0
+    pieces = 2 if line else 1
+    n = per // pieces
+
+    def part_for(i, p, dtype=bf16):
+        return backward_part(k, bar, i, p * n, n, dtype, rt, per)
+
+    places = rt * per * n_row
+    clean = places // 4
+    dims = (places,) + tiles.shape[1:]
+    low, both, k = start(primal_vars, dual_vars, right_side, dims, clean)
     chunks = [everyone(low, "row")]
-    both = everyone(both, "col", (1, 3, 2))
-    k = densify(tiles, tile_rows, tile_cols, tile_count, rt, ct)
+    if n_col == 4:
+        both = [both, swap(both, "col", 1), swap(both, "col", 2)]
+    else:
+        both = everyone(both, "col")
+    k = densify(tiles, tile_rows, tile_cols, tile_count, k, clean, rt)
     k, both = lax.optimization_barrier((k, both))
+    if n_col == 4:
+        both.append(swap(both[2], "col", 1))
     step = step_size[None]
     weight = primal_weight[None]
     low_bound, high_bound, kind = lower_bound[None], upper_bound[None], bound_kind[None]
     xs, y, packed = [primal_vars], [], False
+    order, base = [(i, 0) for i in range(n_row)], []
     for sweep in range(ITERS):
         last = sweep == ITERS - 1
-        pieces = 1 if last else n_piece
-        n = per // pieces
-        part = forward_parts(k, chunks, rt, per, packed)
-        first, *others = partners(n_row)
+        part = forward_parts(k, chunks, rt, per, per // len(chunks), packed, order, base)
+        first = 3 if line else partners(n_row)[0]
         y, bar, moved, sent, weight = call(
-            functools.partial(dual_kernel, rt, per, n_col, packed, len(y), first),
+            functools.partial(
+                dual_kernel, rt, per, n_col, packed, len(y), first, (pieces - 1) * n
+            ),
             "dual",
             [
                 shape(dual_vars.shape if last else (n_col,) + dual_vars.shape, f32),
@@ -454,42 +476,52 @@
             [k, step, weight, *everyone(part, "col", (1, 3, 2)), *both, *y],
             cost=cost(k, n, rt),
         )
-        totals = []
-        for p in range(pieces):
-            got = {}
-            for i in partners(n_row):
-                if p or i != first:
-                    sent = backward_part(k, bar, i, p * n, n, bf16, rt, per)
-                got[i] = swap(sent, "row", i)
+        hop = swap(sent, "row", 1 if line else first)
+        got = [] if line else [hop]
+        for i in partners(n_row):
+            if line or i != first:
+                sent = part_for(i, 0)
+                got.append(swap(sent, "row", i))
                 sent, bar = lax.optimization_barrier((sent, bar))
-            totals.append(list(got.values()))
-        for p in range(pieces):
-            total = backward_part(k, bar, 0, p * n, n, f32, rt, per)
-            for part in totals[p][:-1]:
-                total = add(total, part)
-            totals[p] = [total, totals[p][-1]]
+        totals = [[part_for(0, 0, f32)]]
+        if line:
+            near = part_for(1, 1)
+            cross = part_for(2, 1, f32)
+            near = swap(near, "row", 1)
+            cross = swap(add(cross, hop, bf16), "row", 2)
+            totals.append([add(part_for(0, 1, f32), near), cross])
+        for piece in got[:-1]:
+            totals[0] = [add(totals[0][0], piece)]
+        totals[0].append(got[-1])
         new, chunks = [], []
-        for p in range(pieces):
+        for p, group in enumerate([totals] if last else [[piece] for piece in totals]):
+            cols = n * width * len(group)
             mode = "last" if last else "packed" if p == pieces - 1 else "plain"
             extra = width if mode == "packed" else 0
-            outs = [shape((scen, n * width), f32)]
-            if last:
-                outs.append(shape((2, scen), f32))
-            else:
-                outs.append(shape((scen, n * width + extra), bf16))
+            outs = [shape((scen, cols), f32)]
+            outs.append(shape((2, scen), f32) if last else shape((scen, cols + extra), bf16))
             if mode == "plain":
                 outs.append(shape((scen, 2), f32))
+            sizes = [len(piece) for piece in group]
             x, low, *more = call(
-                functools.partial(primal_kernel, len(totals[p]), len(xs), p * n * width, mode),
+                functools.partial(primal_kernel, sizes, len(xs), p * n * width, mode),
                 "primal",
                 outs,
-                [step, weight, objective, low_bound, high_bound, kind, moved, *totals[p], *xs],
+                [step, weight, objective, low_bound, high_bound, kind, moved, *sum(group, []), *xs],
             )
             moved = more[0] if more else moved
             new.append(x)
-            if not last:
+            if line and mode == "plain":
+                far, near = swap(low, "row", 2), swap(low, "row", 1)
+                chunks.append([low, near, far, swap(far, "row", 1)])
+                base = forward_parts(k, chunks, rt, per, n, False, [(0, 0)])
+                base, totals[1][0] = lax.optimization_barrier((base, totals[1][0]))
+                base = [base]
+            elif not last:
                 chunks.append(everyone(low, "row"))
         xs, y, packed = new, [y], True
+        if line:
+            order = [(0, 1), (1, 0), (2, 0), (1, 1), (3, 0), (2, 1), (3, 1)]
     move = call(sum_kernel, "moves", shape(low.shape, f32), everyone(low, "row", (1, 2, 3)))
     weight = call(
         weight_kernel, "weight", shape((1, scen), f32), [weight, *everyone(move, "col", (1, 2, 3))]

time: 91.1 us -> 87.6 us (0.962)
  waiting for transfers between devices: 21.8 us -> 13.8 us
  starting transfers between devices: 42.8 us -> 46.7 us
    ppermute x33 -> x36, waiting for transfers between devices: 21.8 us -> 13.8 us  [swap(): lax.ppermute(array, axis, [(i, i ^ k) for i in range(lax.axis_size(axis))])]
    ppermute x33 -> x36, starting transfers between devices: 42.8 us -> 46.7 us  [swap(): lax.ppermute(array, axis, [(i, i ^ k) for i in range(lax.axis_size(axis))])]
    pallas_call x37 -> x43, Pallas kernels: 23.1 us -> 23.5 us  [call(): pl.pallas_call(kernel, out_shape=out_shape, in_specs=specs, out_specs=out...]
  transfers between devices with their start and end apart: 33 -> 36, of which waited for: 12 -> 10; matrix products, arithmetic and copies ran while one was open for 1% -> 2% of each run, Pallas kernels for 20% -> 23%
where the time goes in v4:
time: 87.6 us; the launch traced here: 87.7 us
  starting transfers between devices  46.7 us (53%)
  Pallas kernels  23.5 us (27%)
  waiting for transfers between devices  13.8 us (16%)
  local copies, waits for them, and re-layouts  1.9 us (2%)
  between operations  1.81 us (2%)
    ppermute x36, starting transfers between devices, swap(): lax.ppermute(array, axis, [(i, i ^ k) for i in range(lax.axis_size(axis))])  46.7 us
    pallas_call x43, Pallas kernels, call(): pl.pallas_call(kernel, out_shape=out_shape, in_specs=specs, out_specs=out...  23.5 us
    ppermute x36, waiting for transfers between devices, swap(): lax.ppermute(array, axis, [(i, i ^ k) for i in range(lax.axis_size(axis))])  13.8 us
    unnamed x17, local copies, waits for them, and re-layouts  1.9 us
  transfers between devices with their start and end apart: 36, of which 10 were waited for; matrix products, arithmetic and copies ran while one was open for 2% of the time, Pallas kernels for 23%

profile of v4, /device:TPU:0, one launch (start us, length us, event | category | flops | bytes accessed | tf_op | source)
XLA Modules:
  0.0 87.7 jit_solution(4385288128769146529)
XLA Ops:
  1.6 3.1 %collective-permute-start.4 = (bf16[32,2048]{1,0:T(8,128)(2,1)S(1)}, bf16[32,2048]{1,0:T(8,128)(2,1)S(1)}, u32[]{:S(2)}, u32[]{:S(2)}) collective-permute-start(bf16[32,2048]{1,0:T(8,128)(2,1)S(1)} %get-tuple-element.38.x), channel_id=1, source_target_pairs={{0,4},{4,0},{8,12},{12,8},{1,5},{5,1},{9,13},{13,9},{2,6},{6,2},{1... | collective-permute-start | bytes 393224 | tf_op jit(solution)/shard_map/ppermute | solution.py:46
  4.7 2.6 %collective-permute-start.3 = (bf16[32,2048]{1,0:T(8,128)(2,1)S(1)}, bf16[32,2048]{1,0:T(8,128)(2,1)S(1)}, u32[]{:S(2)}, u32[]{:S(2)}) collective-permute-start(bf16[32,2048]{1,0:T(8,128)(2,1)S(1)} %get-tuple-element.38.x), channel_id=1, source_target_pairs={{0,8},{4,12},{8,0},{12,4},{1,9},{5,13},{9,1},{13,5},{2,10},{6,14},... | collective-permute-start | bytes 393224 | tf_op jit(solution)/shard_map/ppermute | solution.py:46
  7.3 1.7 %collective-permute-start.1 = (f32[2,32,256]{2,1,0:T(8,128)S(1)}, f32[2,32,256]{2,1,0:T(8,128)S(1)}, u32[]{:S(2)}, u32[]{:S(2)}) collective-permute-start(f32[2,32,256]{2,1,0:T(8,128)S(1)} %get-tuple-element.39.refs_4_), channel_id=1, source_target_pairs={{0,2},{1,3},{2,0},{3,1},{4,6},{5,7},{6,4},{7,5},{8,10},{9,11},{10,... | collective-permute-start | bytes 196616 | tf_op jit(solution)/shard_map/ppermute | solution.py:46
  9.7 3.5 %densify.1.k = bf16[512,128,128]{2,1,0:T(8,128)(2,1)S(1)} custom-call(s32[1,1]{1,0:T(1,128)S(6)} %copy.21.count, s32[1,1,256]{2,1,0:T(1,128)} %rows_in.1, s32[1,1,256]{2,1,0:T(1,128)} %cols_in.1, bf16[256,128,128]{2,1,0:T(8,128)(2,1)} %bitcast.23, bf16[512,128,128]{2,1,0:T(8,128)(2,1)S(1)} %get-tuple-element.35._), custom_call_target="tpu_custom_call", output_to_operand_aliasing={{}: (4, {})} | custom-call | bytes 33554432 | tf_op jit(solution)/shard_map/densify/pallas_call | solution.py:32
  13.2 3.0 %collective-permute-start.8 = (f32[2,32,256]{2,1,0:T(8,128)S(1)}, f32[2,32,256]{2,1,0:T(8,128)S(1)}, u32[]{:S(2)}, u32[]{:S(2)}) collective-permute-start(f32[2,32,256]{2,1,0:T(8,128)S(1)} %collective-permute-done.1.refs_6_), channel_id=1, source_target_pairs={{0,1},{1,0},{2,3},{3,2},{4,5},{5,4},{6,7},{7,6},{8,9},{9,8},{10,11... | collective-permute-start | bytes 196616 | tf_op jit(solution)/shard_map/ppermute | solution.py:46
  16.3 1.3 %forward.12.refs_0_ = f32[32,1024]{1,0:T(8,128)S(1)} custom-call(bf16[512,128,128]{2,1,0:T(8,128)(2,1)S(1)} %densify.1.k, bf16[32,2048]{1,0:T(8,128)(2,1)S(1)} %get-tuple-element.38.x), custom_call_target="tpu_custom_call" | custom-call | flops 134217728 | bytes 4194304 | tf_op jit(solution)/shard_map/forward/pallas_call | solution.py:32
  17.6 1.3 %forward.13.refs_0_ = f32[32,1024]{1,0:T(8,128)S(1)} custom-call(bf16[512,128,128]{2,1,0:T(8,128)(2,1)S(1)} %densify.1.k, bf16[32,2048]{1,0:T(8,128)(2,1)S(1)} %collective-permute-done.4.x, f32[32,1024]{1,0:T(8,128)S(1)} %forward.12.refs_0_), custom_call_target="tpu_custom_call" | custom-call | flops 134217728 | bytes 4194304 | tf_op jit(solution)/shard_map/forward/pallas_call | solution.py:32
  18.9 1.3 %forward.14.refs_0_ = f32[32,1024]{1,0:T(8,128)S(1)} custom-call(bf16[512,128,128]{2,1,0:T(8,128)(2,1)S(1)} %densify.1.k, bf16[32,2048]{1,0:T(8,128)(2,1)S(1)} %collective-permute-done.3.x, f32[32,1024]{1,0:T(8,128)S(1)} %forward.13.refs_0_), custom_call_target="tpu_custom_call" | custom-call | flops 134217728 | bytes 4194304 | tf_op jit(solution)/shard_map/forward/pallas_call | solution.py:32
  20.3 1.3 %forward.15.refs_0_ = bf16[32,1024]{1,0:T(8,128)(2,1)S(1)} custom-call(bf16[512,128,128]{2,1,0:T(8,128)(2,1)S(1)} %densify.1.k, bf16[32,2048]{1,0:T(8,128)(2,1)S(1)} %collective-permute-done.2.x, f32[32,1024]{1,0:T(8,128)S(1)} %forward.14.refs_0_), custom_call_target="tpu_custom_call" | custom-call | flops 134217728 | bytes 4194304 | tf_op jit(solution)/shard_map/forward/pallas_call | solution.py:32
  21.7 1.6 %collective-permute-start.6 = (bf16[32,1024]{1,0:T(8,128)(2,1)S(1)}, bf16[32,1024]{1,0:T(8,128)(2,1)S(1)}, u32[]{:S(2)}, u32[]{:S(2)}) collective-permute-start(bf16[32,1024]{1,0:T(8,128)(2,1)S(1)} %forward.15.refs_0_), channel_id=1, source_target_pairs={{0,2},{1,3},{2,0},{3,1},{4,6},{5,7},{6,4},{7,5},{8,10},{9,11},{10,... | collective-permute-start | bytes 196616 | tf_op jit(solution)/shard_map/ppermute | solution.py:46
  23.5 2.3 %collective-permute-done.7.refs_3_ = bf16[32,1024]{1,0:T(8,128)(2,1)S(1)} collective-permute-done((bf16[32,1024]{1,0:T(8,128)(2,1)S(1)}, bf16[32,1024]{1,0:T(8,128)(2,1)S(1)}, u32[]{:S(2)}, u32[]{:S(2)}) %collective-permute-start.7) | collective-permute-done | bytes 65568 | tf_op jit(solution)/shard_map/ppermute | solution.py:46
  25.9 1.6 %collective-permute-done.6.refs_2_ = bf16[32,1024]{1,0:T(8,128)(2,1)S(1)} collective-permute-done((bf16[32,1024]{1,0:T(8,128)(2,1)S(1)}, bf16[32,1024]{1,0:T(8,128)(2,1)S(1)}, u32[]{:S(2)}, u32[]{:S(2)}) %collective-permute-start.6) | collective-permute-done | bytes 65568 | tf_op jit(solution)/shard_map/ppermute | solution.py:46
  28.9 2.1 %collective-permute-start.10 = (bf16[32,1024]{1,0:T(8,128)(2,1)S(1)}, bf16[32,1024]{1,0:T(8,128)(2,1)S(1)}, u32[]{:S(2)}, u32[]{:S(2)}) collective-permute-start(bf16[32,1024]{1,0:T(8,128)(2,1)S(1)} %backward.15), channel_id=1, source_target_pairs={{0,4},{4,0},{8,12},{12,8},{1,5},{5,1},{9,13},{13,9},{2,6},{6,2},{1... | collective-permute-start | bytes 196616 | tf_op jit(solution)/shard_map/ppermute | solution.py:46
  31.0 2.3 %collective-permute-start.9 = (bf16[32,1024]{1,0:T(8,128)(2,1)S(1)}, bf16[32,1024]{1,0:T(8,128)(2,1)S(1)}, u32[]{:S(2)}, u32[]{:S(2)}) collective-permute-start(bf16[32,1024]{1,0:T(8,128)(2,1)S(1)} %backward.14), channel_id=1, source_target_pairs={{0,8},{4,12},{8,0},{12,4},{1,9},{5,13},{9,1},{13,5},{2,10},{6,14},... | collective-permute-start | bytes 196616 | tf_op jit(solution)/shard_map/ppermute | solution.py:46
  33.7 1.5 %collective-permute-start.11 = (bf16[32,1024]{1,0:T(8,128)(2,1)S(1)}, bf16[32,1024]{1,0:T(8,128)(2,1)S(1)}, u32[]{:S(2)}, u32[]{:S(2)}) collective-permute-start(bf16[32,1024]{1,0:T(8,128)(2,1)S(1)} %backward.16), channel_id=1, source_target_pairs={{0,12},{4,8},{8,4},{12,0},{1,13},{5,9},{9,5},{13,1},{2,14},{6,10},... | collective-permute-start | bytes 196616 | tf_op jit(solution)/shard_map/ppermute | solution.py:46
  36.7 2.5 %collective-permute-start.14 = (bf16[32,1024]{1,0:T(8,128)(2,1)S(1)}, bf16[32,1024]{1,0:T(8,128)(2,1)S(1)}, u32[]{:S(2)}, u32[]{:S(2)}) collective-permute-start(bf16[32,1024]{1,0:T(8,128)(2,1)S(1)} %add.11), channel_id=1, source_target_pairs={{0,8},{4,12},{8,0},{12,4},{1,9},{5,13},{9,1},{13,5},{2,10},{6,14},... | collective-permute-start | bytes 196616 | tf_op jit(solution)/shard_map/ppermute | solution.py:46
  40.3 3.5 %collective-permute-start.17 = (bf16[32,1024]{1,0:T(8,128)(2,1)S(1)}, bf16[32,1024]{1,0:T(8,128)(2,1)S(1)}, u32[]{:S(2)}, u32[]{:S(2)}) collective-permute-start(bf16[32,1024]{1,0:T(8,128)(2,1)S(1)} %get-tuple-element.49.x), channel_id=1, source_target_pairs={{0,8},{4,12},{8,0},{12,4},{1,9},{5,13},{9,1},{13,5},{2,10},{6,14},... | collective-permute-start | bytes 196616 | tf_op jit(solution)/shard_map/ppermute | solution.py:46
  45.4 2.1 %collective-permute-start.19 = (bf16[32,1152]{1,0:T(8,128)(2,1)S(1)}, bf16[32,1152]{1,0:T(8,128)(2,1)S(1)}, u32[]{:S(2)}, u32[]{:S(2)}) collective-permute-start(bf16[32,1152]{1,0:T(8,128)(2,1)S(1)} %get-tuple-element.52.x.refs_1_), channel_id=1, source_target_pairs={{0,4},{4,0},{8,12},{12,8},{1,5},{5,1},{9,13},{13,9},{2,6},{6,2},{1... | collective-permute-start | bytes 221192 | tf_op jit(solution)/shard_map/ppermute | solution.py:46
  49.0 2.9 %collective-permute-start.15 = (bf16[32,1152]{1,0:T(8,128)(2,1)S(1)}, bf16[32,1152]{1,0:T(8,128)(2,1)S(1)}, u32[]{:S(2)}, u32[]{:S(2)}) collective-permute-start(bf16[32,1152]{1,0:T(8,128)(2,1)S(1)} %get-tuple-element.52.x.refs_1_), channel_id=1, source_target_pairs={{0,12},{4,8},{8,4},{12,0},{1,13},{5,9},{9,5},{13,1},{2,14},{6,10},... | collective-permute-start | bytes 221192 | tf_op jit(solution)/shard_map/ppermute | solution.py:46
  57.7 1.2 %collective-permute-start.21 = (bf16[32,1152]{1,0:T(8,128)(2,1)S(1)}, bf16[32,1152]{1,0:T(8,128)(2,1)S(1)}, u32[]{:S(2)}, u32[]{:S(2)}) collective-permute-start(bf16[32,1152]{1,0:T(8,128)(2,1)S(1)} %forward.23.refs_0_), channel_id=1, source_target_pairs={{0,1},{1,0},{2,3},{3,2},{4,5},{5,4},{6,7},{7,6},{8,9},{9,8},{10,11... | collective-permute-start | bytes 221192 | tf_op jit(solution)/shard_map/ppermute | solution.py:46
  58.9 2.1 %collective-permute-done.23.refs_3_ = bf16[32,1152]{1,0:T(8,128)(2,1)S(1)} collective-permute-done((bf16[32,1152]{1,0:T(8,128)(2,1)S(1)}, bf16[32,1152]{1,0:T(8,128)(2,1)S(1)}, u32[]{:S(2)}, u32[]{:S(2)}) %collective-permute-start.23) | collective-permute-done | bytes 73760 | tf_op jit(solution)/shard_map/ppermute | solution.py:46
  61.0 1.2 %collective-permute-done.22.refs_2_ = bf16[32,1152]{1,0:T(8,128)(2,1)S(1)} collective-permute-done((bf16[32,1152]{1,0:T(8,128)(2,1)S(1)}, bf16[32,1152]{1,0:T(8,128)(2,1)S(1)}, u32[]{:S(2)}, u32[]{:S(2)}) %collective-permute-start.22) | collective-permute-done | bytes 73760 | tf_op jit(solution)/shard_map/ppermute | solution.py:46
  64.3 1.8 %collective-permute-start.26 = (bf16[32,1024]{1,0:T(8,128)(2,1)S(1)}, bf16[32,1024]{1,0:T(8,128)(2,1)S(1)}, u32[]{:S(2)}, u32[]{:S(2)}) collective-permute-start(bf16[32,1024]{1,0:T(8,128)(2,1)S(1)} %backward.23), channel_id=1, source_target_pairs={{0,12},{4,8},{8,4},{12,0},{1,13},{5,9},{9,5},{13,1},{2,14},{6,10},... | collective-permute-start | bytes 196616 | tf_op jit(solution)/shard_map/ppermute | solution.py:46
  66.1 1.1 %collective-permute-start.25 = (bf16[32,1024]{1,0:T(8,128)(2,1)S(1)}, bf16[32,1024]{1,0:T(8,128)(2,1)S(1)}, u32[]{:S(2)}, u32[]{:S(2)}) collective-permute-start(bf16[32,1024]{1,0:T(8,128)(2,1)S(1)} %backward.22), channel_id=1, source_target_pairs={{0,4},{4,0},{8,12},{12,8},{1,5},{5,1},{9,13},{13,9},{2,6},{6,2},{1... | collective-permute-start | bytes 196616 | tf_op jit(solution)/shard_map/ppermute | solution.py:46
  67.2 1.5 %collective-permute-start.24 = (bf16[32,1024]{1,0:T(8,128)(2,1)S(1)}, bf16[32,1024]{1,0:T(8,128)(2,1)S(1)}, u32[]{:S(2)}, u32[]{:S(2)}) collective-permute-start(bf16[32,1024]{1,0:T(8,128)(2,1)S(1)} %backward.21), channel_id=1, source_target_pairs={{0,8},{4,12},{8,0},{12,4},{1,9},{5,13},{9,1},{13,5},{2,10},{6,14},... | collective-permute-start | bytes 196616 | tf_op jit(solution)/shard_map/ppermute | solution.py:46
  69.2 1.2 %collective-permute-start.27 = (bf16[32,1024]{1,0:T(8,128)(2,1)S(1)}, bf16[32,1024]{1,0:T(8,128)(2,1)S(1)}, u32[]{:S(2)}, u32[]{:S(2)}) collective-permute-start(bf16[32,1024]{1,0:T(8,128)(2,1)S(1)} %backward.26), channel_id=1, source_target_pairs={{0,4},{4,0},{8,12},{12,8},{1,5},{5,1},{9,13},{13,9},{2,6},{6,2},{1... | collective-permute-start | bytes 196616 | tf_op jit(solution)/shard_map/ppermute | solution.py:46
  70.8 1.3 %collective-permute-start.29 = (bf16[32,1024]{1,0:T(8,128)(2,1)S(1)}, bf16[32,1024]{1,0:T(8,128)(2,1)S(1)}, u32[]{:S(2)}, u32[]{:S(2)}) collective-permute-start(bf16[32,1024]{1,0:T(8,128)(2,1)S(1)} %add.15), channel_id=1, source_target_pairs={{0,8},{4,12},{8,0},{12,4},{1,9},{5,13},{9,1},{13,5},{2,10},{6,14},... | collective-permute-start | bytes 196616 | tf_op jit(solution)/shard_map/ppermute | solution.py:46
  72.9 1.7 %collective-permute-done.24.part = bf16[32,1024]{1,0:T(8,128)(2,1)S(1)} collective-permute-done((bf16[32,1024]{1,0:T(8,128)(2,1)S(1)}, bf16[32,1024]{1,0:T(8,128)(2,1)S(1)}, u32[]{:S(2)}, u32[]{:S(2)}) %collective-permute-start.24) | collective-permute-done | bytes 65568 | tf_op jit(solution)/shard_map/ppermute | solution.py:46
  74.7 2.1 %collective-permute-done.29.refs_3_ = bf16[32,1024]{1,0:T(8,128)(2,1)S(1)} collective-permute-done((bf16[32,1024]{1,0:T(8,128)(2,1)S(1)}, bf16[32,1024]{1,0:T(8,128)(2,1)S(1)}, u32[]{:S(2)}, u32[]{:S(2)}) %collective-permute-start.29) | collective-permute-done | bytes 65568 | tf_op jit(solution)/shard_map/ppermute | solution.py:46
  77.1 1.8 %collective-permute-start.32 = (f32[2,32]{1,0:T(2,128)S(1)}, f32[2,32]{1,0:T(2,128)S(1)}, u32[]{:S(2)}, u32[]{:S(2)}) collective-permute-start(f32[2,32]{1,0:T(2,128)S(1)} %get-tuple-element.66.refs_0_), channel_id=1, source_target_pairs={{0,12},{4,8},{8,4},{12,0},{1,13},{5,9},{9,5},{13,1},{2,14},{6,10},... | collective-permute-start | bytes 776 | tf_op jit(solution)/shard_map/ppermute | solution.py:46
  79.0 2.6 %collective-permute-start.30 = (f32[2,32]{1,0:T(2,128)S(1)}, f32[2,32]{1,0:T(2,128)S(1)}, u32[]{:S(2)}, u32[]{:S(2)}) collective-permute-start(f32[2,32]{1,0:T(2,128)S(1)} %get-tuple-element.66.refs_0_), channel_id=1, source_target_pairs={{0,4},{4,0},{8,12},{12,8},{1,5},{5,1},{9,13},{13,9},{2,6},{6,2},{1... | collective-permute-start | bytes 776 | tf_op jit(solution)/shard_map/ppermute | solution.py:46
  83.5 1.6 %collective-permute-start.34 = (f32[2,32]{1,0:T(2,128)S(1)}, f32[2,32]{1,0:T(2,128)S(1)}, u32[]{:S(2)}, u32[]{:S(2)}) collective-permute-start(f32[2,32]{1,0:T(2,128)S(1)} %moves.1.refs_0_), channel_id=1, source_target_pairs={{0,2},{1,3},{2,0},{3,1},{4,6},{5,7},{6,4},{7,5},{8,10},{9,11},{10,... | collective-permute-start | bytes 776 | tf_op jit(solution)/shard_map/ppermute | solution.py:46
  (100 shorter events, 23.2 us)
Async XLA Ops:
  1.6 15.9 %collective-permute-start.4 = (bf16[32,2048]{1,0:T(8,128)(2,1)S(1)}, bf16[32,2048]{1,0:T(8,128)(2,1)S(1)}, u32[]{:S(2)}, u32[]{:S(2)}) collective-permute-start(bf16[32,2048]{1,0:T(8,128)(2,1)S(1)} %get-tuple-element.38.x), channel_id=1, source_target_pairs={{0,4},{4,0},{8,12},{12,8},{1,5},{5,1},{9,13},{13,9},{2,6},{6,2},{1... | collective-permute-start | bytes 393224 | tf_op jit(solution)/shard_map/ppermute | solution.py:46
  4.7 14.2 %collective-permute-start.3 = (bf16[32,2048]{1,0:T(8,128)(2,1)S(1)}, bf16[32,2048]{1,0:T(8,128)(2,1)S(1)}, u32[]{:S(2)}, u32[]{:S(2)}) collective-permute-start(bf16[32,2048]{1,0:T(8,128)(2,1)S(1)} %get-tuple-element.38.x), channel_id=1, source_target_pairs={{0,8},{4,12},{8,0},{12,4},{1,9},{5,13},{9,1},{13,5},{2,10},{6,14},... | collective-permute-start | bytes 393224 | tf_op jit(solution)/shard_map/ppermute | solution.py:46
  7.3 13.0 %collective-permute-start.2 = (bf16[32,2048]{1,0:T(8,128)(2,1)S(1)}, bf16[32,2048]{1,0:T(8,128)(2,1)S(1)}, u32[]{:S(2)}, u32[]{:S(2)}) collective-permute-start(bf16[32,2048]{1,0:T(8,128)(2,1)S(1)} %get-tuple-element.38.x), channel_id=1, source_target_pairs={{0,12},{4,8},{8,4},{12,0},{1,13},{5,9},{9,5},{13,1},{2,14},{6,10},... | collective-permute-start | bytes 393224 | tf_op jit(solution)/shard_map/ppermute | solution.py:46
  7.3 5.9 %collective-permute-start.1 = (f32[2,32,256]{2,1,0:T(8,128)S(1)}, f32[2,32,256]{2,1,0:T(8,128)S(1)}, u32[]{:S(2)}, u32[]{:S(2)}) collective-permute-start(f32[2,32,256]{2,1,0:T(8,128)S(1)} %get-tuple-element.39.refs_4_), channel_id=1, source_target_pairs={{0,2},{1,3},{2,0},{3,1},{4,6},{5,7},{6,4},{7,5},{8,10},{9,11},{10,... | collective-permute-start | bytes 196616 | tf_op jit(solution)/shard_map/ppermute | solution.py:46
  9.0 4.2 %collective-permute-start = (f32[2,32,256]{2,1,0:T(8,128)S(1)}, f32[2,32,256]{2,1,0:T(8,128)S(1)}, u32[]{:S(2)}, u32[]{:S(2)}) collective-permute-start(f32[2,32,256]{2,1,0:T(8,128)S(1)} %get-tuple-element.39.refs_4_), channel_id=1, source_target_pairs={{0,1},{1,0},{2,3},{3,2},{4,5},{5,4},{6,7},{7,6},{8,9},{9,8},{10,11... | collective-permute-start | bytes 196616 | tf_op jit(solution)/shard_map/ppermute | solution.py:46
  13.2 10.3 %collective-permute-start.8 = (f32[2,32,256]{2,1,0:T(8,128)S(1)}, f32[2,32,256]{2,1,0:T(8,128)S(1)}, u32[]{:S(2)}, u32[]{:S(2)}) collective-permute-start(f32[2,32,256]{2,1,0:T(8,128)S(1)} %collective-permute-done.1.refs_6_), channel_id=1, source_target_pairs={{0,1},{1,0},{2,3},{3,2},{4,5},{5,4},{6,7},{7,6},{8,9},{9,8},{10,11... | collective-permute-start | bytes 196616 | tf_op jit(solution)/shard_map/ppermute | solution.py:46
  21.6 4.3 %collective-permute-start.7 = (bf16[32,1024]{1,0:T(8,128)(2,1)S(1)}, bf16[32,1024]{1,0:T(8,128)(2,1)S(1)}, u32[]{:S(2)}, u32[]{:S(2)}) collective-permute-start(bf16[32,1024]{1,0:T(8,128)(2,1)S(1)} %forward.15.refs_0_), channel_id=1, source_target_pairs={{0,3},{1,2},{2,1},{3,0},{4,7},{5,6},{6,5},{7,4},{8,11},{9,10},{10,... | collective-permute-start | bytes 196616 | tf_op jit(solution)/shard_map/ppermute | solution.py:46
  21.7 5.8 %collective-permute-start.6 = (bf16[32,1024]{1,0:T(8,128)(2,1)S(1)}, bf16[32,1024]{1,0:T(8,128)(2,1)S(1)}, u32[]{:S(2)}, u32[]{:S(2)}) collective-permute-start(bf16[32,1024]{1,0:T(8,128)(2,1)S(1)} %forward.15.refs_0_), channel_id=1, source_target_pairs={{0,2},{1,3},{2,0},{3,1},{4,6},{5,7},{6,4},{7,5},{8,10},{9,11},{10,... | collective-permute-start | bytes 196616 | tf_op jit(solution)/shard_map/ppermute | solution.py:46
  23.3 4.1 %collective-permute-start.5 = (bf16[32,1024]{1,0:T(8,128)(2,1)S(1)}, bf16[32,1024]{1,0:T(8,128)(2,1)S(1)}, u32[]{:S(2)}, u32[]{:S(2)}) collective-permute-start(bf16[32,1024]{1,0:T(8,128)(2,1)S(1)} %forward.15.refs_0_), channel_id=1, source_target_pairs={{0,1},{1,0},{2,3},{3,2},{4,5},{5,4},{6,7},{7,6},{8,9},{9,8},{10,11... | collective-permute-start | bytes 196616 | tf_op jit(solution)/shard_map/ppermute | solution.py:46
  28.0 8.7 %collective-permute-start.13 = (bf16[32,1024]{1,0:T(8,128)(2,1)S(1)}, bf16[32,1024]{1,0:T(8,128)(2,1)S(1)}, u32[]{:S(2)}, u32[]{:S(2)}) collective-permute-start(bf16[32,1024]{1,0:T(8,128)(2,1)S(1)} %get-tuple-element.51), channel_id=1, source_target_pairs={{0,4},{4,0},{8,12},{12,8},{1,5},{5,1},{9,13},{13,9},{2,6},{6,2},{1... | collective-permute-start | bytes 196616 | tf_op jit(solution)/shard_map/ppermute | solution.py:46
  28.9 10.7 %collective-permute-start.10 = (bf16[32,1024]{1,0:T(8,128)(2,1)S(1)}, bf16[32,1024]{1,0:T(8,128)(2,1)S(1)}, u32[]{:S(2)}, u32[]{:S(2)}) collective-permute-start(bf16[32,1024]{1,0:T(8,128)(2,1)S(1)} %backward.15), channel_id=1, source_target_pairs={{0,4},{4,0},{8,12},{12,8},{1,5},{5,1},{9,13},{13,9},{2,6},{6,2},{1... | collective-permute-start | bytes 196616 | tf_op jit(solution)/shard_map/ppermute | solution.py:46
  31.0 8.6 %collective-permute-start.9 = (bf16[32,1024]{1,0:T(8,128)(2,1)S(1)}, bf16[32,1024]{1,0:T(8,128)(2,1)S(1)}, u32[]{:S(2)}, u32[]{:S(2)}) collective-permute-start(bf16[32,1024]{1,0:T(8,128)(2,1)S(1)} %backward.14), channel_id=1, source_target_pairs={{0,8},{4,12},{8,0},{12,4},{1,9},{5,13},{9,1},{13,5},{2,10},{6,14},... | collective-permute-start | bytes 196616 | tf_op jit(solution)/shard_map/ppermute | solution.py:46
  33.7 6.3 %collective-permute-start.11 = (bf16[32,1024]{1,0:T(8,128)(2,1)S(1)}, bf16[32,1024]{1,0:T(8,128)(2,1)S(1)}, u32[]{:S(2)}, u32[]{:S(2)}) collective-permute-start(bf16[32,1024]{1,0:T(8,128)(2,1)S(1)} %backward.16), channel_id=1, source_target_pairs={{0,12},{4,8},{8,4},{12,0},{1,13},{5,9},{9,5},{13,1},{2,14},{6,10},... | collective-permute-start | bytes 196616 | tf_op jit(solution)/shard_map/ppermute | solution.py:46
  35.6 8.7 %collective-permute-start.12 = (bf16[32,1024]{1,0:T(8,128)(2,1)S(1)}, bf16[32,1024]{1,0:T(8,128)(2,1)S(1)}, u32[]{:S(2)}, u32[]{:S(2)}) collective-permute-start(bf16[32,1024]{1,0:T(8,128)(2,1)S(1)} %backward.19), channel_id=1, source_target_pairs={{0,4},{4,0},{8,12},{12,8},{1,5},{5,1},{9,13},{13,9},{2,6},{6,2},{1... | collective-permute-start | bytes 196616 | tf_op jit(solution)/shard_map/ppermute | solution.py:46
  36.7 8.3 %collective-permute-start.14 = (bf16[32,1024]{1,0:T(8,128)(2,1)S(1)}, bf16[32,1024]{1,0:T(8,128)(2,1)S(1)}, u32[]{:S(2)}, u32[]{:S(2)}) collective-permute-start(bf16[32,1024]{1,0:T(8,128)(2,1)S(1)} %add.11), channel_id=1, source_target_pairs={{0,8},{4,12},{8,0},{12,4},{1,9},{5,13},{9,1},{13,5},{2,10},{6,14},... | collective-permute-start | bytes 196616 | tf_op jit(solution)/shard_map/ppermute | solution.py:46
  40.3 7.8 %collective-permute-start.17 = (bf16[32,1024]{1,0:T(8,128)(2,1)S(1)}, bf16[32,1024]{1,0:T(8,128)(2,1)S(1)}, u32[]{:S(2)}, u32[]{:S(2)}) collective-permute-start(bf16[32,1024]{1,0:T(8,128)(2,1)S(1)} %get-tuple-element.49.x), channel_id=1, source_target_pairs={{0,8},{4,12},{8,0},{12,4},{1,9},{5,13},{9,1},{13,5},{2,10},{6,14},... | collective-permute-start | bytes 196616 | tf_op jit(solution)/shard_map/ppermute | solution.py:46
  44.2 8.3 %collective-permute-start.20 = (bf16[32,1024]{1,0:T(8,128)(2,1)S(1)}, bf16[32,1024]{1,0:T(8,128)(2,1)S(1)}, u32[]{:S(2)}, u32[]{:S(2)}) collective-permute-start(bf16[32,1024]{1,0:T(8,128)(2,1)S(1)} %get-tuple-element.49.x), channel_id=1, source_target_pairs={{0,4},{4,0},{8,12},{12,8},{1,5},{5,1},{9,13},{13,9},{2,6},{6,2},{1... | collective-permute-start | bytes 196616 | tf_op jit(solution)/shard_map/ppermute | solution.py:46
  45.4 8.6 %collective-permute-start.19 = (bf16[32,1152]{1,0:T(8,128)(2,1)S(1)}, bf16[32,1152]{1,0:T(8,128)(2,1)S(1)}, u32[]{:S(2)}, u32[]{:S(2)}) collective-permute-start(bf16[32,1152]{1,0:T(8,128)(2,1)S(1)} %get-tuple-element.52.x.refs_1_), channel_id=1, source_target_pairs={{0,4},{4,0},{8,12},{12,8},{1,5},{5,1},{9,13},{13,9},{2,6},{6,2},{1... | collective-permute-start | bytes 221192 | tf_op jit(solution)/shard_map/ppermute | solution.py:46
  47.4 8.1 %collective-permute-start.16 = (bf16[32,1152]{1,0:T(8,128)(2,1)S(1)}, bf16[32,1152]{1,0:T(8,128)(2,1)S(1)}, u32[]{:S(2)}, u32[]{:S(2)}) collective-permute-start(bf16[32,1152]{1,0:T(8,128)(2,1)S(1)} %get-tuple-element.52.x.refs_1_), channel_id=1, source_target_pairs={{0,8},{4,12},{8,0},{12,4},{1,9},{5,13},{9,1},{13,5},{2,10},{6,14},... | collective-permute-start | bytes 221192 | tf_op jit(solution)/shard_map/ppermute | solution.py:46
  48.0 6.7 %collective-permute-start.18 = (bf16[32,1024]{1,0:T(8,128)(2,1)S(1)}, bf16[32,1024]{1,0:T(8,128)(2,1)S(1)}, u32[]{:S(2)}, u32[]{:S(2)}) collective-permute-start(bf16[32,1024]{1,0:T(8,128)(2,1)S(1)} %collective-permute-done.17.x), channel_id=1, source_target_pairs={{0,4},{4,0},{8,12},{12,8},{1,5},{5,1},{9,13},{13,9},{2,6},{6,2},{1... | collective-permute-start | bytes 196616 | tf_op jit(solution)/shard_map/ppermute | solution.py:46
  49.0 7.2 %collective-permute-start.15 = (bf16[32,1152]{1,0:T(8,128)(2,1)S(1)}, bf16[32,1152]{1,0:T(8,128)(2,1)S(1)}, u32[]{:S(2)}, u32[]{:S(2)}) collective-permute-start(bf16[32,1152]{1,0:T(8,128)(2,1)S(1)} %get-tuple-element.52.x.refs_1_), channel_id=1, source_target_pairs={{0,12},{4,8},{8,4},{12,0},{1,13},{5,9},{9,5},{13,1},{2,14},{6,10},... | collective-permute-start | bytes 221192 | tf_op jit(solution)/shard_map/ppermute | solution.py:46
  57.1 5.2 %collective-permute-start.22 = (bf16[32,1152]{1,0:T(8,128)(2,1)S(1)}, bf16[32,1152]{1,0:T(8,128)(2,1)S(1)}, u32[]{:S(2)}, u32[]{:S(2)}) collective-permute-start(bf16[32,1152]{1,0:T(8,128)(2,1)S(1)} %forward.23.refs_0_), channel_id=1, source_target_pairs={{0,2},{1,3},{2,0},{3,1},{4,6},{5,7},{6,4},{7,5},{8,10},{9,11},{10,... | collective-permute-start | bytes 221192 | tf_op jit(solution)/shard_map/ppermute | solution.py:46
  57.7 4.6 %collective-permute-start.21 = (bf16[32,1152]{1,0:T(8,128)(2,1)S(1)}, bf16[32,1152]{1,0:T(8,128)(2,1)S(1)}, u32[]{:S(2)}, u32[]{:S(2)}) collective-permute-start(bf16[32,1152]{1,0:T(8,128)(2,1)S(1)} %forward.23.refs_0_), channel_id=1, source_target_pairs={{0,1},{1,0},{2,3},{3,2},{4,5},{5,4},{6,7},{7,6},{8,9},{9,8},{10,11... | collective-permute-start | bytes 221192 | tf_op jit(solution)/shard_map/ppermute | solution.py:46
  63.0 7.8 %collective-permute-start.28 = (bf16[32,1024]{1,0:T(8,128)(2,1)S(1)}, bf16[32,1024]{1,0:T(8,128)(2,1)S(1)}, u32[]{:S(2)}, u32[]{:S(2)}) collective-permute-start(bf16[32,1024]{1,0:T(8,128)(2,1)S(1)} %get-tuple-element.61), channel_id=1, source_target_pairs={{0,4},{4,0},{8,12},{12,8},{1,5},{5,1},{9,13},{13,9},{2,6},{6,2},{1... | collective-permute-start | bytes 196616 | tf_op jit(solution)/shard_map/ppermute | solution.py:46
  64.3 10.3 %collective-permute-start.26 = (bf16[32,1024]{1,0:T(8,128)(2,1)S(1)}, bf16[32,1024]{1,0:T(8,128)(2,1)S(1)}, u32[]{:S(2)}, u32[]{:S(2)}) collective-permute-start(bf16[32,1024]{1,0:T(8,128)(2,1)S(1)} %backward.23), channel_id=1, source_target_pairs={{0,12},{4,8},{8,4},{12,0},{1,13},{5,9},{9,5},{13,1},{2,14},{6,10},... | collective-permute-start | bytes 196616 | tf_op jit(solution)/shard_map/ppermute | solution.py:46
  66.1 8.5 %collective-permute-start.25 = (bf16[32,1024]{1,0:T(8,128)(2,1)S(1)}, bf16[32,1024]{1,0:T(8,128)(2,1)S(1)}, u32[]{:S(2)}, u32[]{:S(2)}) collective-permute-start(bf16[32,1024]{1,0:T(8,128)(2,1)S(1)} %backward.22), channel_id=1, source_target_pairs={{0,4},{4,0},{8,12},{12,8},{1,5},{5,1},{9,13},{13,9},{2,6},{6,2},{1... | collective-permute-start | bytes 196616 | tf_op jit(solution)/shard_map/ppermute | solution.py:46
  67.2 7.3 %collective-permute-start.24 = (bf16[32,1024]{1,0:T(8,128)(2,1)S(1)}, bf16[32,1024]{1,0:T(8,128)(2,1)S(1)}, u32[]{:S(2)}, u32[]{:S(2)}) collective-permute-start(bf16[32,1024]{1,0:T(8,128)(2,1)S(1)} %backward.21), channel_id=1, source_target_pairs={{0,8},{4,12},{8,0},{12,4},{1,9},{5,13},{9,1},{13,5},{2,10},{6,14},... | collective-permute-start | bytes 196616 | tf_op jit(solution)/shard_map/ppermute | solution.py:46
  69.2 5.4 %collective-permute-start.27 = (bf16[32,1024]{1,0:T(8,128)(2,1)S(1)}, bf16[32,1024]{1,0:T(8,128)(2,1)S(1)}, u32[]{:S(2)}, u32[]{:S(2)}) collective-permute-start(bf16[32,1024]{1,0:T(8,128)(2,1)S(1)} %backward.26), channel_id=1, source_target_pairs={{0,4},{4,0},{8,12},{12,8},{1,5},{5,1},{9,13},{13,9},{2,6},{6,2},{1... | collective-permute-start | bytes 196616 | tf_op jit(solution)/shard_map/ppermute | solution.py:46
  70.8 5.9 %collective-permute-start.29 = (bf16[32,1024]{1,0:T(8,128)(2,1)S(1)}, bf16[32,1024]{1,0:T(8,128)(2,1)S(1)}, u32[]{:S(2)}, u32[]{:S(2)}) collective-permute-start(bf16[32,1024]{1,0:T(8,128)(2,1)S(1)} %add.15), channel_id=1, source_target_pairs={{0,8},{4,12},{8,0},{12,4},{1,9},{5,13},{9,1},{13,5},{2,10},{6,14},... | collective-permute-start | bytes 196616 | tf_op jit(solution)/shard_map/ppermute | solution.py:46
  77.1 5.4 %collective-permute-start.32 = (f32[2,32]{1,0:T(2,128)S(1)}, f32[2,32]{1,0:T(2,128)S(1)}, u32[]{:S(2)}, u32[]{:S(2)}) collective-permute-start(f32[2,32]{1,0:T(2,128)S(1)} %get-tuple-element.66.refs_0_), channel_id=1, source_target_pairs={{0,12},{4,8},{8,4},{12,0},{1,13},{5,9},{9,5},{13,1},{2,14},{6,10},... | collective-permute-start | bytes 776 | tf_op jit(solution)/shard_map/ppermute | solution.py:46
  78.9 4.5 %collective-permute-start.31 = (f32[2,32]{1,0:T(2,128)S(1)}, f32[2,32]{1,0:T(2,128)S(1)}, u32[]{:S(2)}, u32[]{:S(2)}) collective-permute-start(f32[2,32]{1,0:T(2,128)S(1)} %get-tuple-element.66.refs_0_), channel_id=1, source_target_pairs={{0,8},{4,12},{8,0},{12,4},{1,9},{5,13},{9,1},{13,5},{2,10},{6,14},... | collective-permute-start | bytes 776 | tf_op jit(solution)/shard_map/ppermute | solution.py:46
  79.0 4.4 %collective-permute-start.30 = (f32[2,32]{1,0:T(2,128)S(1)}, f32[2,32]{1,0:T(2,128)S(1)}, u32[]{:S(2)}, u32[]{:S(2)}) collective-permute-start(f32[2,32]{1,0:T(2,128)S(1)} %get-tuple-element.66.refs_0_), channel_id=1, source_target_pairs={{0,4},{4,0},{8,12},{12,8},{1,5},{5,1},{9,13},{13,9},{2,6},{6,2},{1... | collective-permute-start | bytes 776 | tf_op jit(solution)/shard_map/ppermute | solution.py:46
  (11 other events, 52.3 us)

commit v5 on v4

--- a/solution.py
+++ b/solution.py
@@ -328,10 +328,10 @@
     return jnp.sqrt(weight * jnp.sqrt(primal + EPSILON) / jnp.sqrt(dual + EPSILON))
 
 
-def dual_kernel(rt, per, n_col, packed, has_y, first, start, k, step, weight, *refs):
+def dual_kernel(rt, per, n_col, packed, has_y, sends, k, step, weight, *refs):
     row, col = lax.axis_index("row"), lax.axis_index("col")
     parts, both, refs = refs[:n_col], refs[n_col : 2 * n_col], refs[2 * n_col :]
-    y_out, bar_out, move_out, send_out, weight_out = refs[has_y:]
+    y_out, bar_out, move_out, weight_out, *send_out = refs[has_y:]
     w = to_column(weight[...])
     if packed:
         moves = [unpack_columns(part[:, bar_out.shape[1] :], 2) for part in parts]
@@ -353,7 +353,8 @@
             y_out[...] = new
         bar_out[:, here] = (2.0 * new - old).astype(bf16)
 
-    backward(k, bar_out[...], row ^ first, start, rt, per, send_out)
+    for (i, start), out in zip(sends, send_out):
+        backward(k, bar_out[...], row ^ i, start, rt, per, out)
 
 
 def backward_kernel(rt, per, i, start, k, d, out):
@@ -440,7 +441,7 @@
         return backward_part(k, bar, i, p * n, n, dtype, rt, per)
 
     places = rt * per * n_row
-    clean = places // 4
+    clean = places // 2
     dims = (places,) + tiles.shape[1:]
     low, both, k = start(primal_vars, dual_vars, right_side, dims, clean)
     chunks = [everyone(low, "row")]
@@ -456,43 +457,47 @@
     weight = primal_weight[None]
     low_bound, high_bound, kind = lower_bound[None], upper_bound[None], bound_kind[None]
     xs, y, packed = [primal_vars], [], False
-    order, base = [(i, 0) for i in range(n_row)], []
+    visits, base = [(i, 0) for i in range(n_row)], []
     for sweep in range(ITERS):
         last = sweep == ITERS - 1
-        part = forward_parts(k, chunks, rt, per, per // len(chunks), packed, order, base)
-        first = 3 if line else partners(n_row)[0]
-        y, bar, moved, sent, weight = call(
-            functools.partial(
-                dual_kernel, rt, per, n_col, packed, len(y), first, (pieces - 1) * n
-            ),
+        part = forward_parts(k, chunks, rt, per, per // len(chunks), packed, visits, base)
+        order = partners(n_row, (2, 3, 1))
+        sends = [(3, n), (order[0], 0)] if line else [(order[0], 0)]
+        y, bar, moved, weight, *sent = call(
+            functools.partial(dual_kernel, rt, per, n_col, packed, len(y), sends),
             "dual",
             [
                 shape(dual_vars.shape if last else (n_col,) + dual_vars.shape, f32),
                 shape((scen, rt * width), bf16),
                 shape((scen, 2), f32),
-                shape((scen, n * width), bf16),
                 shape((1, scen), f32),
+                *[shape((scen, n * width), bf16)] * len(sends),
             ],
             [k, step, weight, *everyone(part, "col", (1, 3, 2)), *both, *y],
             cost=cost(k, n, rt),
         )
-        hop = swap(sent, "row", 1 if line else first)
-        got = [] if line else [hop]
-        for i in partners(n_row):
-            if line or i != first:
-                sent = part_for(i, 0)
-                got.append(swap(sent, "row", i))
-                sent, bar = lax.optimization_barrier((sent, bar))
+        hop = swap(sent[0], "row", 1) if line else None
+        got = [swap(sent[-1], "row", order[0])]
+        for i in order[1:]:
+            sent = part_for(i, 0)
+            got.append(swap(sent, "row", i))
+            sent, bar = lax.optimization_barrier((sent, bar))
         totals = [[part_for(0, 0, f32)]]
         if line:
             near = part_for(1, 1)
             cross = part_for(2, 1, f32)
             near = swap(near, "row", 1)
+            hop, got[0] = lax.optimization_barrier((hop, got[0]))
             cross = swap(add(cross, hop, bf16), "row", 2)
-            totals.append([add(part_for(0, 1, f32), near), cross])
-        for piece in got[:-1]:
+            totals.append([part_for(0, 1, f32), near, cross])
+        for piece in got if last else got[:-1]:
             totals[0] = [add(totals[0][0], piece)]
-        totals[0].append(got[-1])
+        if not last:
+            totals[0].append(got[-1])
+        elif line:
+            totals[0][0], near = lax.optimization_barrier((totals[0][0], near))
+        if line:
+            totals[1] = [add(totals[1][0], near), cross]
         new, chunks = [], []
         for p, group in enumerate([totals] if last else [[piece] for piece in totals]):
             cols = n * width * len(group)
@@ -521,7 +526,7 @@
                 chunks.append(everyone(low, "row"))
         xs, y, packed = new, [y], True
         if line:
-            order = [(0, 1), (1, 0), (2, 0), (1, 1), (3, 0), (2, 1), (3, 1)]
+            visits = [(0, 1), (1, 0), (2, 0), (1, 1), (3, 0), (2, 1), (3, 1)]
     move = call(sum_kernel, "moves", shape(low.shape, f32), everyone(low, "row", (1, 2, 3)))
     weight = call(
         weight_kernel, "weight", shape((1, scen), f32), [weight, *everyone(move, "col", (1, 2, 3))]

time: 87.6 us -> 85.4 us (0.975)
  starting transfers between devices: 46.7 us -> 42.9 us
  waiting for transfers between devices: 13.8 us -> 15.1 us
    ppermute x36, starting transfers between devices: 46.7 us -> 42.9 us  [swap(): lax.ppermute(array, axis, [(i, i ^ k) for i in range(lax.axis_size(axis))])]
    ppermute x36, waiting for transfers between devices: 13.8 us -> 15.1 us  [swap(): lax.ppermute(array, axis, [(i, i ^ k) for i in range(lax.axis_size(axis))])]
    pallas_call x43 -> x42, Pallas kernels: 23.5 us -> 23.6 us  [call(): pl.pallas_call(kernel, out_shape=out_shape, in_specs=specs, out_specs=out...]
  transfers between devices with their start and end apart: 36 -> 36, of which waited for: 10 -> 14; matrix products, arithmetic and copies ran while one was open for 2% -> 2% of each run, Pallas kernels for 23% -> 23%
where the time goes in v5:
time: 85.4 us; the launch traced here: 85.2 us
  starting transfers between devices  42.9 us (50%)
  Pallas kernels  23.6 us (28%)
  waiting for transfers between devices  15.1 us (18%)
  local copies, waits for them, and re-layouts  1.9 us (2%)
  between operations  1.75 us (2%)
    ppermute x36, starting transfers between devices, swap(): lax.ppermute(array, axis, [(i, i ^ k) for i in range(lax.axis_size(axis))])  42.9 us
    pallas_call x42, Pallas kernels, call(): pl.pallas_call(kernel, out_shape=out_shape, in_specs=specs, out_specs=out...  23.6 us
    ppermute x36, waiting for transfers between devices, swap(): lax.ppermute(array, axis, [(i, i ^ k) for i in range(lax.axis_size(axis))])  15.1 us
    unnamed x17, local copies, waits for them, and re-layouts  1.9 us
  transfers between devices with their start and end apart: 36, of which 14 were waited for; matrix products, arithmetic and copies ran while one was open for 2% of the time, Pallas kernels for 23%

profile of v5, /device:TPU:0, one launch (start us, length us, event | category | flops | bytes accessed | tf_op | source)
XLA Modules:
  0.0 85.2 jit_solution(12032391842971295229)
XLA Ops:
  0.6 1.2 %start.1 = (bf16[32,2048]{1,0:T(8,128)(2,1)S(1)}, f32[2,32,256]{2,1,0:T(8,128)S(1)}, bf16[512,128,128]{2,1,0:T(8,128)(2,1)S(1)}) custom-call(f32[32,2048]{1,0:T(8,128)} %refs_2_.3, f32[32,256]{1,0:T(8,128)} %y.1, f32[32,256]{1,0:T(8,128)} %rhs.1), custom_call_target="tpu_custom_call" | custom-call | tf_op jit(solution)/shard_map/start/pallas_call | solution.py:32
  1.8 3.1 %collective-permute-start.4 = (bf16[32,2048]{1,0:T(8,128)(2,1)S(1)}, bf16[32,2048]{1,0:T(8,128)(2,1)S(1)}, u32[]{:S(2)}, u32[]{:S(2)}) collective-permute-start(bf16[32,2048]{1,0:T(8,128)(2,1)S(1)} %get-tuple-element.44.x), channel_id=1, source_target_pairs={{0,4},{4,0},{8,12},{12,8},{1,5},{5,1},{9,13},{13,9},{2,6},{6,2},{1... | collective-permute-start | bytes 393224 | tf_op jit(solution)/shard_map/ppermute | solution.py:46
  4.9 2.6 %collective-permute-start.3 = (bf16[32,2048]{1,0:T(8,128)(2,1)S(1)}, bf16[32,2048]{1,0:T(8,128)(2,1)S(1)}, u32[]{:S(2)}, u32[]{:S(2)}) collective-permute-start(bf16[32,2048]{1,0:T(8,128)(2,1)S(1)} %get-tuple-element.44.x), channel_id=1, source_target_pairs={{0,8},{4,12},{8,0},{12,4},{1,9},{5,13},{9,1},{13,5},{2,10},{6,14},... | collective-permute-start | bytes 393224 | tf_op jit(solution)/shard_map/ppermute | solution.py:46
  7.5 1.7 %collective-permute-start.1 = (f32[2,32,256]{2,1,0:T(8,128)S(1)}, f32[2,32,256]{2,1,0:T(8,128)S(1)}, u32[]{:S(2)}, u32[]{:S(2)}) collective-permute-start(f32[2,32,256]{2,1,0:T(8,128)S(1)} %get-tuple-element.45.refs_4_), channel_id=1, source_target_pairs={{0,2},{1,3},{2,0},{3,1},{4,6},{5,7},{6,4},{7,5},{8,10},{9,11},{10,... | collective-permute-start | bytes 196616 | tf_op jit(solution)/shard_map/ppermute | solution.py:46
  9.8 3.7 %densify.1.k = bf16[512,128,128]{2,1,0:T(8,128)(2,1)S(1)} custom-call(s32[1,1]{1,0:T(1,128)S(6)} %copy.21.count, s32[1,1,256]{2,1,0:T(1,128)} %rows_in.1, s32[1,1,256]{2,1,0:T(1,128)} %cols_in.1, bf16[256,128,128]{2,1,0:T(8,128)(2,1)} %bitcast.23, bf16[512,128,128]{2,1,0:T(8,128)(2,1)S(1)} %get-tuple-element.41._), custom_call_target="tpu_custom_call", output_to_operand_aliasing={{}: (4, {})} | custom-call | bytes 33554432 | tf_op jit(solution)/shard_map/densify/pallas_call | solution.py:32
  14.1 1.3 %forward.12.refs_0_ = f32[32,1024]{1,0:T(8,128)S(1)} custom-call(bf16[512,128,128]{2,1,0:T(8,128)(2,1)S(1)} %densify.1.k, bf16[32,2048]{1,0:T(8,128)(2,1)S(1)} %get-tuple-element.44.x), custom_call_target="tpu_custom_call" | custom-call | flops 134217728 | bytes 4194304 | tf_op jit(solution)/shard_map/forward/pallas_call | solution.py:32
  15.4 1.3 %forward.13.refs_0_ = f32[32,1024]{1,0:T(8,128)S(1)} custom-call(bf16[512,128,128]{2,1,0:T(8,128)(2,1)S(1)} %densify.1.k, bf16[32,2048]{1,0:T(8,128)(2,1)S(1)} %collective-permute-done.4.x, f32[32,1024]{1,0:T(8,128)S(1)} %forward.12.refs_0_), custom_call_target="tpu_custom_call" | custom-call | flops 134217728 | bytes 4194304 | tf_op jit(solution)/shard_map/forward/pallas_call | solution.py:32
  17.8 1.3 %forward.14.refs_0_ = f32[32,1024]{1,0:T(8,128)S(1)} custom-call(bf16[512,128,128]{2,1,0:T(8,128)(2,1)S(1)} %densify.1.k, bf16[32,2048]{1,0:T(8,128)(2,1)S(1)} %collective-permute-done.3.x, f32[32,1024]{1,0:T(8,128)S(1)} %forward.13.refs_0_), custom_call_target="tpu_custom_call" | custom-call | flops 134217728 | bytes 4194304 | tf_op jit(solution)/shard_map/forward/pallas_call | solution.py:32
  19.1 1.3 %forward.15.refs_0_ = bf16[32,1024]{1,0:T(8,128)(2,1)S(1)} custom-call(bf16[512,128,128]{2,1,0:T(8,128)(2,1)S(1)} %densify.1.k, bf16[32,2048]{1,0:T(8,128)(2,1)S(1)} %collective-permute-done.2.x, f32[32,1024]{1,0:T(8,128)S(1)} %forward.14.refs_0_), custom_call_target="tpu_custom_call" | custom-call | flops 134217728 | bytes 4194304 | tf_op jit(solution)/shard_map/forward/pallas_call | solution.py:32
  20.6 1.6 %collective-permute-start.6 = (bf16[32,1024]{1,0:T(8,128)(2,1)S(1)}, bf16[32,1024]{1,0:T(8,128)(2,1)S(1)}, u32[]{:S(2)}, u32[]{:S(2)}) collective-permute-start(bf16[32,1024]{1,0:T(8,128)(2,1)S(1)} %forward.15.refs_0_), channel_id=1, source_target_pairs={{0,2},{1,3},{2,0},{3,1},{4,6},{5,7},{6,4},{7,5},{8,10},{9,11},{10,... | collective-permute-start | bytes 196616 | tf_op jit(solution)/shard_map/ppermute | solution.py:46
  22.4 2.5 %collective-permute-done.7.refs_3_ = bf16[32,1024]{1,0:T(8,128)(2,1)S(1)} collective-permute-done((bf16[32,1024]{1,0:T(8,128)(2,1)S(1)}, bf16[32,1024]{1,0:T(8,128)(2,1)S(1)}, u32[]{:S(2)}, u32[]{:S(2)}) %collective-permute-start.7) | collective-permute-done | bytes 65568 | tf_op jit(solution)/shard_map/ppermute | solution.py:46
  24.9 1.4 %collective-permute-done.6.refs_2_ = bf16[32,1024]{1,0:T(8,128)(2,1)S(1)} collective-permute-done((bf16[32,1024]{1,0:T(8,128)(2,1)S(1)}, bf16[32,1024]{1,0:T(8,128)(2,1)S(1)}, u32[]{:S(2)}, u32[]{:S(2)}) %collective-permute-start.6) | collective-permute-done | bytes 65568 | tf_op jit(solution)/shard_map/ppermute | solution.py:46
  27.9 3.8 %collective-permute-start.10 = (bf16[32,1024]{1,0:T(8,128)(2,1)S(1)}, bf16[32,1024]{1,0:T(8,128)(2,1)S(1)}, u32[]{:S(2)}, u32[]{:S(2)}) collective-permute-start(bf16[32,1024]{1,0:T(8,128)(2,1)S(1)} %get-tuple-element.54), channel_id=1, source_target_pairs={{0,8},{4,12},{8,0},{12,4},{1,9},{5,13},{9,1},{13,5},{2,10},{6,14},... | collective-permute-start | bytes 196616 | tf_op jit(solution)/shard_map/ppermute | solution.py:46
  33.6 1.5 %collective-permute-start.13 = (bf16[32,1024]{1,0:T(8,128)(2,1)S(1)}, bf16[32,1024]{1,0:T(8,128)(2,1)S(1)}, u32[]{:S(2)}, u32[]{:S(2)}) collective-permute-start(bf16[32,1024]{1,0:T(8,128)(2,1)S(1)} %backward.16), channel_id=1, source_target_pairs={{0,4},{4,0},{8,12},{12,8},{1,5},{5,1},{9,13},{13,9},{2,6},{6,2},{1... | collective-permute-start | bytes 196616 | tf_op jit(solution)/shard_map/ppermute | solution.py:46
  35.6 2.4 %collective-permute-start.14 = (bf16[32,1024]{1,0:T(8,128)(2,1)S(1)}, bf16[32,1024]{1,0:T(8,128)(2,1)S(1)}, u32[]{:S(2)}, u32[]{:S(2)}) collective-permute-start(bf16[32,1024]{1,0:T(8,128)(2,1)S(1)} %add.12), channel_id=1, source_target_pairs={{0,8},{4,12},{8,0},{12,4},{1,9},{5,13},{9,1},{13,5},{2,10},{6,14},... | collective-permute-start | bytes 196616 | tf_op jit(solution)/shard_map/ppermute | solution.py:46
  38.9 1.9 %collective-permute-start.17 = (bf16[32,1024]{1,0:T(8,128)(2,1)S(1)}, bf16[32,1024]{1,0:T(8,128)(2,1)S(1)}, u32[]{:S(2)}, u32[]{:S(2)}) collective-permute-start(bf16[32,1024]{1,0:T(8,128)(2,1)S(1)} %get-tuple-element.57.x), channel_id=1, source_target_pairs={{0,8},{4,12},{8,0},{12,4},{1,9},{5,13},{9,1},{13,5},{2,10},{6,14},... | collective-permute-start | bytes 196616 | tf_op jit(solution)/shard_map/ppermute | solution.py:46
  43.3 1.1 %collective-permute-start.19 = (bf16[32,1152]{1,0:T(8,128)(2,1)S(1)}, bf16[32,1152]{1,0:T(8,128)(2,1)S(1)}, u32[]{:S(2)}, u32[]{:S(2)}) collective-permute-start(bf16[32,1152]{1,0:T(8,128)(2,1)S(1)} %get-tuple-element.60.x.refs_1_), channel_id=1, source_target_pairs={{0,4},{4,0},{8,12},{12,8},{1,5},{5,1},{9,13},{13,9},{2,6},{6,2},{1... | collective-permute-start | bytes 221192 | tf_op jit(solution)/shard_map/ppermute | solution.py:46
  44.4 1.8 %collective-permute-start.16 = (bf16[32,1152]{1,0:T(8,128)(2,1)S(1)}, bf16[32,1152]{1,0:T(8,128)(2,1)S(1)}, u32[]{:S(2)}, u32[]{:S(2)}) collective-permute-start(bf16[32,1152]{1,0:T(8,128)(2,1)S(1)} %get-tuple-element.60.x.refs_1_), channel_id=1, source_target_pairs={{0,8},{4,12},{8,0},{12,4},{1,9},{5,13},{9,1},{13,5},{2,10},{6,14},... | collective-permute-start | bytes 221192 | tf_op jit(solution)/shard_map/ppermute | solution.py:46
  46.2 1.2 %collective-permute-start.18 = (bf16[32,1024]{1,0:T(8,128)(2,1)S(1)}, bf16[32,1024]{1,0:T(8,128)(2,1)S(1)}, u32[]{:S(2)}, u32[]{:S(2)}) collective-permute-start(bf16[32,1024]{1,0:T(8,128)(2,1)S(1)} %collective-permute-done.17.x), channel_id=1, source_target_pairs={{0,4},{4,0},{8,12},{12,8},{1,5},{5,1},{9,13},{13,9},{2,6},{6,2},{1... | collective-permute-start | bytes 196616 | tf_op jit(solution)/shard_map/ppermute | solution.py:46
  47.4 1.4 %collective-permute-start.15 = (bf16[32,1152]{1,0:T(8,128)(2,1)S(1)}, bf16[32,1152]{1,0:T(8,128)(2,1)S(1)}, u32[]{:S(2)}, u32[]{:S(2)}) collective-permute-start(bf16[32,1152]{1,0:T(8,128)(2,1)S(1)} %get-tuple-element.60.x.refs_1_), channel_id=1, source_target_pairs={{0,12},{4,8},{8,4},{12,0},{1,13},{5,9},{9,5},{13,1},{2,14},{6,10},... | collective-permute-start | bytes 221192 | tf_op jit(solution)/shard_map/ppermute | solution.py:46
  55.0 1.2 %collective-permute-start.21 = (bf16[32,1152]{1,0:T(8,128)(2,1)S(1)}, bf16[32,1152]{1,0:T(8,128)(2,1)S(1)}, u32[]{:S(2)}, u32[]{:S(2)}) collective-permute-start(bf16[32,1152]{1,0:T(8,128)(2,1)S(1)} %forward.23.refs_0_), channel_id=1, source_target_pairs={{0,1},{1,0},{2,3},{3,2},{4,5},{5,4},{6,7},{7,6},{8,9},{9,8},{10,11... | collective-permute-start | bytes 221192 | tf_op jit(solution)/shard_map/ppermute | solution.py:46
  56.2 2.1 %collective-permute-done.23.refs_3_ = bf16[32,1152]{1,0:T(8,128)(2,1)S(1)} collective-permute-done((bf16[32,1152]{1,0:T(8,128)(2,1)S(1)}, bf16[32,1152]{1,0:T(8,128)(2,1)S(1)}, u32[]{:S(2)}, u32[]{:S(2)}) %collective-permute-start.23) | collective-permute-done | bytes 73760 | tf_op jit(solution)/shard_map/ppermute | solution.py:46
  58.3 1.2 %collective-permute-done.22.refs_2_ = bf16[32,1152]{1,0:T(8,128)(2,1)S(1)} collective-permute-done((bf16[32,1152]{1,0:T(8,128)(2,1)S(1)}, bf16[32,1152]{1,0:T(8,128)(2,1)S(1)}, u32[]{:S(2)}, u32[]{:S(2)}) %collective-permute-start.22) | collective-permute-done | bytes 73760 | tf_op jit(solution)/shard_map/ppermute | solution.py:46
  60.6 2.6 %collective-permute-start.25 = (bf16[32,1024]{1,0:T(8,128)(2,1)S(1)}, bf16[32,1024]{1,0:T(8,128)(2,1)S(1)}, u32[]{:S(2)}, u32[]{:S(2)}) collective-permute-start(bf16[32,1024]{1,0:T(8,128)(2,1)S(1)} %get-tuple-element.69), channel_id=1, source_target_pairs={{0,8},{4,12},{8,0},{12,4},{1,9},{5,13},{9,1},{13,5},{2,10},{6,14},... | collective-permute-start | bytes 196616 | tf_op jit(solution)/shard_map/ppermute | solution.py:46
  64.3 1.7 %collective-permute-start.26 = (bf16[32,1024]{1,0:T(8,128)(2,1)S(1)}, bf16[32,1024]{1,0:T(8,128)(2,1)S(1)}, u32[]{:S(2)}, u32[]{:S(2)}) collective-permute-start(bf16[32,1024]{1,0:T(8,128)(2,1)S(1)} %backward.18), channel_id=1, source_target_pairs={{0,12},{4,8},{8,4},{12,0},{1,13},{5,9},{9,5},{13,1},{2,14},{6,10},... | collective-permute-start | bytes 196616 | tf_op jit(solution)/shard_map/ppermute | solution.py:46
  66.8 1.1 %collective-permute-start.28 = (bf16[32,1024]{1,0:T(8,128)(2,1)S(1)}, bf16[32,1024]{1,0:T(8,128)(2,1)S(1)}, u32[]{:S(2)}, u32[]{:S(2)}) collective-permute-start(bf16[32,1024]{1,0:T(8,128)(2,1)S(1)} %backward.21), channel_id=1, source_target_pairs={{0,4},{4,0},{8,12},{12,8},{1,5},{5,1},{9,13},{13,9},{2,6},{6,2},{1... | collective-permute-start | bytes 196616 | tf_op jit(solution)/shard_map/ppermute | solution.py:46
  68.0 1.7 %collective-permute-start.29 = (bf16[32,1024]{1,0:T(8,128)(2,1)S(1)}, bf16[32,1024]{1,0:T(8,128)(2,1)S(1)}, u32[]{:S(2)}, u32[]{:S(2)}) collective-permute-start(bf16[32,1024]{1,0:T(8,128)(2,1)S(1)} %add.17), channel_id=1, source_target_pairs={{0,8},{4,12},{8,0},{12,4},{1,9},{5,13},{9,1},{13,5},{2,10},{6,14},... | collective-permute-start | bytes 196616 | tf_op jit(solution)/shard_map/ppermute | solution.py:46
  71.8 2.1 %collective-permute-done.29.refs_2_ = bf16[32,1024]{1,0:T(8,128)(2,1)S(1)} collective-permute-done((bf16[32,1024]{1,0:T(8,128)(2,1)S(1)}, bf16[32,1024]{1,0:T(8,128)(2,1)S(1)}, u32[]{:S(2)}, u32[]{:S(2)}) %collective-permute-start.29) | collective-permute-done | bytes 65568 | tf_op jit(solution)/shard_map/ppermute | solution.py:46
  74.3 2.2 %collective-permute-start.32 = (f32[2,32]{1,0:T(2,128)S(1)}, f32[2,32]{1,0:T(2,128)S(1)}, u32[]{:S(2)}, u32[]{:S(2)}) collective-permute-start(f32[2,32]{1,0:T(2,128)S(1)} %get-tuple-element.78.refs_0_), channel_id=1, source_target_pairs={{0,12},{4,8},{8,4},{12,0},{1,13},{5,9},{9,5},{13,1},{2,14},{6,10},... | collective-permute-start | bytes 776 | tf_op jit(solution)/shard_map/ppermute | solution.py:46
  76.4 2.3 %collective-permute-start.30 = (f32[2,32]{1,0:T(2,128)S(1)}, f32[2,32]{1,0:T(2,128)S(1)}, u32[]{:S(2)}, u32[]{:S(2)}) collective-permute-start(f32[2,32]{1,0:T(2,128)S(1)} %get-tuple-element.78.refs_0_), channel_id=1, source_target_pairs={{0,4},{4,0},{8,12},{12,8},{1,5},{5,1},{9,13},{13,9},{2,6},{6,2},{1... | collective-permute-start | bytes 776 | tf_op jit(solution)/shard_map/ppermute | solution.py:46
  79.7 1.2 %collective-permute-done.31.refs_2_ = f32[2,32]{1,0:T(2,128)S(1)} collective-permute-done((f32[2,32]{1,0:T(2,128)S(1)}, f32[2,32]{1,0:T(2,128)S(1)}, u32[]{:S(2)}, u32[]{:S(2)}) %collective-permute-start.31) | collective-permute-done | bytes 288 | tf_op jit(solution)/shard_map/ppermute | solution.py:46
  81.0 1.6 %collective-permute-start.34 = (f32[2,32]{1,0:T(2,128)S(1)}, f32[2,32]{1,0:T(2,128)S(1)}, u32[]{:S(2)}, u32[]{:S(2)}) collective-permute-start(f32[2,32]{1,0:T(2,128)S(1)} %moves.1.refs_0_), channel_id=1, source_target_pairs={{0,2},{1,3},{2,0},{3,1},{4,6},{5,7},{6,4},{7,5},{8,10},{9,11},{10,... | collective-permute-start | bytes 776 | tf_op jit(solution)/shard_map/ppermute | solution.py:46
  (99 shorter events, 24.4 us)
Async XLA Ops:
  1.8 13.6 %collective-permute-start.4 = (bf16[32,2048]{1,0:T(8,128)(2,1)S(1)}, bf16[32,2048]{1,0:T(8,128)(2,1)S(1)}, u32[]{:S(2)}, u32[]{:S(2)}) collective-permute-start(bf16[32,2048]{1,0:T(8,128)(2,1)S(1)} %get-tuple-element.44.x), channel_id=1, source_target_pairs={{0,4},{4,0},{8,12},{12,8},{1,5},{5,1},{9,13},{13,9},{2,6},{6,2},{1... | collective-permute-start | bytes 393224 | tf_op jit(solution)/shard_map/ppermute | solution.py:46
  4.9 12.9 %collective-permute-start.3 = (bf16[32,2048]{1,0:T(8,128)(2,1)S(1)}, bf16[32,2048]{1,0:T(8,128)(2,1)S(1)}, u32[]{:S(2)}, u32[]{:S(2)}) collective-permute-start(bf16[32,2048]{1,0:T(8,128)(2,1)S(1)} %get-tuple-element.44.x), channel_id=1, source_target_pairs={{0,8},{4,12},{8,0},{12,4},{1,9},{5,13},{9,1},{13,5},{2,10},{6,14},... | collective-permute-start | bytes 393224 | tf_op jit(solution)/shard_map/ppermute | solution.py:46
  7.5 11.7 %collective-permute-start.2 = (bf16[32,2048]{1,0:T(8,128)(2,1)S(1)}, bf16[32,2048]{1,0:T(8,128)(2,1)S(1)}, u32[]{:S(2)}, u32[]{:S(2)}) collective-permute-start(bf16[32,2048]{1,0:T(8,128)(2,1)S(1)} %get-tuple-element.44.x), channel_id=1, source_target_pairs={{0,12},{4,8},{8,4},{12,0},{1,13},{5,9},{9,5},{13,1},{2,14},{6,10},... | collective-permute-start | bytes 393224 | tf_op jit(solution)/shard_map/ppermute | solution.py:46
  7.5 6.1 %collective-permute-start.1 = (f32[2,32,256]{2,1,0:T(8,128)S(1)}, f32[2,32,256]{2,1,0:T(8,128)S(1)}, u32[]{:S(2)}, u32[]{:S(2)}) collective-permute-start(f32[2,32,256]{2,1,0:T(8,128)S(1)} %get-tuple-element.45.refs_4_), channel_id=1, source_target_pairs={{0,2},{1,3},{2,0},{3,1},{4,6},{5,7},{6,4},{7,5},{8,10},{9,11},{10,... | collective-permute-start | bytes 196616 | tf_op jit(solution)/shard_map/ppermute | solution.py:46
  9.2 4.4 %collective-permute-start = (f32[2,32,256]{2,1,0:T(8,128)S(1)}, f32[2,32,256]{2,1,0:T(8,128)S(1)}, u32[]{:S(2)}, u32[]{:S(2)}) collective-permute-start(f32[2,32,256]{2,1,0:T(8,128)S(1)} %get-tuple-element.45.refs_4_), channel_id=1, source_target_pairs={{0,1},{1,0},{2,3},{3,2},{4,5},{5,4},{6,7},{7,6},{8,9},{9,8},{10,11... | collective-permute-start | bytes 196616 | tf_op jit(solution)/shard_map/ppermute | solution.py:46
  13.6 8.8 %collective-permute-start.8 = (f32[2,32,256]{2,1,0:T(8,128)S(1)}, f32[2,32,256]{2,1,0:T(8,128)S(1)}, u32[]{:S(2)}, u32[]{:S(2)}) collective-permute-start(f32[2,32,256]{2,1,0:T(8,128)S(1)} %collective-permute-done.1.refs_6_), channel_id=1, source_target_pairs={{0,1},{1,0},{2,3},{3,2},{4,5},{5,4},{6,7},{7,6},{8,9},{9,8},{10,11... | collective-permute-start | bytes 196616 | tf_op jit(solution)/shard_map/ppermute | solution.py:46
  20.5 4.4 %collective-permute-start.7 = (bf16[32,1024]{1,0:T(8,128)(2,1)S(1)}, bf16[32,1024]{1,0:T(8,128)(2,1)S(1)}, u32[]{:S(2)}, u32[]{:S(2)}) collective-permute-start(bf16[32,1024]{1,0:T(8,128)(2,1)S(1)} %forward.15.refs_0_), channel_id=1, source_target_pairs={{0,3},{1,2},{2,1},{3,0},{4,7},{5,6},{6,5},{7,4},{8,11},{9,10},{10,... | collective-permute-start | bytes 196616 | tf_op jit(solution)/shard_map/ppermute | solution.py:46
  20.6 5.8 %collective-permute-start.6 = (bf16[32,1024]{1,0:T(8,128)(2,1)S(1)}, bf16[32,1024]{1,0:T(8,128)(2,1)S(1)}, u32[]{:S(2)}, u32[]{:S(2)}) collective-permute-start(bf16[32,1024]{1,0:T(8,128)(2,1)S(1)} %forward.15.refs_0_), channel_id=1, source_target_pairs={{0,2},{1,3},{2,0},{3,1},{4,6},{5,7},{6,4},{7,5},{8,10},{9,11},{10,... | collective-permute-start | bytes 196616 | tf_op jit(solution)/shard_map/ppermute | solution.py:46
  22.1 4.2 %collective-permute-start.5 = (bf16[32,1024]{1,0:T(8,128)(2,1)S(1)}, bf16[32,1024]{1,0:T(8,128)(2,1)S(1)}, u32[]{:S(2)}, u32[]{:S(2)}) collective-permute-start(bf16[32,1024]{1,0:T(8,128)(2,1)S(1)} %forward.15.refs_0_), channel_id=1, source_target_pairs={{0,1},{1,0},{2,3},{3,2},{4,5},{5,4},{6,7},{7,6},{8,9},{9,8},{10,11... | collective-permute-start | bytes 196616 | tf_op jit(solution)/shard_map/ppermute | solution.py:46
  27.2 8.4 %collective-permute-start.9 = (bf16[32,1024]{1,0:T(8,128)(2,1)S(1)}, bf16[32,1024]{1,0:T(8,128)(2,1)S(1)}, u32[]{:S(2)}, u32[]{:S(2)}) collective-permute-start(bf16[32,1024]{1,0:T(8,128)(2,1)S(1)} %get-tuple-element.53), channel_id=1, source_target_pairs={{0,4},{4,0},{8,12},{12,8},{1,5},{5,1},{9,13},{13,9},{2,6},{6,2},{1... | collective-permute-start | bytes 196616 | tf_op jit(solution)/shard_map/ppermute | solution.py:46
  27.9 7.7 %collective-permute-start.10 = (bf16[32,1024]{1,0:T(8,128)(2,1)S(1)}, bf16[32,1024]{1,0:T(8,128)(2,1)S(1)}, u32[]{:S(2)}, u32[]{:S(2)}) collective-permute-start(bf16[32,1024]{1,0:T(8,128)(2,1)S(1)} %get-tuple-element.54), channel_id=1, source_target_pairs={{0,8},{4,12},{8,0},{12,4},{1,9},{5,13},{9,1},{13,5},{2,10},{6,14},... | collective-permute-start | bytes 196616 | tf_op jit(solution)/shard_map/ppermute | solution.py:46
  32.1 6.6 %collective-permute-start.11 = (bf16[32,1024]{1,0:T(8,128)(2,1)S(1)}, bf16[32,1024]{1,0:T(8,128)(2,1)S(1)}, u32[]{:S(2)}, u32[]{:S(2)}) collective-permute-start(bf16[32,1024]{1,0:T(8,128)(2,1)S(1)} %backward.12), channel_id=1, source_target_pairs={{0,12},{4,8},{8,4},{12,0},{1,13},{5,9},{9,5},{13,1},{2,14},{6,10},... | collective-permute-start | bytes 196616 | tf_op jit(solution)/shard_map/ppermute | solution.py:46
  32.6 6.1 %collective-permute-start.12 = (bf16[32,1024]{1,0:T(8,128)(2,1)S(1)}, bf16[32,1024]{1,0:T(8,128)(2,1)S(1)}, u32[]{:S(2)}, u32[]{:S(2)}) collective-permute-start(bf16[32,1024]{1,0:T(8,128)(2,1)S(1)} %backward.13), channel_id=1, source_target_pairs={{0,4},{4,0},{8,12},{12,8},{1,5},{5,1},{9,13},{13,9},{2,6},{6,2},{1... | collective-permute-start | bytes 196616 | tf_op jit(solution)/shard_map/ppermute | solution.py:46
  33.6 8.4 %collective-permute-start.13 = (bf16[32,1024]{1,0:T(8,128)(2,1)S(1)}, bf16[32,1024]{1,0:T(8,128)(2,1)S(1)}, u32[]{:S(2)}, u32[]{:S(2)}) collective-permute-start(bf16[32,1024]{1,0:T(8,128)(2,1)S(1)} %backward.16), channel_id=1, source_target_pairs={{0,4},{4,0},{8,12},{12,8},{1,5},{5,1},{9,13},{13,9},{2,6},{6,2},{1... | collective-permute-start | bytes 196616 | tf_op jit(solution)/shard_map/ppermute | solution.py:46
  35.6 7.4 %collective-permute-start.14 = (bf16[32,1024]{1,0:T(8,128)(2,1)S(1)}, bf16[32,1024]{1,0:T(8,128)(2,1)S(1)}, u32[]{:S(2)}, u32[]{:S(2)}) collective-permute-start(bf16[32,1024]{1,0:T(8,128)(2,1)S(1)} %add.12), channel_id=1, source_target_pairs={{0,8},{4,12},{8,0},{12,4},{1,9},{5,13},{9,1},{13,5},{2,10},{6,14},... | collective-permute-start | bytes 196616 | tf_op jit(solution)/shard_map/ppermute | solution.py:46
  38.9 7.3 %collective-permute-start.17 = (bf16[32,1024]{1,0:T(8,128)(2,1)S(1)}, bf16[32,1024]{1,0:T(8,128)(2,1)S(1)}, u32[]{:S(2)}, u32[]{:S(2)}) collective-permute-start(bf16[32,1024]{1,0:T(8,128)(2,1)S(1)} %get-tuple-element.57.x), channel_id=1, source_target_pairs={{0,8},{4,12},{8,0},{12,4},{1,9},{5,13},{9,1},{13,5},{2,10},{6,14},... | collective-permute-start | bytes 196616 | tf_op jit(solution)/shard_map/ppermute | solution.py:46
  41.2 8.3 %collective-permute-start.20 = (bf16[32,1024]{1,0:T(8,128)(2,1)S(1)}, bf16[32,1024]{1,0:T(8,128)(2,1)S(1)}, u32[]{:S(2)}, u32[]{:S(2)}) collective-permute-start(bf16[32,1024]{1,0:T(8,128)(2,1)S(1)} %get-tuple-element.57.x), channel_id=1, source_target_pairs={{0,4},{4,0},{8,12},{12,8},{1,5},{5,1},{9,13},{13,9},{2,6},{6,2},{1... | collective-permute-start | bytes 196616 | tf_op jit(solution)/shard_map/ppermute | solution.py:46
  43.3 7.7 %collective-permute-start.19 = (bf16[32,1152]{1,0:T(8,128)(2,1)S(1)}, bf16[32,1152]{1,0:T(8,128)(2,1)S(1)}, u32[]{:S(2)}, u32[]{:S(2)}) collective-permute-start(bf16[32,1152]{1,0:T(8,128)(2,1)S(1)} %get-tuple-element.60.x.refs_1_), channel_id=1, source_target_pairs={{0,4},{4,0},{8,12},{12,8},{1,5},{5,1},{9,13},{13,9},{2,6},{6,2},{1... | collective-permute-start | bytes 221192 | tf_op jit(solution)/shard_map/ppermute | solution.py:46
  44.4 8.1 %collective-permute-start.16 = (bf16[32,1152]{1,0:T(8,128)(2,1)S(1)}, bf16[32,1152]{1,0:T(8,128)(2,1)S(1)}, u32[]{:S(2)}, u32[]{:S(2)}) collective-permute-start(bf16[32,1152]{1,0:T(8,128)(2,1)S(1)} %get-tuple-element.60.x.refs_1_), channel_id=1, source_target_pairs={{0,8},{4,12},{8,0},{12,4},{1,9},{5,13},{9,1},{13,5},{2,10},{6,14},... | collective-permute-start | bytes 221192 | tf_op jit(solution)/shard_map/ppermute | solution.py:46
  46.2 5.5 %collective-permute-start.18 = (bf16[32,1024]{1,0:T(8,128)(2,1)S(1)}, bf16[32,1024]{1,0:T(8,128)(2,1)S(1)}, u32[]{:S(2)}, u32[]{:S(2)}) collective-permute-start(bf16[32,1024]{1,0:T(8,128)(2,1)S(1)} %collective-permute-done.17.x), channel_id=1, source_target_pairs={{0,4},{4,0},{8,12},{12,8},{1,5},{5,1},{9,13},{13,9},{2,6},{6,2},{1... | collective-permute-start | bytes 196616 | tf_op jit(solution)/shard_map/ppermute | solution.py:46
  47.4 6.2 %collective-permute-start.15 = (bf16[32,1152]{1,0:T(8,128)(2,1)S(1)}, bf16[32,1152]{1,0:T(8,128)(2,1)S(1)}, u32[]{:S(2)}, u32[]{:S(2)}) collective-permute-start(bf16[32,1152]{1,0:T(8,128)(2,1)S(1)} %get-tuple-element.60.x.refs_1_), channel_id=1, source_target_pairs={{0,12},{4,8},{8,4},{12,0},{1,13},{5,9},{9,5},{13,1},{2,14},{6,10},... | collective-permute-start | bytes 221192 | tf_op jit(solution)/shard_map/ppermute | solution.py:46
  54.4 5.2 %collective-permute-start.22 = (bf16[32,1152]{1,0:T(8,128)(2,1)S(1)}, bf16[32,1152]{1,0:T(8,128)(2,1)S(1)}, u32[]{:S(2)}, u32[]{:S(2)}) collective-permute-start(bf16[32,1152]{1,0:T(8,128)(2,1)S(1)} %forward.23.refs_0_), channel_id=1, source_target_pairs={{0,2},{1,3},{2,0},{3,1},{4,6},{5,7},{6,4},{7,5},{8,10},{9,11},{10,... | collective-permute-start | bytes 221192 | tf_op jit(solution)/shard_map/ppermute | solution.py:46
  55.0 4.5 %collective-permute-start.21 = (bf16[32,1152]{1,0:T(8,128)(2,1)S(1)}, bf16[32,1152]{1,0:T(8,128)(2,1)S(1)}, u32[]{:S(2)}, u32[]{:S(2)}) collective-permute-start(bf16[32,1152]{1,0:T(8,128)(2,1)S(1)} %forward.23.refs_0_), channel_id=1, source_target_pairs={{0,1},{1,0},{2,3},{3,2},{4,5},{5,4},{6,7},{7,6},{8,9},{9,8},{10,11... | collective-permute-start | bytes 221192 | tf_op jit(solution)/shard_map/ppermute | solution.py:46
  60.6 7.4 %collective-permute-start.24 = (bf16[32,1024]{1,0:T(8,128)(2,1)S(1)}, bf16[32,1024]{1,0:T(8,128)(2,1)S(1)}, u32[]{:S(2)}, u32[]{:S(2)}) collective-permute-start(bf16[32,1024]{1,0:T(8,128)(2,1)S(1)} %get-tuple-element.68), channel_id=1, source_target_pairs={{0,4},{4,0},{8,12},{12,8},{1,5},{5,1},{9,13},{13,9},{2,6},{6,2},{1... | collective-permute-start | bytes 196616 | tf_op jit(solution)/shard_map/ppermute | solution.py:46
  60.6 7.3 %collective-permute-start.25 = (bf16[32,1024]{1,0:T(8,128)(2,1)S(1)}, bf16[32,1024]{1,0:T(8,128)(2,1)S(1)}, u32[]{:S(2)}, u32[]{:S(2)}) collective-permute-start(bf16[32,1024]{1,0:T(8,128)(2,1)S(1)} %get-tuple-element.69), channel_id=1, source_target_pairs={{0,8},{4,12},{8,0},{12,4},{1,9},{5,13},{9,1},{13,5},{2,10},{6,14},... | collective-permute-start | bytes 196616 | tf_op jit(solution)/shard_map/ppermute | solution.py:46
  64.1 7.1 %collective-permute-start.27 = (bf16[32,1024]{1,0:T(8,128)(2,1)S(1)}, bf16[32,1024]{1,0:T(8,128)(2,1)S(1)}, u32[]{:S(2)}, u32[]{:S(2)}) collective-permute-start(bf16[32,1024]{1,0:T(8,128)(2,1)S(1)} %backward.19), channel_id=1, source_target_pairs={{0,4},{4,0},{8,12},{12,8},{1,5},{5,1},{9,13},{13,9},{2,6},{6,2},{1... | collective-permute-start | bytes 196616 | tf_op jit(solution)/shard_map/ppermute | solution.py:46
  64.3 6.9 %collective-permute-start.26 = (bf16[32,1024]{1,0:T(8,128)(2,1)S(1)}, bf16[32,1024]{1,0:T(8,128)(2,1)S(1)}, u32[]{:S(2)}, u32[]{:S(2)}) collective-permute-start(bf16[32,1024]{1,0:T(8,128)(2,1)S(1)} %backward.18), channel_id=1, source_target_pairs={{0,12},{4,8},{8,4},{12,0},{1,13},{5,9},{9,5},{13,1},{2,14},{6,10},... | collective-permute-start | bytes 196616 | tf_op jit(solution)/shard_map/ppermute | solution.py:46
  66.8 5.0 %collective-permute-start.28 = (bf16[32,1024]{1,0:T(8,128)(2,1)S(1)}, bf16[32,1024]{1,0:T(8,128)(2,1)S(1)}, u32[]{:S(2)}, u32[]{:S(2)}) collective-permute-start(bf16[32,1024]{1,0:T(8,128)(2,1)S(1)} %backward.21), channel_id=1, source_target_pairs={{0,4},{4,0},{8,12},{12,8},{1,5},{5,1},{9,13},{13,9},{2,6},{6,2},{1... | collective-permute-start | bytes 196616 | tf_op jit(solution)/shard_map/ppermute | solution.py:46
  68.0 5.9 %collective-permute-start.29 = (bf16[32,1024]{1,0:T(8,128)(2,1)S(1)}, bf16[32,1024]{1,0:T(8,128)(2,1)S(1)}, u32[]{:S(2)}, u32[]{:S(2)}) collective-permute-start(bf16[32,1024]{1,0:T(8,128)(2,1)S(1)} %add.17), channel_id=1, source_target_pairs={{0,8},{4,12},{8,0},{12,4},{1,9},{5,13},{9,1},{13,5},{2,10},{6,14},... | collective-permute-start | bytes 196616 | tf_op jit(solution)/shard_map/ppermute | solution.py:46
  74.3 5.4 %collective-permute-start.32 = (f32[2,32]{1,0:T(2,128)S(1)}, f32[2,32]{1,0:T(2,128)S(1)}, u32[]{:S(2)}, u32[]{:S(2)}) collective-permute-start(f32[2,32]{1,0:T(2,128)S(1)} %get-tuple-element.78.refs_0_), channel_id=1, source_target_pairs={{0,12},{4,8},{8,4},{12,0},{1,13},{5,9},{9,5},{13,1},{2,14},{6,10},... | collective-permute-start | bytes 776 | tf_op jit(solution)/shard_map/ppermute | solution.py:46
  76.4 4.5 %collective-permute-start.31 = (f32[2,32]{1,0:T(2,128)S(1)}, f32[2,32]{1,0:T(2,128)S(1)}, u32[]{:S(2)}, u32[]{:S(2)}) collective-permute-start(f32[2,32]{1,0:T(2,128)S(1)} %get-tuple-element.78.refs_0_), channel_id=1, source_target_pairs={{0,8},{4,12},{8,0},{12,4},{1,9},{5,13},{9,1},{13,5},{2,10},{6,14},... | collective-permute-start | bytes 776 | tf_op jit(solution)/shard_map/ppermute | solution.py:46
  76.4 4.5 %collective-permute-start.30 = (f32[2,32]{1,0:T(2,128)S(1)}, f32[2,32]{1,0:T(2,128)S(1)}, u32[]{:S(2)}, u32[]{:S(2)}) collective-permute-start(f32[2,32]{1,0:T(2,128)S(1)} %get-tuple-element.78.refs_0_), channel_id=1, source_target_pairs={{0,4},{4,0},{8,12},{12,8},{1,5},{5,1},{9,13},{13,9},{2,6},{6,2},{1... | collective-permute-start | bytes 776 | tf_op jit(solution)/shard_map/ppermute | solution.py:46
  (11 other events, 57.5 us)

commit v6 on v5

--- a/solution.py
+++ b/solution.py
@@ -445,14 +445,13 @@
     dims = (places,) + tiles.shape[1:]
     low, both, k = start(primal_vars, dual_vars, right_side, dims, clean)
     chunks = [everyone(low, "row")]
-    if n_col == 4:
-        both = [both, swap(both, "col", 1), swap(both, "col", 2)]
-    else:
-        both = everyone(both, "col")
+    four = n_col == 4
+    both = [both, swap(both, "col", 2)] if four else everyone(both, "col")
     k = densify(tiles, tile_rows, tile_cols, tile_count, k, clean, rt)
     k, both = lax.optimization_barrier((k, both))
-    if n_col == 4:
-        both.append(swap(both[2], "col", 1))
+    if four:
+        near, cross = [swap(half, "col", 1) for half in both]
+        both = [both[0], near, both[1], cross]
     step = step_size[None]
     weight = primal_weight[None]
     low_bound, high_bound, kind = lower_bound[None], upper_bound[None], bound_kind[None]
@@ -462,6 +461,9 @@
         last = sweep == ITERS - 1
         part = forward_parts(k, chunks, rt, per, per // len(chunks), packed, visits, base)
         order = partners(n_row, (2, 3, 1))
+        parts = everyone(part, "col")
+        if n_col == 4:
+            parts[1], parts[3] = lax.optimization_barrier((parts[1], parts[3]))
         sends = [(3, n), (order[0], 0)] if line else [(order[0], 0)]
         y, bar, moved, weight, *sent = call(
             functools.partial(dual_kernel, rt, per, n_col, packed, len(y), sends),
@@ -473,7 +475,7 @@
                 shape((1, scen), f32),
                 *[shape((scen, n * width), bf16)] * len(sends),
             ],
-            [k, step, weight, *everyone(part, "col", (1, 3, 2)), *both, *y],
+            [k, step, weight, *parts, *both, *y],
             cost=cost(k, n, rt),
         )
         hop = swap(sent[0], "row", 1) if line else None

time: 85.4 us -> 84.9 us (level); the launches traced: 85.2 us -> 83.7 us
  starting transfers between devices: 42.9 us -> 41.2 us
    ppermute x36, starting transfers between devices: 42.9 us -> 41.2 us  [swap(): lax.ppermute(array, axis, [(i, i ^ k) for i in range(lax.axis_size(axis))])]
  transfers between devices with their start and end apart: 36 -> 36, of which waited for: 14 -> 15; matrix products, arithmetic and copies ran while one was open for 2% -> 2% of each run, Pallas kernels for 23% -> 22%
where the time goes in v6:
time: 84.9 us; the launch traced here: 83.7 us
  starting transfers between devices  41.2 us (49%)
  Pallas kernels  23.4 us (28%)
  waiting for transfers between devices  15.4 us (18%)
  local copies, waits for them, and re-layouts  1.9 us (2%)
  between operations  1.7 us (2%)
    ppermute x36, starting transfers between devices, swap(): lax.ppermute(array, axis, [(i, i ^ k) for i in range(lax.axis_size(axis))])  41.2 us
    pallas_call x42, Pallas kernels, call(): pl.pallas_call(kernel, out_shape=out_shape, in_specs=specs, out_specs=out...  23.4 us
    ppermute x36, waiting for transfers between devices, swap(): lax.ppermute(array, axis, [(i, i ^ k) for i in range(lax.axis_size(axis))])  15.4 us
    unnamed x17, local copies, waits for them, and re-layouts  1.9 us
  transfers between devices with their start and end apart: 36, of which 15 were waited for; matrix products, arithmetic and copies ran while one was open for 2% of the time, Pallas kernels for 22%

profile of v6, /device:TPU:0, one launch (start us, length us, event | category | flops | bytes accessed | tf_op | source)
XLA Modules:
  0.0 83.7 jit_solution(17042789937408817266)
XLA Ops:
  0.6 1.2 %start.1 = (bf16[32,2048]{1,0:T(8,128)(2,1)S(1)}, f32[2,32,256]{2,1,0:T(8,128)S(1)}, bf16[512,128,128]{2,1,0:T(8,128)(2,1)S(1)}) custom-call(f32[32,2048]{1,0:T(8,128)} %refs_2_.3, f32[32,256]{1,0:T(8,128)} %y.1, f32[32,256]{1,0:T(8,128)} %rhs.1), custom_call_target="tpu_custom_call" | custom-call | tf_op jit(solution)/shard_map/start/pallas_call | solution.py:32
  1.8 3.1 %collective-permute-start.3 = (bf16[32,2048]{1,0:T(8,128)(2,1)S(1)}, bf16[32,2048]{1,0:T(8,128)(2,1)S(1)}, u32[]{:S(2)}, u32[]{:S(2)}) collective-permute-start(bf16[32,2048]{1,0:T(8,128)(2,1)S(1)} %get-tuple-element.47.x), channel_id=1, source_target_pairs={{0,4},{4,0},{8,12},{12,8},{1,5},{5,1},{9,13},{13,9},{2,6},{6,2},{1... | collective-permute-start | bytes 393224 | tf_op jit(solution)/shard_map/ppermute | solution.py:46
  4.9 2.6 %collective-permute-start.2 = (bf16[32,2048]{1,0:T(8,128)(2,1)S(1)}, bf16[32,2048]{1,0:T(8,128)(2,1)S(1)}, u32[]{:S(2)}, u32[]{:S(2)}) collective-permute-start(bf16[32,2048]{1,0:T(8,128)(2,1)S(1)} %get-tuple-element.47.x), channel_id=1, source_target_pairs={{0,8},{4,12},{8,0},{12,4},{1,9},{5,13},{9,1},{13,5},{2,10},{6,14},... | collective-permute-start | bytes 393224 | tf_op jit(solution)/shard_map/ppermute | solution.py:46
  7.5 1.7 %collective-permute-start = (f32[2,32,256]{2,1,0:T(8,128)S(1)}, f32[2,32,256]{2,1,0:T(8,128)S(1)}, u32[]{:S(2)}, u32[]{:S(2)}) collective-permute-start(f32[2,32,256]{2,1,0:T(8,128)S(1)} %get-tuple-element.50.refs_4_), channel_id=1, source_target_pairs={{0,2},{1,3},{2,0},{3,1},{4,6},{5,7},{6,4},{7,5},{8,10},{9,11},{10,... | collective-permute-start | bytes 196616 | tf_op jit(solution)/shard_map/ppermute | solution.py:46
  9.8 3.6 %densify.1.k = bf16[512,128,128]{2,1,0:T(8,128)(2,1)S(1)} custom-call(s32[1,1]{1,0:T(1,128)S(6)} %copy.21.count, s32[1,1,256]{2,1,0:T(1,128)} %rows_in.1, s32[1,1,256]{2,1,0:T(1,128)} %cols_in.1, bf16[256,128,128]{2,1,0:T(8,128)(2,1)} %bitcast.23, bf16[512,128,128]{2,1,0:T(8,128)(2,1)S(1)} %get-tuple-element.44._), custom_call_target="tpu_custom_call", output_to_operand_aliasing={{}: (4, {})} | custom-call | bytes 33554432 | tf_op jit(solution)/shard_map/densify/pallas_call | solution.py:32
  13.4 1.3 %forward.12.refs_0_ = f32[32,1024]{1,0:T(8,128)S(1)} custom-call(bf16[512,128,128]{2,1,0:T(8,128)(2,1)S(1)} %densify.1.k, bf16[32,2048]{1,0:T(8,128)(2,1)S(1)} %get-tuple-element.47.x), custom_call_target="tpu_custom_call" | custom-call | flops 134217728 | bytes 4194304 | tf_op jit(solution)/shard_map/forward/pallas_call | solution.py:32
  14.8 1.3 %forward.13.refs_0_ = f32[32,1024]{1,0:T(8,128)S(1)} custom-call(bf16[512,128,128]{2,1,0:T(8,128)(2,1)S(1)} %densify.1.k, bf16[32,2048]{1,0:T(8,128)(2,1)S(1)} %collective-permute-done.3.x, f32[32,1024]{1,0:T(8,128)S(1)} %forward.12.refs_0_), custom_call_target="tpu_custom_call" | custom-call | flops 134217728 | bytes 4194304 | tf_op jit(solution)/shard_map/forward/pallas_call | solution.py:32
  16.1 1.7 %collective-permute-done.2.x = bf16[32,2048]{1,0:T(8,128)(2,1)S(1)} collective-permute-done((bf16[32,2048]{1,0:T(8,128)(2,1)S(1)}, bf16[32,2048]{1,0:T(8,128)(2,1)S(1)}, u32[]{:S(2)}, u32[]{:S(2)}) %collective-permute-start.2) | collective-permute-done | bytes 131104 | tf_op jit(solution)/shard_map/ppermute | solution.py:46
  17.8 1.3 %forward.14.refs_0_ = f32[32,1024]{1,0:T(8,128)S(1)} custom-call(bf16[512,128,128]{2,1,0:T(8,128)(2,1)S(1)} %densify.1.k, bf16[32,2048]{1,0:T(8,128)(2,1)S(1)} %collective-permute-done.2.x, f32[32,1024]{1,0:T(8,128)S(1)} %forward.13.refs_0_), custom_call_target="tpu_custom_call" | custom-call | flops 134217728 | bytes 4194304 | tf_op jit(solution)/shard_map/forward/pallas_call | solution.py:32
  19.1 1.3 %forward.15.refs_0_ = bf16[32,1024]{1,0:T(8,128)(2,1)S(1)} custom-call(bf16[512,128,128]{2,1,0:T(8,128)(2,1)S(1)} %densify.1.k, bf16[32,2048]{1,0:T(8,128)(2,1)S(1)} %collective-permute-done.1.x, f32[32,1024]{1,0:T(8,128)S(1)} %forward.14.refs_0_), custom_call_target="tpu_custom_call" | custom-call | flops 134217728 | bytes 4194304 | tf_op jit(solution)/shard_map/forward/pallas_call | solution.py:32
  20.6 1.6 %collective-permute-start.4 = (bf16[32,1024]{1,0:T(8,128)(2,1)S(1)}, bf16[32,1024]{1,0:T(8,128)(2,1)S(1)}, u32[]{:S(2)}, u32[]{:S(2)}) collective-permute-start(bf16[32,1024]{1,0:T(8,128)(2,1)S(1)} %forward.15.refs_0_), channel_id=1, source_target_pairs={{0,1},{1,0},{2,3},{3,2},{4,5},{5,4},{6,7},{7,6},{8,9},{9,8},{10,11... | collective-permute-start | bytes 196616 | tf_op jit(solution)/shard_map/ppermute | solution.py:46
  23.2 1.7 %collective-permute-done.5.refs_3_ = bf16[32,1024]{1,0:T(8,128)(2,1)S(1)} collective-permute-done((bf16[32,1024]{1,0:T(8,128)(2,1)S(1)}, bf16[32,1024]{1,0:T(8,128)(2,1)S(1)}, u32[]{:S(2)}, u32[]{:S(2)}) %collective-permute-start.5) | collective-permute-done | bytes 65568 | tf_op jit(solution)/shard_map/ppermute | solution.py:46
  24.9 2.0 %collective-permute-done.6.refs_2_ = bf16[32,1024]{1,0:T(8,128)(2,1)S(1)} collective-permute-done((bf16[32,1024]{1,0:T(8,128)(2,1)S(1)}, bf16[32,1024]{1,0:T(8,128)(2,1)S(1)}, u32[]{:S(2)}, u32[]{:S(2)}) %collective-permute-start.6) | collective-permute-done | bytes 65568 | tf_op jit(solution)/shard_map/ppermute | solution.py:46
  28.4 2.2 %collective-permute-start.10 = (bf16[32,1024]{1,0:T(8,128)(2,1)S(1)}, bf16[32,1024]{1,0:T(8,128)(2,1)S(1)}, u32[]{:S(2)}, u32[]{:S(2)}) collective-permute-start(bf16[32,1024]{1,0:T(8,128)(2,1)S(1)} %get-tuple-element.58), channel_id=1, source_target_pairs={{0,8},{4,12},{8,0},{12,4},{1,9},{5,13},{9,1},{13,5},{2,10},{6,14},... | collective-permute-start | bytes 196616 | tf_op jit(solution)/shard_map/ppermute | solution.py:46
  31.1 1.6 %collective-permute-start.11 = (bf16[32,1024]{1,0:T(8,128)(2,1)S(1)}, bf16[32,1024]{1,0:T(8,128)(2,1)S(1)}, u32[]{:S(2)}, u32[]{:S(2)}) collective-permute-start(bf16[32,1024]{1,0:T(8,128)(2,1)S(1)} %backward.12), channel_id=1, source_target_pairs={{0,12},{4,8},{8,4},{12,0},{1,13},{5,9},{9,5},{13,1},{2,14},{6,10},... | collective-permute-start | bytes 196616 | tf_op jit(solution)/shard_map/ppermute | solution.py:46
  33.6 2.1 %collective-permute-start.13 = (bf16[32,1024]{1,0:T(8,128)(2,1)S(1)}, bf16[32,1024]{1,0:T(8,128)(2,1)S(1)}, u32[]{:S(2)}, u32[]{:S(2)}) collective-permute-start(bf16[32,1024]{1,0:T(8,128)(2,1)S(1)} %backward.16), channel_id=1, source_target_pairs={{0,4},{4,0},{8,12},{12,8},{1,5},{5,1},{9,13},{13,9},{2,6},{6,2},{1... | collective-permute-start | bytes 196616 | tf_op jit(solution)/shard_map/ppermute | solution.py:46
  38.7 1.2 %collective-permute-start.17 = (bf16[32,1024]{1,0:T(8,128)(2,1)S(1)}, bf16[32,1024]{1,0:T(8,128)(2,1)S(1)}, u32[]{:S(2)}, u32[]{:S(2)}) collective-permute-start(bf16[32,1024]{1,0:T(8,128)(2,1)S(1)} %get-tuple-element.61.x), channel_id=1, source_target_pairs={{0,8},{4,12},{8,0},{12,4},{1,9},{5,13},{9,1},{13,5},{2,10},{6,14},... | collective-permute-start | bytes 196616 | tf_op jit(solution)/shard_map/ppermute | solution.py:46
  40.4 1.3 %collective-permute-start.20 = (bf16[32,1024]{1,0:T(8,128)(2,1)S(1)}, bf16[32,1024]{1,0:T(8,128)(2,1)S(1)}, u32[]{:S(2)}, u32[]{:S(2)}) collective-permute-start(bf16[32,1024]{1,0:T(8,128)(2,1)S(1)} %get-tuple-element.61.x), channel_id=1, source_target_pairs={{0,4},{4,0},{8,12},{12,8},{1,5},{5,1},{9,13},{13,9},{2,6},{6,2},{1... | collective-permute-start | bytes 196616 | tf_op jit(solution)/shard_map/ppermute | solution.py:46
  43.6 1.7 %collective-permute-start.16 = (bf16[32,1152]{1,0:T(8,128)(2,1)S(1)}, bf16[32,1152]{1,0:T(8,128)(2,1)S(1)}, u32[]{:S(2)}, u32[]{:S(2)}) collective-permute-start(bf16[32,1152]{1,0:T(8,128)(2,1)S(1)} %get-tuple-element.64.x.refs_1_), channel_id=1, source_target_pairs={{0,8},{4,12},{8,0},{12,4},{1,9},{5,13},{9,1},{13,5},{2,10},{6,14},... | collective-permute-start | bytes 221192 | tf_op jit(solution)/shard_map/ppermute | solution.py:46
  46.4 1.6 %collective-permute-start.15 = (bf16[32,1152]{1,0:T(8,128)(2,1)S(1)}, bf16[32,1152]{1,0:T(8,128)(2,1)S(1)}, u32[]{:S(2)}, u32[]{:S(2)}) collective-permute-start(bf16[32,1152]{1,0:T(8,128)(2,1)S(1)} %get-tuple-element.64.x.refs_1_), channel_id=1, source_target_pairs={{0,12},{4,8},{8,4},{12,0},{1,13},{5,9},{9,5},{13,1},{2,14},{6,10},... | collective-permute-start | bytes 221192 | tf_op jit(solution)/shard_map/ppermute | solution.py:46
  54.0 1.5 %collective-permute-start.23 = (bf16[32,1152]{1,0:T(8,128)(2,1)S(1)}, bf16[32,1152]{1,0:T(8,128)(2,1)S(1)}, u32[]{:S(2)}, u32[]{:S(2)}) collective-permute-start(bf16[32,1152]{1,0:T(8,128)(2,1)S(1)} %forward.23.refs_0_), channel_id=1, source_target_pairs={{0,2},{1,3},{2,0},{3,1},{4,6},{5,7},{6,4},{7,5},{8,10},{9,11},{10,... | collective-permute-start | bytes 221192 | tf_op jit(solution)/shard_map/ppermute | solution.py:46
  55.5 1.6 %collective-permute-done.22.refs_3_ = bf16[32,1152]{1,0:T(8,128)(2,1)S(1)} collective-permute-done((bf16[32,1152]{1,0:T(8,128)(2,1)S(1)}, bf16[32,1152]{1,0:T(8,128)(2,1)S(1)}, u32[]{:S(2)}, u32[]{:S(2)}) %collective-permute-start.22) | collective-permute-done | bytes 73760 | tf_op jit(solution)/shard_map/ppermute | solution.py:46
  57.1 1.6 %collective-permute-done.23.refs_2_ = bf16[32,1152]{1,0:T(8,128)(2,1)S(1)} collective-permute-done((bf16[32,1152]{1,0:T(8,128)(2,1)S(1)}, bf16[32,1152]{1,0:T(8,128)(2,1)S(1)}, u32[]{:S(2)}, u32[]{:S(2)}) %collective-permute-start.23) | collective-permute-done | bytes 73760 | tf_op jit(solution)/shard_map/ppermute | solution.py:46
  58.7 1.0 %dual.3 = (f32[32,256]{1,0:T(8,128)S(1)}, bf16[32,1024]{1,0:T(8,128)(2,1)S(1)}, f32[32,2]{1,0:T(8,128)S(1)}, f32[1,32]{1,0:T(1,128)S(1)}, bf16[32,1024]{1,0:T(8,128)(2,1)S(1)}, /*index=5*/bf16[32,1024]{1,0:T(8,128)(2,1)S(1)}) custom-call(bf16[512,128,128]{2,1,0:T(8,128)(2,1)S(1)} %densify.1.k, f32[1,32]{1,0:T(1,128)S(1)} %bitcast.20, ...), custom_call_target="tpu_custom_call" | custom-call | flops 67108864 | bytes 2097152 | tf_op jit(solution)/shard_map/dual/pallas_call | solution.py:32
  60.6 1.9 %collective-permute-start.25 = (bf16[32,1024]{1,0:T(8,128)(2,1)S(1)}, bf16[32,1024]{1,0:T(8,128)(2,1)S(1)}, u32[]{:S(2)}, u32[]{:S(2)}) collective-permute-start(bf16[32,1024]{1,0:T(8,128)(2,1)S(1)} %get-tuple-element.75), channel_id=1, source_target_pairs={{0,8},{4,12},{8,0},{12,4},{1,9},{5,13},{9,1},{13,5},{2,10},{6,14},... | collective-permute-start | bytes 196616 | tf_op jit(solution)/shard_map/ppermute | solution.py:46
  64.0 1.9 %collective-permute-start.26 = (bf16[32,1024]{1,0:T(8,128)(2,1)S(1)}, bf16[32,1024]{1,0:T(8,128)(2,1)S(1)}, u32[]{:S(2)}, u32[]{:S(2)}) collective-permute-start(bf16[32,1024]{1,0:T(8,128)(2,1)S(1)} %backward.18), channel_id=1, source_target_pairs={{0,12},{4,8},{8,4},{12,0},{1,13},{5,9},{9,5},{13,1},{2,14},{6,10},... | collective-permute-start | bytes 196616 | tf_op jit(solution)/shard_map/ppermute | solution.py:46
  67.2 2.2 %collective-permute-start.29 = (bf16[32,1024]{1,0:T(8,128)(2,1)S(1)}, bf16[32,1024]{1,0:T(8,128)(2,1)S(1)}, u32[]{:S(2)}, u32[]{:S(2)}) collective-permute-start(bf16[32,1024]{1,0:T(8,128)(2,1)S(1)} %add.17), channel_id=1, source_target_pairs={{0,8},{4,12},{8,0},{12,4},{1,9},{5,13},{9,1},{13,5},{2,10},{6,14},... | collective-permute-start | bytes 196616 | tf_op jit(solution)/shard_map/ppermute | solution.py:46
  70.3 1.2 %collective-permute-done.28.part = bf16[32,1024]{1,0:T(8,128)(2,1)S(1)} collective-permute-done((bf16[32,1024]{1,0:T(8,128)(2,1)S(1)}, bf16[32,1024]{1,0:T(8,128)(2,1)S(1)}, u32[]{:S(2)}, u32[]{:S(2)}) %collective-permute-start.28) | collective-permute-done | bytes 65568 | tf_op jit(solution)/shard_map/ppermute | solution.py:46
  72.8 2.2 %collective-permute-start.32 = (f32[2,32]{1,0:T(2,128)S(1)}, f32[2,32]{1,0:T(2,128)S(1)}, u32[]{:S(2)}, u32[]{:S(2)}) collective-permute-start(f32[2,32]{1,0:T(2,128)S(1)} %get-tuple-element.84.refs_0_), channel_id=1, source_target_pairs={{0,12},{4,8},{8,4},{12,0},{1,13},{5,9},{9,5},{13,1},{2,14},{6,10},... | collective-permute-start | bytes 776 | tf_op jit(solution)/shard_map/ppermute | solution.py:46
  76.0 1.3 %collective-permute-start.30 = (f32[2,32]{1,0:T(2,128)S(1)}, f32[2,32]{1,0:T(2,128)S(1)}, u32[]{:S(2)}, u32[]{:S(2)}) collective-permute-start(f32[2,32]{1,0:T(2,128)S(1)} %get-tuple-element.84.refs_0_), channel_id=1, source_target_pairs={{0,4},{4,0},{8,12},{12,8},{1,5},{5,1},{9,13},{13,9},{2,6},{6,2},{1... | collective-permute-start | bytes 776 | tf_op jit(solution)/shard_map/ppermute | solution.py:46
  78.2 1.2 %collective-permute-done.31.refs_2_ = f32[2,32]{1,0:T(2,128)S(1)} collective-permute-done((f32[2,32]{1,0:T(2,128)S(1)}, f32[2,32]{1,0:T(2,128)S(1)}, u32[]{:S(2)}, u32[]{:S(2)}) %collective-permute-start.31) | collective-permute-done | bytes 288 | tf_op jit(solution)/shard_map/ppermute | solution.py:46
  79.6 1.4 %collective-permute-start.34 = (f32[2,32]{1,0:T(2,128)S(1)}, f32[2,32]{1,0:T(2,128)S(1)}, u32[]{:S(2)}, u32[]{:S(2)}) collective-permute-start(f32[2,32]{1,0:T(2,128)S(1)} %moves.1.refs_0_), channel_id=1, source_target_pairs={{0,2},{1,3},{2,0},{3,1},{4,6},{5,7},{6,4},{7,5},{8,10},{9,11},{10,... | collective-permute-start | bytes 776 | tf_op jit(solution)/shard_map/ppermute | solution.py:46
  (99 shorter events, 27.1 us)
Async XLA Ops:
  1.8 12.9 %collective-permute-start.3 = (bf16[32,2048]{1,0:T(8,128)(2,1)S(1)}, bf16[32,2048]{1,0:T(8,128)(2,1)S(1)}, u32[]{:S(2)}, u32[]{:S(2)}) collective-permute-start(bf16[32,2048]{1,0:T(8,128)(2,1)S(1)} %get-tuple-element.47.x), channel_id=1, source_target_pairs={{0,4},{4,0},{8,12},{12,8},{1,5},{5,1},{9,13},{13,9},{2,6},{6,2},{1... | collective-permute-start | bytes 393224 | tf_op jit(solution)/shard_map/ppermute | solution.py:46
  4.9 12.9 %collective-permute-start.2 = (bf16[32,2048]{1,0:T(8,128)(2,1)S(1)}, bf16[32,2048]{1,0:T(8,128)(2,1)S(1)}, u32[]{:S(2)}, u32[]{:S(2)}) collective-permute-start(bf16[32,2048]{1,0:T(8,128)(2,1)S(1)} %get-tuple-element.47.x), channel_id=1, source_target_pairs={{0,8},{4,12},{8,0},{12,4},{1,9},{5,13},{9,1},{13,5},{2,10},{6,14},... | collective-permute-start | bytes 393224 | tf_op jit(solution)/shard_map/ppermute | solution.py:46
  7.5 11.7 %collective-permute-start.1 = (bf16[32,2048]{1,0:T(8,128)(2,1)S(1)}, bf16[32,2048]{1,0:T(8,128)(2,1)S(1)}, u32[]{:S(2)}, u32[]{:S(2)}) collective-permute-start(bf16[32,2048]{1,0:T(8,128)(2,1)S(1)} %get-tuple-element.47.x), channel_id=1, source_target_pairs={{0,12},{4,8},{8,4},{12,0},{1,13},{5,9},{9,5},{13,1},{2,14},{6,10},... | collective-permute-start | bytes 393224 | tf_op jit(solution)/shard_map/ppermute | solution.py:46
  7.5 5.9 %collective-permute-start = (f32[2,32,256]{2,1,0:T(8,128)S(1)}, f32[2,32,256]{2,1,0:T(8,128)S(1)}, u32[]{:S(2)}, u32[]{:S(2)}) collective-permute-start(f32[2,32,256]{2,1,0:T(8,128)S(1)} %get-tuple-element.50.refs_4_), channel_id=1, source_target_pairs={{0,2},{1,3},{2,0},{3,1},{4,6},{5,7},{6,4},{7,5},{8,10},{9,11},{10,... | collective-permute-start | bytes 196616 | tf_op jit(solution)/shard_map/ppermute | solution.py:46
  20.5 4.4 %collective-permute-start.5 = (bf16[32,1024]{1,0:T(8,128)(2,1)S(1)}, bf16[32,1024]{1,0:T(8,128)(2,1)S(1)}, u32[]{:S(2)}, u32[]{:S(2)}) collective-permute-start(bf16[32,1024]{1,0:T(8,128)(2,1)S(1)} %forward.15.refs_0_), channel_id=1, source_target_pairs={{0,3},{1,2},{2,1},{3,0},{4,7},{5,6},{6,5},{7,4},{8,11},{9,10},{10,... | collective-permute-start | bytes 196616 | tf_op jit(solution)/shard_map/ppermute | solution.py:46
  20.6 4.3 %collective-permute-start.4 = (bf16[32,1024]{1,0:T(8,128)(2,1)S(1)}, bf16[32,1024]{1,0:T(8,128)(2,1)S(1)}, u32[]{:S(2)}, u32[]{:S(2)}) collective-permute-start(bf16[32,1024]{1,0:T(8,128)(2,1)S(1)} %forward.15.refs_0_), channel_id=1, source_target_pairs={{0,1},{1,0},{2,3},{3,2},{4,5},{5,4},{6,7},{7,6},{8,9},{9,8},{10,11... | collective-permute-start | bytes 196616 | tf_op jit(solution)/shard_map/ppermute | solution.py:46
  22.7 4.3 %collective-permute-start.6 = (bf16[32,1024]{1,0:T(8,128)(2,1)S(1)}, bf16[32,1024]{1,0:T(8,128)(2,1)S(1)}, u32[]{:S(2)}, u32[]{:S(2)}) collective-permute-start(bf16[32,1024]{1,0:T(8,128)(2,1)S(1)} %forward.15.refs_0_), channel_id=1, source_target_pairs={{0,2},{1,3},{2,0},{3,1},{4,6},{5,7},{6,4},{7,5},{8,10},{9,11},{10,... | collective-permute-start | bytes 196616 | tf_op jit(solution)/shard_map/ppermute | solution.py:46
  27.7 8.4 %collective-permute-start.9 = (bf16[32,1024]{1,0:T(8,128)(2,1)S(1)}, bf16[32,1024]{1,0:T(8,128)(2,1)S(1)}, u32[]{:S(2)}, u32[]{:S(2)}) collective-permute-start(bf16[32,1024]{1,0:T(8,128)(2,1)S(1)} %get-tuple-element.57), channel_id=1, source_target_pairs={{0,4},{4,0},{8,12},{12,8},{1,5},{5,1},{9,13},{13,9},{2,6},{6,2},{1... | collective-permute-start | bytes 196616 | tf_op jit(solution)/shard_map/ppermute | solution.py:46
  28.4 7.7 %collective-permute-start.10 = (bf16[32,1024]{1,0:T(8,128)(2,1)S(1)}, bf16[32,1024]{1,0:T(8,128)(2,1)S(1)}, u32[]{:S(2)}, u32[]{:S(2)}) collective-permute-start(bf16[32,1024]{1,0:T(8,128)(2,1)S(1)} %get-tuple-element.58), channel_id=1, source_target_pairs={{0,8},{4,12},{8,0},{12,4},{1,9},{5,13},{9,1},{13,5},{2,10},{6,14},... | collective-permute-start | bytes 196616 | tf_op jit(solution)/shard_map/ppermute | solution.py:46
  31.1 6.9 %collective-permute-start.11 = (bf16[32,1024]{1,0:T(8,128)(2,1)S(1)}, bf16[32,1024]{1,0:T(8,128)(2,1)S(1)}, u32[]{:S(2)}, u32[]{:S(2)}) collective-permute-start(bf16[32,1024]{1,0:T(8,128)(2,1)S(1)} %backward.12), channel_id=1, source_target_pairs={{0,12},{4,8},{8,4},{12,0},{1,13},{5,9},{9,5},{13,1},{2,14},{6,10},... | collective-permute-start | bytes 196616 | tf_op jit(solution)/shard_map/ppermute | solution.py:46
  33.1 5.4 %collective-permute-start.12 = (bf16[32,1024]{1,0:T(8,128)(2,1)S(1)}, bf16[32,1024]{1,0:T(8,128)(2,1)S(1)}, u32[]{:S(2)}, u32[]{:S(2)}) collective-permute-start(bf16[32,1024]{1,0:T(8,128)(2,1)S(1)} %backward.13), channel_id=1, source_target_pairs={{0,4},{4,0},{8,12},{12,8},{1,5},{5,1},{9,13},{13,9},{2,6},{6,2},{1... | collective-permute-start | bytes 196616 | tf_op jit(solution)/shard_map/ppermute | solution.py:46
  33.6 8.0 %collective-permute-start.13 = (bf16[32,1024]{1,0:T(8,128)(2,1)S(1)}, bf16[32,1024]{1,0:T(8,128)(2,1)S(1)}, u32[]{:S(2)}, u32[]{:S(2)}) collective-permute-start(bf16[32,1024]{1,0:T(8,128)(2,1)S(1)} %backward.16), channel_id=1, source_target_pairs={{0,4},{4,0},{8,12},{12,8},{1,5},{5,1},{9,13},{13,9},{2,6},{6,2},{1... | collective-permute-start | bytes 196616 | tf_op jit(solution)/shard_map/ppermute | solution.py:46
  36.2 6.3 %collective-permute-start.14 = (bf16[32,1024]{1,0:T(8,128)(2,1)S(1)}, bf16[32,1024]{1,0:T(8,128)(2,1)S(1)}, u32[]{:S(2)}, u32[]{:S(2)}) collective-permute-start(bf16[32,1024]{1,0:T(8,128)(2,1)S(1)} %add.12), channel_id=1, source_target_pairs={{0,8},{4,12},{8,0},{12,4},{1,9},{5,13},{9,1},{13,5},{2,10},{6,14},... | collective-permute-start | bytes 196616 | tf_op jit(solution)/shard_map/ppermute | solution.py:46
  38.7 7.2 %collective-permute-start.17 = (bf16[32,1024]{1,0:T(8,128)(2,1)S(1)}, bf16[32,1024]{1,0:T(8,128)(2,1)S(1)}, u32[]{:S(2)}, u32[]{:S(2)}) collective-permute-start(bf16[32,1024]{1,0:T(8,128)(2,1)S(1)} %get-tuple-element.61.x), channel_id=1, source_target_pairs={{0,8},{4,12},{8,0},{12,4},{1,9},{5,13},{9,1},{13,5},{2,10},{6,14},... | collective-permute-start | bytes 196616 | tf_op jit(solution)/shard_map/ppermute | solution.py:46
  40.4 8.3 %collective-permute-start.20 = (bf16[32,1024]{1,0:T(8,128)(2,1)S(1)}, bf16[32,1024]{1,0:T(8,128)(2,1)S(1)}, u32[]{:S(2)}, u32[]{:S(2)}) collective-permute-start(bf16[32,1024]{1,0:T(8,128)(2,1)S(1)} %get-tuple-element.61.x), channel_id=1, source_target_pairs={{0,4},{4,0},{8,12},{12,8},{1,5},{5,1},{9,13},{13,9},{2,6},{6,2},{1... | collective-permute-start | bytes 196616 | tf_op jit(solution)/shard_map/ppermute | solution.py:46
  42.8 7.4 %collective-permute-start.19 = (bf16[32,1152]{1,0:T(8,128)(2,1)S(1)}, bf16[32,1152]{1,0:T(8,128)(2,1)S(1)}, u32[]{:S(2)}, u32[]{:S(2)}) collective-permute-start(bf16[32,1152]{1,0:T(8,128)(2,1)S(1)} %get-tuple-element.64.x.refs_1_), channel_id=1, source_target_pairs={{0,4},{4,0},{8,12},{12,8},{1,5},{5,1},{9,13},{13,9},{2,6},{6,2},{1... | collective-permute-start | bytes 221192 | tf_op jit(solution)/shard_map/ppermute | solution.py:46
  43.6 8.1 %collective-permute-start.16 = (bf16[32,1152]{1,0:T(8,128)(2,1)S(1)}, bf16[32,1152]{1,0:T(8,128)(2,1)S(1)}, u32[]{:S(2)}, u32[]{:S(2)}) collective-permute-start(bf16[32,1152]{1,0:T(8,128)(2,1)S(1)} %get-tuple-element.64.x.refs_1_), channel_id=1, source_target_pairs={{0,8},{4,12},{8,0},{12,4},{1,9},{5,13},{9,1},{13,5},{2,10},{6,14},... | collective-permute-start | bytes 221192 | tf_op jit(solution)/shard_map/ppermute | solution.py:46
  45.9 5.0 %collective-permute-start.18 = (bf16[32,1024]{1,0:T(8,128)(2,1)S(1)}, bf16[32,1024]{1,0:T(8,128)(2,1)S(1)}, u32[]{:S(2)}, u32[]{:S(2)}) collective-permute-start(bf16[32,1024]{1,0:T(8,128)(2,1)S(1)} %collective-permute-done.17.x), channel_id=1, source_target_pairs={{0,4},{4,0},{8,12},{12,8},{1,5},{5,1},{9,13},{13,9},{2,6},{6,2},{1... | collective-permute-start | bytes 196616 | tf_op jit(solution)/shard_map/ppermute | solution.py:46
  46.4 6.2 %collective-permute-start.15 = (bf16[32,1152]{1,0:T(8,128)(2,1)S(1)}, bf16[32,1152]{1,0:T(8,128)(2,1)S(1)}, u32[]{:S(2)}, u32[]{:S(2)}) collective-permute-start(bf16[32,1152]{1,0:T(8,128)(2,1)S(1)} %get-tuple-element.64.x.refs_1_), channel_id=1, source_target_pairs={{0,12},{4,8},{8,4},{12,0},{1,13},{5,9},{9,5},{13,1},{2,14},{6,10},... | collective-permute-start | bytes 221192 | tf_op jit(solution)/shard_map/ppermute | solution.py:46
  53.3 3.8 %collective-permute-start.22 = (bf16[32,1152]{1,0:T(8,128)(2,1)S(1)}, bf16[32,1152]{1,0:T(8,128)(2,1)S(1)}, u32[]{:S(2)}, u32[]{:S(2)}) collective-permute-start(bf16[32,1152]{1,0:T(8,128)(2,1)S(1)} %forward.23.refs_0_), channel_id=1, source_target_pairs={{0,3},{1,2},{2,1},{3,0},{4,7},{5,6},{6,5},{7,4},{8,11},{9,10},{10,... | collective-permute-start | bytes 221192 | tf_op jit(solution)/shard_map/ppermute | solution.py:46
  53.4 3.8 %collective-permute-start.21 = (bf16[32,1152]{1,0:T(8,128)(2,1)S(1)}, bf16[32,1152]{1,0:T(8,128)(2,1)S(1)}, u32[]{:S(2)}, u32[]{:S(2)}) collective-permute-start(bf16[32,1152]{1,0:T(8,128)(2,1)S(1)} %forward.23.refs_0_), channel_id=1, source_target_pairs={{0,1},{1,0},{2,3},{3,2},{4,5},{5,4},{6,7},{7,6},{8,9},{9,8},{10,11... | collective-permute-start | bytes 221192 | tf_op jit(solution)/shard_map/ppermute | solution.py:46
  54.0 4.7 %collective-permute-start.23 = (bf16[32,1152]{1,0:T(8,128)(2,1)S(1)}, bf16[32,1152]{1,0:T(8,128)(2,1)S(1)}, u32[]{:S(2)}, u32[]{:S(2)}) collective-permute-start(bf16[32,1152]{1,0:T(8,128)(2,1)S(1)} %forward.23.refs_0_), channel_id=1, source_target_pairs={{0,2},{1,3},{2,0},{3,1},{4,6},{5,7},{6,4},{7,5},{8,10},{9,11},{10,... | collective-permute-start | bytes 221192 | tf_op jit(solution)/shard_map/ppermute | solution.py:46
  59.8 7.4 %collective-permute-start.24 = (bf16[32,1024]{1,0:T(8,128)(2,1)S(1)}, bf16[32,1024]{1,0:T(8,128)(2,1)S(1)}, u32[]{:S(2)}, u32[]{:S(2)}) collective-permute-start(bf16[32,1024]{1,0:T(8,128)(2,1)S(1)} %get-tuple-element.74), channel_id=1, source_target_pairs={{0,4},{4,0},{8,12},{12,8},{1,5},{5,1},{9,13},{13,9},{2,6},{6,2},{1... | collective-permute-start | bytes 196616 | tf_op jit(solution)/shard_map/ppermute | solution.py:46
  60.6 6.5 %collective-permute-start.25 = (bf16[32,1024]{1,0:T(8,128)(2,1)S(1)}, bf16[32,1024]{1,0:T(8,128)(2,1)S(1)}, u32[]{:S(2)}, u32[]{:S(2)}) collective-permute-start(bf16[32,1024]{1,0:T(8,128)(2,1)S(1)} %get-tuple-element.75), channel_id=1, source_target_pairs={{0,8},{4,12},{8,0},{12,4},{1,9},{5,13},{9,1},{13,5},{2,10},{6,14},... | collective-permute-start | bytes 196616 | tf_op jit(solution)/shard_map/ppermute | solution.py:46
  63.3 6.9 %collective-permute-start.27 = (bf16[32,1024]{1,0:T(8,128)(2,1)S(1)}, bf16[32,1024]{1,0:T(8,128)(2,1)S(1)}, u32[]{:S(2)}, u32[]{:S(2)}) collective-permute-start(bf16[32,1024]{1,0:T(8,128)(2,1)S(1)} %backward.19), channel_id=1, source_target_pairs={{0,4},{4,0},{8,12},{12,8},{1,5},{5,1},{9,13},{13,9},{2,6},{6,2},{1... | collective-permute-start | bytes 196616 | tf_op jit(solution)/shard_map/ppermute | solution.py:46
  64.0 6.2 %collective-permute-start.26 = (bf16[32,1024]{1,0:T(8,128)(2,1)S(1)}, bf16[32,1024]{1,0:T(8,128)(2,1)S(1)}, u32[]{:S(2)}, u32[]{:S(2)}) collective-permute-start(bf16[32,1024]{1,0:T(8,128)(2,1)S(1)} %backward.18), channel_id=1, source_target_pairs={{0,12},{4,8},{8,4},{12,0},{1,13},{5,9},{9,5},{13,1},{2,14},{6,10},... | collective-permute-start | bytes 196616 | tf_op jit(solution)/shard_map/ppermute | solution.py:46
  66.7 4.7 %collective-permute-start.28 = (bf16[32,1024]{1,0:T(8,128)(2,1)S(1)}, bf16[32,1024]{1,0:T(8,128)(2,1)S(1)}, u32[]{:S(2)}, u32[]{:S(2)}) collective-permute-start(bf16[32,1024]{1,0:T(8,128)(2,1)S(1)} %backward.21), channel_id=1, source_target_pairs={{0,4},{4,0},{8,12},{12,8},{1,5},{5,1},{9,13},{13,9},{2,6},{6,2},{1... | collective-permute-start | bytes 196616 | tf_op jit(solution)/shard_map/ppermute | solution.py:46
  67.2 5.2 %collective-permute-start.29 = (bf16[32,1024]{1,0:T(8,128)(2,1)S(1)}, bf16[32,1024]{1,0:T(8,128)(2,1)S(1)}, u32[]{:S(2)}, u32[]{:S(2)}) collective-permute-start(bf16[32,1024]{1,0:T(8,128)(2,1)S(1)} %add.17), channel_id=1, source_target_pairs={{0,8},{4,12},{8,0},{12,4},{1,9},{5,13},{9,1},{13,5},{2,10},{6,14},... | collective-permute-start | bytes 196616 | tf_op jit(solution)/shard_map/ppermute | solution.py:46
  72.8 5.4 %collective-permute-start.32 = (f32[2,32]{1,0:T(2,128)S(1)}, f32[2,32]{1,0:T(2,128)S(1)}, u32[]{:S(2)}, u32[]{:S(2)}) collective-permute-start(f32[2,32]{1,0:T(2,128)S(1)} %get-tuple-element.84.refs_0_), channel_id=1, source_target_pairs={{0,12},{4,8},{8,4},{12,0},{1,13},{5,9},{9,5},{13,1},{2,14},{6,10},... | collective-permute-start | bytes 776 | tf_op jit(solution)/shard_map/ppermute | solution.py:46
  74.9 4.5 %collective-permute-start.31 = (f32[2,32]{1,0:T(2,128)S(1)}, f32[2,32]{1,0:T(2,128)S(1)}, u32[]{:S(2)}, u32[]{:S(2)}) collective-permute-start(f32[2,32]{1,0:T(2,128)S(1)} %get-tuple-element.84.refs_0_), channel_id=1, source_target_pairs={{0,8},{4,12},{8,0},{12,4},{1,9},{5,13},{9,1},{13,5},{2,10},{6,14},... | collective-permute-start | bytes 776 | tf_op jit(solution)/shard_map/ppermute | solution.py:46
  76.0 3.6 %collective-permute-start.30 = (f32[2,32]{1,0:T(2,128)S(1)}, f32[2,32]{1,0:T(2,128)S(1)}, u32[]{:S(2)}, u32[]{:S(2)}) collective-permute-start(f32[2,32]{1,0:T(2,128)S(1)} %get-tuple-element.84.refs_0_), channel_id=1, source_target_pairs={{0,4},{4,0},{8,12},{12,8},{1,5},{5,1},{9,13},{13,9},{2,6},{6,2},{1... | collective-permute-start | bytes 776 | tf_op jit(solution)/shard_map/ppermute | solution.py:46
  79.6 3.6 %collective-permute-start.34 = (f32[2,32]{1,0:T(2,128)S(1)}, f32[2,32]{1,0:T(2,128)S(1)}, u32[]{:S(2)}, u32[]{:S(2)}) collective-permute-start(f32[2,32]{1,0:T(2,128)S(1)} %moves.1.refs_0_), channel_id=1, source_target_pairs={{0,2},{1,3},{2,0},{3,1},{4,6},{5,7},{6,4},{7,5},{8,10},{9,11},{10,... | collective-permute-start | bytes 776 | tf_op jit(solution)/shard_map/ppermute | solution.py:46
  (11 other events, 56.9 us)

commit v7 on v6

--- a/solution.py
+++ b/solution.py
@@ -531,7 +531,10 @@
             visits = [(0, 1), (1, 0), (2, 0), (1, 1), (3, 0), (2, 1), (3, 1)]
     move = call(sum_kernel, "moves", shape(low.shape, f32), everyone(low, "row", (1, 2, 3)))
     weight = call(
-        weight_kernel, "weight", shape((1, scen), f32), [weight, *everyone(move, "col", (1, 2, 3))]
+        weight_kernel,
+        "weight",
+        jax.ShapeDtypeStruct((1, scen), f32),
+        [weight, *everyone(move, "col", (1, 2, 3))],
     )
     return xs[0], y[0], weight.reshape(-1)
 

time: 84.9 us -> 84 us (0.989); the launches traced: 83.7 us -> 83.7 us
    unnamed x17 -> x16, local copies, waits for them, and re-layouts: 1.9 us -> 1.37 us
where the time goes in v7:
time: 84 us; the launch traced here: 83.7 us
  starting transfers between devices  41.2 us (49%)
  Pallas kernels  24.1 us (29%)
  waiting for transfers between devices  15.3 us (18%)
  between operations  1.7 us (2%)
  local copies, waits for them, and re-layouts  1.37 us (2%)
    ppermute x36, starting transfers between devices, swap(): lax.ppermute(array, axis, [(i, i ^ k) for i in range(lax.axis_size(axis))])  41.2 us
    pallas_call x42, Pallas kernels, call(): pl.pallas_call(kernel, out_shape=out_shape, in_specs=specs, out_specs=out...  24.1 us
    ppermute x36, waiting for transfers between devices, swap(): lax.ppermute(array, axis, [(i, i ^ k) for i in range(lax.axis_size(axis))])  15.3 us
  transfers between devices with their start and end apart: 36, of which 15 were waited for; matrix products, arithmetic and copies ran while one was open for 2% of the time, Pallas kernels for 22%

profile of v7, /device:TPU:0, one launch (start us, length us, event | category | flops | bytes accessed | tf_op | source)
XLA Modules:
  0.0 83.7 jit_solution(7377297633823185136)
XLA Ops:
  0.6 1.2 %start.1 = (bf16[32,2048]{1,0:T(8,128)(2,1)S(1)}, f32[2,32,256]{2,1,0:T(8,128)S(1)}, bf16[512,128,128]{2,1,0:T(8,128)(2,1)S(1)}) custom-call(f32[32,2048]{1,0:T(8,128)} %refs_2_.3, f32[32,256]{1,0:T(8,128)} %y.1, f32[32,256]{1,0:T(8,128)} %rhs.1), custom_call_target="tpu_custom_call" | custom-call | tf_op jit(solution)/shard_map/start/pallas_call | solution.py:32
  1.8 3.1 %collective-permute-start.3 = (bf16[32,2048]{1,0:T(8,128)(2,1)S(1)}, bf16[32,2048]{1,0:T(8,128)(2,1)S(1)}, u32[]{:S(2)}, u32[]{:S(2)}) collective-permute-start(bf16[32,2048]{1,0:T(8,128)(2,1)S(1)} %get-tuple-element.47.x), channel_id=1, source_target_pairs={{0,4},{4,0},{8,12},{12,8},{1,5},{5,1},{9,13},{13,9},{2,6},{6,2},{1... | collective-permute-start | bytes 393224 | tf_op jit(solution)/shard_map/ppermute | solution.py:46
  4.9 2.6 %collective-permute-start.2 = (bf16[32,2048]{1,0:T(8,128)(2,1)S(1)}, bf16[32,2048]{1,0:T(8,128)(2,1)S(1)}, u32[]{:S(2)}, u32[]{:S(2)}) collective-permute-start(bf16[32,2048]{1,0:T(8,128)(2,1)S(1)} %get-tuple-element.47.x), channel_id=1, source_target_pairs={{0,8},{4,12},{8,0},{12,4},{1,9},{5,13},{9,1},{13,5},{2,10},{6,14},... | collective-permute-start | bytes 393224 | tf_op jit(solution)/shard_map/ppermute | solution.py:46
  7.5 1.7 %collective-permute-start = (f32[2,32,256]{2,1,0:T(8,128)S(1)}, f32[2,32,256]{2,1,0:T(8,128)S(1)}, u32[]{:S(2)}, u32[]{:S(2)}) collective-permute-start(f32[2,32,256]{2,1,0:T(8,128)S(1)} %get-tuple-element.50.refs_4_), channel_id=1, source_target_pairs={{0,2},{1,3},{2,0},{3,1},{4,6},{5,7},{6,4},{7,5},{8,10},{9,11},{10,... | collective-permute-start | bytes 196616 | tf_op jit(solution)/shard_map/ppermute | solution.py:46
  9.8 3.7 %densify.1.k = bf16[512,128,128]{2,1,0:T(8,128)(2,1)S(1)} custom-call(s32[1,1]{1,0:T(1,128)S(6)} %copy.20.count, s32[1,1,256]{2,1,0:T(1,128)} %rows_in.1, s32[1,1,256]{2,1,0:T(1,128)} %cols_in.1, bf16[256,128,128]{2,1,0:T(8,128)(2,1)} %bitcast.22, bf16[512,128,128]{2,1,0:T(8,128)(2,1)S(1)} %get-tuple-element.44._), custom_call_target="tpu_custom_call", output_to_operand_aliasing={{}: (4, {})} | custom-call | bytes 33554432 | tf_op jit(solution)/shard_map/densify/pallas_call | solution.py:32
  13.6 1.3 %forward.12.refs_0_ = f32[32,1024]{1,0:T(8,128)S(1)} custom-call(bf16[512,128,128]{2,1,0:T(8,128)(2,1)S(1)} %densify.1.k, bf16[32,2048]{1,0:T(8,128)(2,1)S(1)} %get-tuple-element.47.x), custom_call_target="tpu_custom_call" | custom-call | flops 134217728 | bytes 4194304 | tf_op jit(solution)/shard_map/forward/pallas_call | solution.py:32
  14.9 1.3 %forward.13.refs_0_ = f32[32,1024]{1,0:T(8,128)S(1)} custom-call(bf16[512,128,128]{2,1,0:T(8,128)(2,1)S(1)} %densify.1.k, bf16[32,2048]{1,0:T(8,128)(2,1)S(1)} %collective-permute-done.3.x, f32[32,1024]{1,0:T(8,128)S(1)} %forward.12.refs_0_), custom_call_target="tpu_custom_call" | custom-call | flops 134217728 | bytes 4194304 | tf_op jit(solution)/shard_map/forward/pallas_call | solution.py:32
  16.2 1.6 %collective-permute-done.2.x = bf16[32,2048]{1,0:T(8,128)(2,1)S(1)} collective-permute-done((bf16[32,2048]{1,0:T(8,128)(2,1)S(1)}, bf16[32,2048]{1,0:T(8,128)(2,1)S(1)}, u32[]{:S(2)}, u32[]{:S(2)}) %collective-permute-start.2) | collective-permute-done | bytes 131104 | tf_op jit(solution)/shard_map/ppermute | solution.py:46
  17.8 1.3 %forward.14.refs_0_ = f32[32,1024]{1,0:T(8,128)S(1)} custom-call(bf16[512,128,128]{2,1,0:T(8,128)(2,1)S(1)} %densify.1.k, bf16[32,2048]{1,0:T(8,128)(2,1)S(1)} %collective-permute-done.2.x, f32[32,1024]{1,0:T(8,128)S(1)} %forward.13.refs_0_), custom_call_target="tpu_custom_call" | custom-call | flops 134217728 | bytes 4194304 | tf_op jit(solution)/shard_map/forward/pallas_call | solution.py:32
  19.1 1.3 %forward.15.refs_0_ = bf16[32,1024]{1,0:T(8,128)(2,1)S(1)} custom-call(bf16[512,128,128]{2,1,0:T(8,128)(2,1)S(1)} %densify.1.k, bf16[32,2048]{1,0:T(8,128)(2,1)S(1)} %collective-permute-done.1.x, f32[32,1024]{1,0:T(8,128)S(1)} %forward.14.refs_0_), custom_call_target="tpu_custom_call" | custom-call | flops 134217728 | bytes 4194304 | tf_op jit(solution)/shard_map/forward/pallas_call | solution.py:32
  20.6 1.6 %collective-permute-start.4 = (bf16[32,1024]{1,0:T(8,128)(2,1)S(1)}, bf16[32,1024]{1,0:T(8,128)(2,1)S(1)}, u32[]{:S(2)}, u32[]{:S(2)}) collective-permute-start(bf16[32,1024]{1,0:T(8,128)(2,1)S(1)} %forward.15.refs_0_), channel_id=1, source_target_pairs={{0,1},{1,0},{2,3},{3,2},{4,5},{5,4},{6,7},{7,6},{8,9},{9,8},{10,11... | collective-permute-start | bytes 196616 | tf_op jit(solution)/shard_map/ppermute | solution.py:46
  23.2 1.7 %collective-permute-done.5.refs_3_ = bf16[32,1024]{1,0:T(8,128)(2,1)S(1)} collective-permute-done((bf16[32,1024]{1,0:T(8,128)(2,1)S(1)}, bf16[32,1024]{1,0:T(8,128)(2,1)S(1)}, u32[]{:S(2)}, u32[]{:S(2)}) %collective-permute-start.5) | collective-permute-done | bytes 65568 | tf_op jit(solution)/shard_map/ppermute | solution.py:46
  24.9 2.0 %collective-permute-done.6.refs_2_ = bf16[32,1024]{1,0:T(8,128)(2,1)S(1)} collective-permute-done((bf16[32,1024]{1,0:T(8,128)(2,1)S(1)}, bf16[32,1024]{1,0:T(8,128)(2,1)S(1)}, u32[]{:S(2)}, u32[]{:S(2)}) %collective-permute-start.6) | collective-permute-done | bytes 65568 | tf_op jit(solution)/shard_map/ppermute | solution.py:46
  28.4 2.2 %collective-permute-start.10 = (bf16[32,1024]{1,0:T(8,128)(2,1)S(1)}, bf16[32,1024]{1,0:T(8,128)(2,1)S(1)}, u32[]{:S(2)}, u32[]{:S(2)}) collective-permute-start(bf16[32,1024]{1,0:T(8,128)(2,1)S(1)} %get-tuple-element.58), channel_id=1, source_target_pairs={{0,8},{4,12},{8,0},{12,4},{1,9},{5,13},{9,1},{13,5},{2,10},{6,14},... | collective-permute-start | bytes 196616 | tf_op jit(solution)/shard_map/ppermute | solution.py:46
  31.1 1.6 %collective-permute-start.11 = (bf16[32,1024]{1,0:T(8,128)(2,1)S(1)}, bf16[32,1024]{1,0:T(8,128)(2,1)S(1)}, u32[]{:S(2)}, u32[]{:S(2)}) collective-permute-start(bf16[32,1024]{1,0:T(8,128)(2,1)S(1)} %backward.12), channel_id=1, source_target_pairs={{0,12},{4,8},{8,4},{12,0},{1,13},{5,9},{9,5},{13,1},{2,14},{6,10},... | collective-permute-start | bytes 196616 | tf_op jit(solution)/shard_map/ppermute | solution.py:46
  33.6 2.1 %collective-permute-start.13 = (bf16[32,1024]{1,0:T(8,128)(2,1)S(1)}, bf16[32,1024]{1,0:T(8,128)(2,1)S(1)}, u32[]{:S(2)}, u32[]{:S(2)}) collective-permute-start(bf16[32,1024]{1,0:T(8,128)(2,1)S(1)} %backward.16), channel_id=1, source_target_pairs={{0,4},{4,0},{8,12},{12,8},{1,5},{5,1},{9,13},{13,9},{2,6},{6,2},{1... | collective-permute-start | bytes 196616 | tf_op jit(solution)/shard_map/ppermute | solution.py:46
  38.7 1.2 %collective-permute-start.17 = (bf16[32,1024]{1,0:T(8,128)(2,1)S(1)}, bf16[32,1024]{1,0:T(8,128)(2,1)S(1)}, u32[]{:S(2)}, u32[]{:S(2)}) collective-permute-start(bf16[32,1024]{1,0:T(8,128)(2,1)S(1)} %get-tuple-element.61.x), channel_id=1, source_target_pairs={{0,8},{4,12},{8,0},{12,4},{1,9},{5,13},{9,1},{13,5},{2,10},{6,14},... | collective-permute-start | bytes 196616 | tf_op jit(solution)/shard_map/ppermute | solution.py:46
  40.4 1.3 %collective-permute-start.20 = (bf16[32,1024]{1,0:T(8,128)(2,1)S(1)}, bf16[32,1024]{1,0:T(8,128)(2,1)S(1)}, u32[]{:S(2)}, u32[]{:S(2)}) collective-permute-start(bf16[32,1024]{1,0:T(8,128)(2,1)S(1)} %get-tuple-element.61.x), channel_id=1, source_target_pairs={{0,4},{4,0},{8,12},{12,8},{1,5},{5,1},{9,13},{13,9},{2,6},{6,2},{1... | collective-permute-start | bytes 196616 | tf_op jit(solution)/shard_map/ppermute | solution.py:46
  43.6 1.7 %collective-permute-start.16 = (bf16[32,1152]{1,0:T(8,128)(2,1)S(1)}, bf16[32,1152]{1,0:T(8,128)(2,1)S(1)}, u32[]{:S(2)}, u32[]{:S(2)}) collective-permute-start(bf16[32,1152]{1,0:T(8,128)(2,1)S(1)} %get-tuple-element.64.x.refs_1_), channel_id=1, source_target_pairs={{0,8},{4,12},{8,0},{12,4},{1,9},{5,13},{9,1},{13,5},{2,10},{6,14},... | collective-permute-start | bytes 221192 | tf_op jit(solution)/shard_map/ppermute | solution.py:46
  46.4 1.6 %collective-permute-start.15 = (bf16[32,1152]{1,0:T(8,128)(2,1)S(1)}, bf16[32,1152]{1,0:T(8,128)(2,1)S(1)}, u32[]{:S(2)}, u32[]{:S(2)}) collective-permute-start(bf16[32,1152]{1,0:T(8,128)(2,1)S(1)} %get-tuple-element.64.x.refs_1_), channel_id=1, source_target_pairs={{0,12},{4,8},{8,4},{12,0},{1,13},{5,9},{9,5},{13,1},{2,14},{6,10},... | collective-permute-start | bytes 221192 | tf_op jit(solution)/shard_map/ppermute | solution.py:46
  54.0 1.5 %collective-permute-start.23 = (bf16[32,1152]{1,0:T(8,128)(2,1)S(1)}, bf16[32,1152]{1,0:T(8,128)(2,1)S(1)}, u32[]{:S(2)}, u32[]{:S(2)}) collective-permute-start(bf16[32,1152]{1,0:T(8,128)(2,1)S(1)} %forward.23.refs_0_), channel_id=1, source_target_pairs={{0,2},{1,3},{2,0},{3,1},{4,6},{5,7},{6,4},{7,5},{8,10},{9,11},{10,... | collective-permute-start | bytes 221192 | tf_op jit(solution)/shard_map/ppermute | solution.py:46
  55.5 1.6 %collective-permute-done.22.refs_3_ = bf16[32,1152]{1,0:T(8,128)(2,1)S(1)} collective-permute-done((bf16[32,1152]{1,0:T(8,128)(2,1)S(1)}, bf16[32,1152]{1,0:T(8,128)(2,1)S(1)}, u32[]{:S(2)}, u32[]{:S(2)}) %collective-permute-start.22) | collective-permute-done | bytes 73760 | tf_op jit(solution)/shard_map/ppermute | solution.py:46
  57.1 1.6 %collective-permute-done.23.refs_2_ = bf16[32,1152]{1,0:T(8,128)(2,1)S(1)} collective-permute-done((bf16[32,1152]{1,0:T(8,128)(2,1)S(1)}, bf16[32,1152]{1,0:T(8,128)(2,1)S(1)}, u32[]{:S(2)}, u32[]{:S(2)}) %collective-permute-start.23) | collective-permute-done | bytes 73760 | tf_op jit(solution)/shard_map/ppermute | solution.py:46
  58.7 1.0 %dual.3 = (f32[32,256]{1,0:T(8,128)S(1)}, bf16[32,1024]{1,0:T(8,128)(2,1)S(1)}, f32[32,2]{1,0:T(8,128)S(1)}, f32[1,32]{1,0:T(1,128)S(1)}, bf16[32,1024]{1,0:T(8,128)(2,1)S(1)}, /*index=5*/bf16[32,1024]{1,0:T(8,128)(2,1)S(1)}) custom-call(bf16[512,128,128]{2,1,0:T(8,128)(2,1)S(1)} %densify.1.k, f32[1,32]{1,0:T(1,128)S(1)} %bitcast.19, ...), custom_call_target="tpu_custom_call" | custom-call | flops 67108864 | bytes 2097152 | tf_op jit(solution)/shard_map/dual/pallas_call | solution.py:32
  60.6 1.9 %collective-permute-start.25 = (bf16[32,1024]{1,0:T(8,128)(2,1)S(1)}, bf16[32,1024]{1,0:T(8,128)(2,1)S(1)}, u32[]{:S(2)}, u32[]{:S(2)}) collective-permute-start(bf16[32,1024]{1,0:T(8,128)(2,1)S(1)} %get-tuple-element.75), channel_id=1, source_target_pairs={{0,8},{4,12},{8,0},{12,4},{1,9},{5,13},{9,1},{13,5},{2,10},{6,14},... | collective-permute-start | bytes 196616 | tf_op jit(solution)/shard_map/ppermute | solution.py:46
  64.0 1.9 %collective-permute-start.26 = (bf16[32,1024]{1,0:T(8,128)(2,1)S(1)}, bf16[32,1024]{1,0:T(8,128)(2,1)S(1)}, u32[]{:S(2)}, u32[]{:S(2)}) collective-permute-start(bf16[32,1024]{1,0:T(8,128)(2,1)S(1)} %backward.18), channel_id=1, source_target_pairs={{0,12},{4,8},{8,4},{12,0},{1,13},{5,9},{9,5},{13,1},{2,14},{6,10},... | collective-permute-start | bytes 196616 | tf_op jit(solution)/shard_map/ppermute | solution.py:46
  67.2 2.2 %collective-permute-start.29 = (bf16[32,1024]{1,0:T(8,128)(2,1)S(1)}, bf16[32,1024]{1,0:T(8,128)(2,1)S(1)}, u32[]{:S(2)}, u32[]{:S(2)}) collective-permute-start(bf16[32,1024]{1,0:T(8,128)(2,1)S(1)} %add.17), channel_id=1, source_target_pairs={{0,8},{4,12},{8,0},{12,4},{1,9},{5,13},{9,1},{13,5},{2,10},{6,14},... | collective-permute-start | bytes 196616 | tf_op jit(solution)/shard_map/ppermute | solution.py:46
  70.3 1.2 %collective-permute-done.28.part = bf16[32,1024]{1,0:T(8,128)(2,1)S(1)} collective-permute-done((bf16[32,1024]{1,0:T(8,128)(2,1)S(1)}, bf16[32,1024]{1,0:T(8,128)(2,1)S(1)}, u32[]{:S(2)}, u32[]{:S(2)}) %collective-permute-start.28) | collective-permute-done | bytes 65568 | tf_op jit(solution)/shard_map/ppermute | solution.py:46
  72.8 2.2 %collective-permute-start.32 = (f32[2,32]{1,0:T(2,128)S(1)}, f32[2,32]{1,0:T(2,128)S(1)}, u32[]{:S(2)}, u32[]{:S(2)}) collective-permute-start(f32[2,32]{1,0:T(2,128)S(1)} %get-tuple-element.84.refs_0_), channel_id=1, source_target_pairs={{0,12},{4,8},{8,4},{12,0},{1,13},{5,9},{9,5},{13,1},{2,14},{6,10},... | collective-permute-start | bytes 776 | tf_op jit(solution)/shard_map/ppermute | solution.py:46
  76.0 1.3 %collective-permute-start.30 = (f32[2,32]{1,0:T(2,128)S(1)}, f32[2,32]{1,0:T(2,128)S(1)}, u32[]{:S(2)}, u32[]{:S(2)}) collective-permute-start(f32[2,32]{1,0:T(2,128)S(1)} %get-tuple-element.84.refs_0_), channel_id=1, source_target_pairs={{0,4},{4,0},{8,12},{12,8},{1,5},{5,1},{9,13},{13,9},{2,6},{6,2},{1... | collective-permute-start | bytes 776 | tf_op jit(solution)/shard_map/ppermute | solution.py:46
  78.2 1.2 %collective-permute-done.31.refs_2_ = f32[2,32]{1,0:T(2,128)S(1)} collective-permute-done((f32[2,32]{1,0:T(2,128)S(1)}, f32[2,32]{1,0:T(2,128)S(1)}, u32[]{:S(2)}, u32[]{:S(2)}) %collective-permute-start.31) | collective-permute-done | bytes 288 | tf_op jit(solution)/shard_map/ppermute | solution.py:46
  79.6 1.4 %collective-permute-start.34 = (f32[2,32]{1,0:T(2,128)S(1)}, f32[2,32]{1,0:T(2,128)S(1)}, u32[]{:S(2)}, u32[]{:S(2)}) collective-permute-start(f32[2,32]{1,0:T(2,128)S(1)} %moves.1.refs_0_), channel_id=1, source_target_pairs={{0,2},{1,3},{2,0},{3,1},{4,6},{5,7},{6,4},{7,5},{8,10},{9,11},{10,... | collective-permute-start | bytes 776 | tf_op jit(solution)/shard_map/ppermute | solution.py:46
  (98 shorter events, 27.1 us)
Async XLA Ops:
  1.8 13.1 %collective-permute-start.3 = (bf16[32,2048]{1,0:T(8,128)(2,1)S(1)}, bf16[32,2048]{1,0:T(8,128)(2,1)S(1)}, u32[]{:S(2)}, u32[]{:S(2)}) collective-permute-start(bf16[32,2048]{1,0:T(8,128)(2,1)S(1)} %get-tuple-element.47.x), channel_id=1, source_target_pairs={{0,4},{4,0},{8,12},{12,8},{1,5},{5,1},{9,13},{13,9},{2,6},{6,2},{1... | collective-permute-start | bytes 393224 | tf_op jit(solution)/shard_map/ppermute | solution.py:46
  4.9 12.9 %collective-permute-start.2 = (bf16[32,2048]{1,0:T(8,128)(2,1)S(1)}, bf16[32,2048]{1,0:T(8,128)(2,1)S(1)}, u32[]{:S(2)}, u32[]{:S(2)}) collective-permute-start(bf16[32,2048]{1,0:T(8,128)(2,1)S(1)} %get-tuple-element.47.x), channel_id=1, source_target_pairs={{0,8},{4,12},{8,0},{12,4},{1,9},{5,13},{9,1},{13,5},{2,10},{6,14},... | collective-permute-start | bytes 393224 | tf_op jit(solution)/shard_map/ppermute | solution.py:46
  7.5 11.7 %collective-permute-start.1 = (bf16[32,2048]{1,0:T(8,128)(2,1)S(1)}, bf16[32,2048]{1,0:T(8,128)(2,1)S(1)}, u32[]{:S(2)}, u32[]{:S(2)}) collective-permute-start(bf16[32,2048]{1,0:T(8,128)(2,1)S(1)} %get-tuple-element.47.x), channel_id=1, source_target_pairs={{0,12},{4,8},{8,4},{12,0},{1,13},{5,9},{9,5},{13,1},{2,14},{6,10},... | collective-permute-start | bytes 393224 | tf_op jit(solution)/shard_map/ppermute | solution.py:46
  7.5 6.1 %collective-permute-start = (f32[2,32,256]{2,1,0:T(8,128)S(1)}, f32[2,32,256]{2,1,0:T(8,128)S(1)}, u32[]{:S(2)}, u32[]{:S(2)}) collective-permute-start(f32[2,32,256]{2,1,0:T(8,128)S(1)} %get-tuple-element.50.refs_4_), channel_id=1, source_target_pairs={{0,2},{1,3},{2,0},{3,1},{4,6},{5,7},{6,4},{7,5},{8,10},{9,11},{10,... | collective-permute-start | bytes 196616 | tf_op jit(solution)/shard_map/ppermute | solution.py:46
  20.5 4.4 %collective-permute-start.5 = (bf16[32,1024]{1,0:T(8,128)(2,1)S(1)}, bf16[32,1024]{1,0:T(8,128)(2,1)S(1)}, u32[]{:S(2)}, u32[]{:S(2)}) collective-permute-start(bf16[32,1024]{1,0:T(8,128)(2,1)S(1)} %forward.15.refs_0_), channel_id=1, source_target_pairs={{0,3},{1,2},{2,1},{3,0},{4,7},{5,6},{6,5},{7,4},{8,11},{9,10},{10,... | collective-permute-start | bytes 196616 | tf_op jit(solution)/shard_map/ppermute | solution.py:46
  20.6 4.3 %collective-permute-start.4 = (bf16[32,1024]{1,0:T(8,128)(2,1)S(1)}, bf16[32,1024]{1,0:T(8,128)(2,1)S(1)}, u32[]{:S(2)}, u32[]{:S(2)}) collective-permute-start(bf16[32,1024]{1,0:T(8,128)(2,1)S(1)} %forward.15.refs_0_), channel_id=1, source_target_pairs={{0,1},{1,0},{2,3},{3,2},{4,5},{5,4},{6,7},{7,6},{8,9},{9,8},{10,11... | collective-permute-start | bytes 196616 | tf_op jit(solution)/shard_map/ppermute | solution.py:46
  22.7 4.3 %collective-permute-start.6 = (bf16[32,1024]{1,0:T(8,128)(2,1)S(1)}, bf16[32,1024]{1,0:T(8,128)(2,1)S(1)}, u32[]{:S(2)}, u32[]{:S(2)}) collective-permute-start(bf16[32,1024]{1,0:T(8,128)(2,1)S(1)} %forward.15.refs_0_), channel_id=1, source_target_pairs={{0,2},{1,3},{2,0},{3,1},{4,6},{5,7},{6,4},{7,5},{8,10},{9,11},{10,... | collective-permute-start | bytes 196616 | tf_op jit(solution)/shard_map/ppermute | solution.py:46
  27.7 8.4 %collective-permute-start.9 = (bf16[32,1024]{1,0:T(8,128)(2,1)S(1)}, bf16[32,1024]{1,0:T(8,128)(2,1)S(1)}, u32[]{:S(2)}, u32[]{:S(2)}) collective-permute-start(bf16[32,1024]{1,0:T(8,128)(2,1)S(1)} %get-tuple-element.57), channel_id=1, source_target_pairs={{0,4},{4,0},{8,12},{12,8},{1,5},{5,1},{9,13},{13,9},{2,6},{6,2},{1... | collective-permute-start | bytes 196616 | tf_op jit(solution)/shard_map/ppermute | solution.py:46
  28.4 7.7 %collective-permute-start.10 = (bf16[32,1024]{1,0:T(8,128)(2,1)S(1)}, bf16[32,1024]{1,0:T(8,128)(2,1)S(1)}, u32[]{:S(2)}, u32[]{:S(2)}) collective-permute-start(bf16[32,1024]{1,0:T(8,128)(2,1)S(1)} %get-tuple-element.58), channel_id=1, source_target_pairs={{0,8},{4,12},{8,0},{12,4},{1,9},{5,13},{9,1},{13,5},{2,10},{6,14},... | collective-permute-start | bytes 196616 | tf_op jit(solution)/shard_map/ppermute | solution.py:46
  31.1 6.9 %collective-permute-start.11 = (bf16[32,1024]{1,0:T(8,128)(2,1)S(1)}, bf16[32,1024]{1,0:T(8,128)(2,1)S(1)}, u32[]{:S(2)}, u32[]{:S(2)}) collective-permute-start(bf16[32,1024]{1,0:T(8,128)(2,1)S(1)} %backward.12), channel_id=1, source_target_pairs={{0,12},{4,8},{8,4},{12,0},{1,13},{5,9},{9,5},{13,1},{2,14},{6,10},... | collective-permute-start | bytes 196616 | tf_op jit(solution)/shard_map/ppermute | solution.py:46
  33.1 5.4 %collective-permute-start.12 = (bf16[32,1024]{1,0:T(8,128)(2,1)S(1)}, bf16[32,1024]{1,0:T(8,128)(2,1)S(1)}, u32[]{:S(2)}, u32[]{:S(2)}) collective-permute-start(bf16[32,1024]{1,0:T(8,128)(2,1)S(1)} %backward.13), channel_id=1, source_target_pairs={{0,4},{4,0},{8,12},{12,8},{1,5},{5,1},{9,13},{13,9},{2,6},{6,2},{1... | collective-permute-start | bytes 196616 | tf_op jit(solution)/shard_map/ppermute | solution.py:46
  33.6 8.0 %collective-permute-start.13 = (bf16[32,1024]{1,0:T(8,128)(2,1)S(1)}, bf16[32,1024]{1,0:T(8,128)(2,1)S(1)}, u32[]{:S(2)}, u32[]{:S(2)}) collective-permute-start(bf16[32,1024]{1,0:T(8,128)(2,1)S(1)} %backward.16), channel_id=1, source_target_pairs={{0,4},{4,0},{8,12},{12,8},{1,5},{5,1},{9,13},{13,9},{2,6},{6,2},{1... | collective-permute-start | bytes 196616 | tf_op jit(solution)/shard_map/ppermute | solution.py:46
  36.2 6.3 %collective-permute-start.14 = (bf16[32,1024]{1,0:T(8,128)(2,1)S(1)}, bf16[32,1024]{1,0:T(8,128)(2,1)S(1)}, u32[]{:S(2)}, u32[]{:S(2)}) collective-permute-start(bf16[32,1024]{1,0:T(8,128)(2,1)S(1)} %add.12), channel_id=1, source_target_pairs={{0,8},{4,12},{8,0},{12,4},{1,9},{5,13},{9,1},{13,5},{2,10},{6,14},... | collective-permute-start | bytes 196616 | tf_op jit(solution)/shard_map/ppermute | solution.py:46
  38.7 7.2 %collective-permute-start.17 = (bf16[32,1024]{1,0:T(8,128)(2,1)S(1)}, bf16[32,1024]{1,0:T(8,128)(2,1)S(1)}, u32[]{:S(2)}, u32[]{:S(2)}) collective-permute-start(bf16[32,1024]{1,0:T(8,128)(2,1)S(1)} %get-tuple-element.61.x), channel_id=1, source_target_pairs={{0,8},{4,12},{8,0},{12,4},{1,9},{5,13},{9,1},{13,5},{2,10},{6,14},... | collective-permute-start | bytes 196616 | tf_op jit(solution)/shard_map/ppermute | solution.py:46
  40.4 8.3 %collective-permute-start.20 = (bf16[32,1024]{1,0:T(8,128)(2,1)S(1)}, bf16[32,1024]{1,0:T(8,128)(2,1)S(1)}, u32[]{:S(2)}, u32[]{:S(2)}) collective-permute-start(bf16[32,1024]{1,0:T(8,128)(2,1)S(1)} %get-tuple-element.61.x), channel_id=1, source_target_pairs={{0,4},{4,0},{8,12},{12,8},{1,5},{5,1},{9,13},{13,9},{2,6},{6,2},{1... | collective-permute-start | bytes 196616 | tf_op jit(solution)/shard_map/ppermute | solution.py:46
  42.8 7.4 %collective-permute-start.19 = (bf16[32,1152]{1,0:T(8,128)(2,1)S(1)}, bf16[32,1152]{1,0:T(8,128)(2,1)S(1)}, u32[]{:S(2)}, u32[]{:S(2)}) collective-permute-start(bf16[32,1152]{1,0:T(8,128)(2,1)S(1)} %get-tuple-element.64.x.refs_1_), channel_id=1, source_target_pairs={{0,4},{4,0},{8,12},{12,8},{1,5},{5,1},{9,13},{13,9},{2,6},{6,2},{1... | collective-permute-start | bytes 221192 | tf_op jit(solution)/shard_map/ppermute | solution.py:46
  43.6 8.1 %collective-permute-start.16 = (bf16[32,1152]{1,0:T(8,128)(2,1)S(1)}, bf16[32,1152]{1,0:T(8,128)(2,1)S(1)}, u32[]{:S(2)}, u32[]{:S(2)}) collective-permute-start(bf16[32,1152]{1,0:T(8,128)(2,1)S(1)} %get-tuple-element.64.x.refs_1_), channel_id=1, source_target_pairs={{0,8},{4,12},{8,0},{12,4},{1,9},{5,13},{9,1},{13,5},{2,10},{6,14},... | collective-permute-start | bytes 221192 | tf_op jit(solution)/shard_map/ppermute | solution.py:46
  45.9 5.0 %collective-permute-start.18 = (bf16[32,1024]{1,0:T(8,128)(2,1)S(1)}, bf16[32,1024]{1,0:T(8,128)(2,1)S(1)}, u32[]{:S(2)}, u32[]{:S(2)}) collective-permute-start(bf16[32,1024]{1,0:T(8,128)(2,1)S(1)} %collective-permute-done.17.x), channel_id=1, source_target_pairs={{0,4},{4,0},{8,12},{12,8},{1,5},{5,1},{9,13},{13,9},{2,6},{6,2},{1... | collective-permute-start | bytes 196616 | tf_op jit(solution)/shard_map/ppermute | solution.py:46
  46.4 6.2 %collective-permute-start.15 = (bf16[32,1152]{1,0:T(8,128)(2,1)S(1)}, bf16[32,1152]{1,0:T(8,128)(2,1)S(1)}, u32[]{:S(2)}, u32[]{:S(2)}) collective-permute-start(bf16[32,1152]{1,0:T(8,128)(2,1)S(1)} %get-tuple-element.64.x.refs_1_), channel_id=1, source_target_pairs={{0,12},{4,8},{8,4},{12,0},{1,13},{5,9},{9,5},{13,1},{2,14},{6,10},... | collective-permute-start | bytes 221192 | tf_op jit(solution)/shard_map/ppermute | solution.py:46
  53.3 3.8 %collective-permute-start.22 = (bf16[32,1152]{1,0:T(8,128)(2,1)S(1)}, bf16[32,1152]{1,0:T(8,128)(2,1)S(1)}, u32[]{:S(2)}, u32[]{:S(2)}) collective-permute-start(bf16[32,1152]{1,0:T(8,128)(2,1)S(1)} %forward.23.refs_0_), channel_id=1, source_target_pairs={{0,3},{1,2},{2,1},{3,0},{4,7},{5,6},{6,5},{7,4},{8,11},{9,10},{10,... | collective-permute-start | bytes 221192 | tf_op jit(solution)/shard_map/ppermute | solution.py:46
  53.4 3.8 %collective-permute-start.21 = (bf16[32,1152]{1,0:T(8,128)(2,1)S(1)}, bf16[32,1152]{1,0:T(8,128)(2,1)S(1)}, u32[]{:S(2)}, u32[]{:S(2)}) collective-permute-start(bf16[32,1152]{1,0:T(8,128)(2,1)S(1)} %forward.23.refs_0_), channel_id=1, source_target_pairs={{0,1},{1,0},{2,3},{3,2},{4,5},{5,4},{6,7},{7,6},{8,9},{9,8},{10,11... | collective-permute-start | bytes 221192 | tf_op jit(solution)/shard_map/ppermute | solution.py:46
  54.0 4.7 %collective-permute-start.23 = (bf16[32,1152]{1,0:T(8,128)(2,1)S(1)}, bf16[32,1152]{1,0:T(8,128)(2,1)S(1)}, u32[]{:S(2)}, u32[]{:S(2)}) collective-permute-start(bf16[32,1152]{1,0:T(8,128)(2,1)S(1)} %forward.23.refs_0_), channel_id=1, source_target_pairs={{0,2},{1,3},{2,0},{3,1},{4,6},{5,7},{6,4},{7,5},{8,10},{9,11},{10,... | collective-permute-start | bytes 221192 | tf_op jit(solution)/shard_map/ppermute | solution.py:46
  59.8 7.4 %collective-permute-start.24 = (bf16[32,1024]{1,0:T(8,128)(2,1)S(1)}, bf16[32,1024]{1,0:T(8,128)(2,1)S(1)}, u32[]{:S(2)}, u32[]{:S(2)}) collective-permute-start(bf16[32,1024]{1,0:T(8,128)(2,1)S(1)} %get-tuple-element.74), channel_id=1, source_target_pairs={{0,4},{4,0},{8,12},{12,8},{1,5},{5,1},{9,13},{13,9},{2,6},{6,2},{1... | collective-permute-start | bytes 196616 | tf_op jit(solution)/shard_map/ppermute | solution.py:46
  60.6 6.5 %collective-permute-start.25 = (bf16[32,1024]{1,0:T(8,128)(2,1)S(1)}, bf16[32,1024]{1,0:T(8,128)(2,1)S(1)}, u32[]{:S(2)}, u32[]{:S(2)}) collective-permute-start(bf16[32,1024]{1,0:T(8,128)(2,1)S(1)} %get-tuple-element.75), channel_id=1, source_target_pairs={{0,8},{4,12},{8,0},{12,4},{1,9},{5,13},{9,1},{13,5},{2,10},{6,14},... | collective-permute-start | bytes 196616 | tf_op jit(solution)/shard_map/ppermute | solution.py:46
  63.3 6.9 %collective-permute-start.27 = (bf16[32,1024]{1,0:T(8,128)(2,1)S(1)}, bf16[32,1024]{1,0:T(8,128)(2,1)S(1)}, u32[]{:S(2)}, u32[]{:S(2)}) collective-permute-start(bf16[32,1024]{1,0:T(8,128)(2,1)S(1)} %backward.19), channel_id=1, source_target_pairs={{0,4},{4,0},{8,12},{12,8},{1,5},{5,1},{9,13},{13,9},{2,6},{6,2},{1... | collective-permute-start | bytes 196616 | tf_op jit(solution)/shard_map/ppermute | solution.py:46
  64.0 6.2 %collective-permute-start.26 = (bf16[32,1024]{1,0:T(8,128)(2,1)S(1)}, bf16[32,1024]{1,0:T(8,128)(2,1)S(1)}, u32[]{:S(2)}, u32[]{:S(2)}) collective-permute-start(bf16[32,1024]{1,0:T(8,128)(2,1)S(1)} %backward.18), channel_id=1, source_target_pairs={{0,12},{4,8},{8,4},{12,0},{1,13},{5,9},{9,5},{13,1},{2,14},{6,10},... | collective-permute-start | bytes 196616 | tf_op jit(solution)/shard_map/ppermute | solution.py:46
  66.7 4.7 %collective-permute-start.28 = (bf16[32,1024]{1,0:T(8,128)(2,1)S(1)}, bf16[32,1024]{1,0:T(8,128)(2,1)S(1)}, u32[]{:S(2)}, u32[]{:S(2)}) collective-permute-start(bf16[32,1024]{1,0:T(8,128)(2,1)S(1)} %backward.21), channel_id=1, source_target_pairs={{0,4},{4,0},{8,12},{12,8},{1,5},{5,1},{9,13},{13,9},{2,6},{6,2},{1... | collective-permute-start | bytes 196616 | tf_op jit(solution)/shard_map/ppermute | solution.py:46
  67.2 5.2 %collective-permute-start.29 = (bf16[32,1024]{1,0:T(8,128)(2,1)S(1)}, bf16[32,1024]{1,0:T(8,128)(2,1)S(1)}, u32[]{:S(2)}, u32[]{:S(2)}) collective-permute-start(bf16[32,1024]{1,0:T(8,128)(2,1)S(1)} %add.17), channel_id=1, source_target_pairs={{0,8},{4,12},{8,0},{12,4},{1,9},{5,13},{9,1},{13,5},{2,10},{6,14},... | collective-permute-start | bytes 196616 | tf_op jit(solution)/shard_map/ppermute | solution.py:46
  72.8 5.4 %collective-permute-start.32 = (f32[2,32]{1,0:T(2,128)S(1)}, f32[2,32]{1,0:T(2,128)S(1)}, u32[]{:S(2)}, u32[]{:S(2)}) collective-permute-start(f32[2,32]{1,0:T(2,128)S(1)} %get-tuple-element.84.refs_0_), channel_id=1, source_target_pairs={{0,12},{4,8},{8,4},{12,0},{1,13},{5,9},{9,5},{13,1},{2,14},{6,10},... | collective-permute-start | bytes 776 | tf_op jit(solution)/shard_map/ppermute | solution.py:46
  74.9 4.5 %collective-permute-start.31 = (f32[2,32]{1,0:T(2,128)S(1)}, f32[2,32]{1,0:T(2,128)S(1)}, u32[]{:S(2)}, u32[]{:S(2)}) collective-permute-start(f32[2,32]{1,0:T(2,128)S(1)} %get-tuple-element.84.refs_0_), channel_id=1, source_target_pairs={{0,8},{4,12},{8,0},{12,4},{1,9},{5,13},{9,1},{13,5},{2,10},{6,14},... | collective-permute-start | bytes 776 | tf_op jit(solution)/shard_map/ppermute | solution.py:46
  76.0 3.6 %collective-permute-start.30 = (f32[2,32]{1,0:T(2,128)S(1)}, f32[2,32]{1,0:T(2,128)S(1)}, u32[]{:S(2)}, u32[]{:S(2)}) collective-permute-start(f32[2,32]{1,0:T(2,128)S(1)} %get-tuple-element.84.refs_0_), channel_id=1, source_target_pairs={{0,4},{4,0},{8,12},{12,8},{1,5},{5,1},{9,13},{13,9},{2,6},{6,2},{1... | collective-permute-start | bytes 776 | tf_op jit(solution)/shard_map/ppermute | solution.py:46
  79.6 3.6 %collective-permute-start.34 = (f32[2,32]{1,0:T(2,128)S(1)}, f32[2,32]{1,0:T(2,128)S(1)}, u32[]{:S(2)}, u32[]{:S(2)}) collective-permute-start(f32[2,32]{1,0:T(2,128)S(1)} %moves.1.refs_0_), channel_id=1, source_target_pairs={{0,2},{1,3},{2,0},{3,1},{4,6},{5,7},{6,4},{7,5},{8,10},{9,11},{10,... | collective-permute-start | bytes 776 | tf_op jit(solution)/shard_map/ppermute | solution.py:46
  (11 other events, 56.6 us)
